TPU v7x, 32 devices: a whole 2x2x4 slice. The times are simulated.
32 devices in a mesh: dp: 8 (over z, y), tensor: 4 (over x, core).
Axes of the slice: x: 2, y: 2, z: 4, core: 2. Of those that a mesh axis runs over, the one named last changes fastest.
Arguments:
- layer_input: bfloat16 [10240, 768], P(('dp', 'tensor')), may hold values from -6 to 6
- cotangent: bfloat16 [10240, 768], P(('dp', 'tensor')), may hold values from -6 to 6
- segments: int32 [10240], replicated, may hold values from 0 to 25, as said below
- parents: int32 [26], replicated, may hold values from 0 to 17, as said below
- norm1_gain: bfloat16 [768], P('dp'), may hold values from 0.099609375 to 1.8984375
- w_query: bfloat16 [768, 768], P('dp', 'tensor'), may hold values from -0.21875 to 0.21875
- w_key: bfloat16 [768, 768], P('dp', 'tensor'), may hold values from -0.21875 to 0.21875
- w_value: bfloat16 [768, 768], P('dp', 'tensor'), may hold values from -0.21875 to 0.21875
- w_out: bfloat16 [768, 768], P('tensor', 'dp'), may hold values from -1.75 to 1.75
- norm2_gain: bfloat16 [768], P('dp'), may hold values from 0.099609375 to 1.8984375
- w_up: bfloat16 [768, 3072], P('dp', 'tensor'), may hold values from -0.21875 to 0.21875
- w_down: bfloat16 [3072, 768], P('tensor', 'dp'), may hold values from -0.109375 to 0.109375
Outputs:
- layer_output: bfloat16 [10240, 768], P(('dp', 'tensor'))
- input_grad: bfloat16 [10240, 768], P(('dp', 'tensor'))
- grad_norm1_gain: float32 [768], P('dp')
- grad_query: float32 [768, 768], P('dp', 'tensor')
- grad_key: float32 [768, 768], P('dp', 'tensor')
- grad_value: float32 [768, 768], P('dp', 'tensor')
- grad_out: float32 [768, 768], P('tensor', 'dp')
- grad_norm2_gain: float32 [768], P('dp')
- grad_up: float32 [768, 3072], P('dp', 'tensor')
- grad_down: float32 [3072, 768], P('tensor', 'dp')
Inputs may be any that keep to these rules, and one draw needn't show every extreme that they name: Tree t holds bytes 5120 t to 5120 (t + 1) - 1 of the stream (the last tree may end at 10240). Its first 2048 bytes are segment 13 t, the trunk; the rest are twelve runs of 256 bytes with the segments 13 t + 1 to 13 t + 12 in some order, every run after the run of its parent segment. parents[s] is the parent segment of s: the trunk 13 t is its own parent, the branches 13 t + 1 to 13 t + 4 have the trunk, and the leaves 13 t + 5 to 13 t + 12 have one of the four branches each, two leaves a branch.
All inputs are finite; a program needn't handle non-finite values.
Results may differ from a plain program's by a relative error of at most 0.017.
Values may be sent and summed in bfloat16 or wider, within the bound.
A program may use at most 256 MiB of HBM per device.

v0:
```python
import math

import jax
import jax.numpy as jnp
from jax import lax
from jax.sharding import PartitionSpec as P

HD = 64
WINDOW = 1536


epsilon = 1e-06
masked_score = -1e30


def from_behind(block, axis, distance):
    devices = range(lax.axis_size(axis))
    route = [(i - distance, i) for i in devices if i - distance in devices]
    return lax.ppermute(block, axis, route)


def split_up(x, dim, peers):
    dims = x.shape
    tiles = x.reshape(*dims[:dim], peers, dims[dim] // peers, *dims[dim + 1 :])
    return jnp.moveaxis(tiles, dim, 0)


def sum_at_owner(x, axis, dim):
    tiles = split_up(x, dim, lax.axis_size(axis))
    arrived = lax.all_to_all(tiles, axis, split_axis=0, concat_axis=0, tiled=True)
    return arrived.astype(jnp.float32).sum(axis=0)


def side_by_side(arrays, axis, dim, along):
    widths = [math.prod(a.shape[along:]) for a in arrays]
    both = jnp.concatenate(
        [a.reshape(*a.shape[:along], w) for a, w in zip(arrays, widths)], axis=along
    )
    whole = sum_at_owner(both, axis, dim)
    tiles = jnp.split(whole, [sum(widths[:k]) for k in range(1, len(widths))], axis=along)
    return tuple((b.reshape(*whole.shape[:along], *a.shape[along:]) for a, b in zip(arrays, tiles)))


def gelu_exact(values):
    return jax.nn.gelu(values, approximate=False)


def row_scale(values):
    return lax.rsqrt(jnp.mean(values * values, axis=-1, keepdims=True) + epsilon)


def norm_backward(incoming, normal_hat, row_factor, gain):
    scaled = incoming * gain
    inner = jnp.mean(scaled * normal_hat, axis=-1, keepdims=True)
    return (row_factor * (scaled - normal_hat * inner), jnp.sum(incoming * normal_hat, axis=0))


def parent_of(seg_ids, parents):
    seg_table = jnp.arange(parents.shape[0], dtype=jnp.int32)
    hits = seg_ids[:, None] == seg_table[None, :]
    return jnp.sum(jnp.where(hits, parents[None, :], 0), axis=1)


def shards(
    layer_input,
    cotangent,
    segments,
    parents,
    norm1_gain,
    w_query,
    w_key,
    w_value,
    w_out,
    norm2_gain,
    w_up,
    w_down,
):
    gain_one, full_query, full_key, full_value, full_out, gain_two, full_up, full_down = (
        lax.all_gather(norm1_gain, "dp", axis=0, tiled=True),
        lax.all_gather(w_query, "dp", axis=0, tiled=True),
        lax.all_gather(w_key, "dp", axis=0, tiled=True),
        lax.all_gather(w_value, "dp", axis=0, tiled=True),
        lax.all_gather(w_out, "dp", axis=1, tiled=True),
        lax.all_gather(norm2_gain, "dp", axis=0, tiled=True),
        lax.all_gather(w_up, "dp", axis=0, tiled=True),
        lax.all_gather(w_down, "dp", axis=1, tiled=True),
    )
    gain_one = gain_one.astype(jnp.float32)
    gain_two = gain_two.astype(jnp.float32)
    row_count = layer_input.shape[0]
    token_count = row_count * lax.axis_size("tensor")
    position = lax.axis_index("dp") * token_count
    head_width = full_query.shape[1]
    head_count = head_width // HD
    scaling = HD ** (-0.5)
    block_rows = min(640, token_count)
    block_count = token_count // block_rows
    span = WINDOW + block_rows
    hop_count = (WINDOW + token_count - 1) // token_count
    inputs = layer_input.astype(jnp.float32)
    factor_one = row_scale(inputs)
    hat_one = inputs * factor_one
    normed = (hat_one * gain_one).astype(jnp.bfloat16)
    normed_all = lax.all_gather(normed, "tensor", axis=0, tiled=True)
    queries = jnp.dot(normed_all, full_query, preferred_element_type=jnp.float32).astype(
        jnp.bfloat16
    )
    keys_own = jnp.dot(normed_all, full_key, preferred_element_type=jnp.float32).astype(
        jnp.bfloat16
    )
    values_own = jnp.dot(normed_all, full_value, preferred_element_type=jnp.float32).astype(
        jnp.bfloat16
    )
    pair_own = jnp.concatenate([keys_own, values_own], axis=1)
    halo_parts = []
    for distance in range(1, hop_count + 1):
        length = min(token_count, WINDOW - (distance - 1) * token_count)
        piece = pair_own[token_count - length :]
        moved = from_behind(piece, "dp", distance)
        halo_parts.append(moved)
    pair_all = jnp.concatenate(halo_parts[::-1] + [pair_own], axis=0)
    seg_padded = jnp.concatenate([jnp.full((WINDOW,), -1, jnp.int32), segments])
    seg_keys = lax.dynamic_slice_in_dim(seg_padded, position, WINDOW + token_count, 0)
    seg_query = seg_keys[WINDOW:]
    parent_one = parent_of(seg_query, parents)
    parent_two = parent_of(parent_one, parents)
    query_spots = jnp.arange(block_rows, dtype=jnp.int32)
    key_spots = jnp.arange(span, dtype=jnp.int32)

    def scores_of(offset):
        query_block = lax.dynamic_slice_in_dim(queries, offset, block_rows, 0).reshape(
            block_rows, head_count, HD
        )
        pair_block = lax.dynamic_slice_in_dim(pair_all, offset, span, 0)
        key_block = pair_block[:, :head_width].reshape(span, head_count, HD)
        value_block = pair_block[:, head_width:].reshape(span, head_count, HD)
        own_seg = lax.dynamic_slice_in_dim(seg_query, offset, block_rows, 0)
        up_one = lax.dynamic_slice_in_dim(parent_one, offset, block_rows, 0)
        up_two = lax.dynamic_slice_in_dim(parent_two, offset, block_rows, 0)
        near_seg = lax.dynamic_slice_in_dim(seg_keys, offset, span, 0)
        gap = WINDOW + query_spots[:, None] - key_spots[None, :]
        same_path = (
            (near_seg[None, :] == own_seg[:, None])
            | (near_seg[None, :] == up_one[:, None])
            | (near_seg[None, :] == up_two[:, None])
        )
        allowed = (gap >= 0) & (gap < WINDOW) & same_path
        raw = (
            jnp.einsum("qhd,khd->hqk", query_block, key_block, preferred_element_type=jnp.float32)
            * scaling
        )
        return (jnp.where(allowed[None], raw, masked_score), query_block, key_block, value_block)

    def forward_block(block_index):
        scores, query_block, key_block, value_block = scores_of(block_index * block_rows)
        row_max = jnp.max(scores, axis=-1, keepdims=True)
        exponent = jnp.exp(scores - row_max)
        denominator = jnp.sum(exponent, axis=-1, keepdims=True)
        weights = (exponent / denominator).astype(jnp.bfloat16)
        mixed = jnp.einsum("hqk,khd->qhd", weights, value_block, preferred_element_type=jnp.float32)
        return (
            mixed.reshape(block_rows, head_width).astype(jnp.bfloat16),
            (row_max + jnp.log(denominator))[..., 0],
        )

    context_blocks, logsum_blocks = lax.map(forward_block, jnp.arange(block_count, dtype=jnp.int32))
    context = context_blocks.reshape(token_count, head_width)
    middle = inputs + lax.psum_scatter(
        jnp.dot(context, full_out, preferred_element_type=jnp.float32).astype(jnp.bfloat16),
        "tensor",
        scatter_dimension=0,
        tiled=True,
    ).astype(jnp.float32)
    factor_two = row_scale(middle)
    hat_two = middle * factor_two
    normed_two = (hat_two * gain_two).astype(jnp.bfloat16)
    normed_two_all = lax.all_gather(normed_two, "tensor", axis=0, tiled=True)
    upper = jnp.dot(normed_two_all, full_up, preferred_element_type=jnp.float32)
    active = gelu_exact(upper).astype(jnp.bfloat16)
    result = middle + lax.psum_scatter(
        jnp.dot(active, full_down, preferred_element_type=jnp.float32).astype(jnp.bfloat16),
        "tensor",
        scatter_dimension=0,
        tiled=True,
    ).astype(jnp.float32)
    incoming = cotangent.astype(jnp.float32)
    incoming_all = lax.all_gather(cotangent, "tensor", axis=0, tiled=True)
    grad_down = jnp.einsum("tf,td->fd", active, incoming_all, preferred_element_type=jnp.float32)
    grad_active = jnp.einsum(
        "td,fd->tf", incoming_all, full_down, preferred_element_type=jnp.float32
    )
    unused_value, gelu_pull = jax.vjp(gelu_exact, upper)
    grad_upper = gelu_pull(grad_active)[0].astype(jnp.bfloat16)
    grad_up = jnp.einsum(
        "tc,tf->cf", normed_two_all, grad_upper, preferred_element_type=jnp.float32
    )
    grad_normed_two = lax.psum_scatter(
        jnp.einsum("tf,cf->tc", grad_upper, full_up, preferred_element_type=jnp.float32).astype(
            jnp.bfloat16
        ),
        "tensor",
        scatter_dimension=0,
        tiled=True,
    ).astype(jnp.float32)
    through_two, gain_two_part = norm_backward(grad_normed_two, hat_two, factor_two, gain_two)
    grad_middle = incoming + through_two
    grad_middle_all = lax.all_gather(grad_middle.astype(jnp.bfloat16), "tensor", axis=0, tiled=True)
    grad_out = jnp.einsum("tc,td->cd", context, grad_middle_all, preferred_element_type=jnp.float32)
    grad_context = jnp.einsum(
        "td,cd->tc", grad_middle_all, full_out, preferred_element_type=jnp.float32
    ).astype(jnp.bfloat16)

    def backward_block(block_index, carry):
        grad_queries, grad_pairs = carry
        offset = block_index * block_rows
        scores, query_block, key_block, value_block = scores_of(offset)
        logsum = lax.dynamic_index_in_dim(logsum_blocks, block_index, 0, keepdims=False)
        probs = jnp.exp(scores - logsum[..., None])
        grad_rows = lax.dynamic_slice_in_dim(grad_context, offset, block_rows, 0).reshape(
            block_rows, head_count, HD
        )
        grad_probs = jnp.einsum(
            "qhd,khd->hqk", grad_rows, value_block, preferred_element_type=jnp.float32
        )
        inner = jnp.sum(probs * grad_probs, axis=-1, keepdims=True)
        grad_scores = (probs * (grad_probs - inner)).astype(jnp.bfloat16)
        grad_query_block = (
            jnp.einsum("hqk,khd->qhd", grad_scores, key_block, preferred_element_type=jnp.float32)
            * scaling
        )
        grad_key_block = (
            jnp.einsum("hqk,qhd->khd", grad_scores, query_block, preferred_element_type=jnp.float32)
            * scaling
        )
        grad_value_block = jnp.einsum(
            "hqk,qhd->khd",
            probs.astype(jnp.bfloat16),
            grad_rows,
            preferred_element_type=jnp.float32,
        )
        grad_queries = lax.dynamic_update_slice_in_dim(
            grad_queries, grad_query_block.reshape(block_rows, head_width), offset, 0
        )
        update = jnp.concatenate(
            [grad_key_block.reshape(span, head_width), grad_value_block.reshape(span, head_width)],
            axis=1,
        )
        current = lax.dynamic_slice_in_dim(grad_pairs, offset, span, 0)
        grad_pairs = lax.dynamic_update_slice_in_dim(grad_pairs, current + update, offset, 0)
        return (grad_queries, grad_pairs)

    start_carry = (
        jnp.zeros((token_count, head_width), jnp.float32),
        jnp.zeros((WINDOW + token_count, 2 * head_width), jnp.float32),
    )
    grad_queries, grad_pairs = lax.fori_loop(0, block_count, backward_block, start_carry)
    grad_own = grad_pairs[WINDOW:]
    for distance in range(1, hop_count + 1):
        length = min(token_count, WINDOW - (distance - 1) * token_count)
        first_row = WINDOW - (distance - 1) * token_count - length
        piece = grad_pairs[first_row : first_row + length]
        returned = from_behind(piece.astype(jnp.bfloat16), "dp", -distance).astype(piece.dtype)
        grad_own = grad_own + jnp.pad(returned, ((token_count - length, 0), (0, 0)))
    grad_keys = grad_own[:, :head_width].astype(jnp.bfloat16)
    grad_values = grad_own[:, head_width:].astype(jnp.bfloat16)
    grad_queries_low = grad_queries.astype(jnp.bfloat16)
    grad_query = jnp.einsum(
        "tc,tq->cq", normed_all, grad_queries_low, preferred_element_type=jnp.float32
    )
    grad_key = jnp.einsum("tc,tq->cq", normed_all, grad_keys, preferred_element_type=jnp.float32)
    grad_value = jnp.einsum(
        "tc,tq->cq", normed_all, grad_values, preferred_element_type=jnp.float32
    )
    part_query = jnp.einsum(
        "tq,cq->tc", grad_queries_low, full_query, preferred_element_type=jnp.float32
    )
    part_key = jnp.einsum("tq,cq->tc", grad_keys, full_key, preferred_element_type=jnp.float32)
    part_value = jnp.einsum(
        "tq,cq->tc", grad_values, full_value, preferred_element_type=jnp.float32
    )
    grad_normed = lax.psum_scatter(
        (part_query + part_key + part_value).astype(jnp.bfloat16),
        "tensor",
        scatter_dimension=0,
        tiled=True,
    ).astype(jnp.float32)
    through_one, gain_one_part = norm_backward(grad_normed, hat_one, factor_one, gain_one)
    grad_inputs = grad_middle + through_one
    gain_one_sum, gain_two_sum = lax.psum((gain_one_part, gain_two_part), "tensor")
    summed = (
        *side_by_side(
            (
                gain_one_sum.astype(jnp.bfloat16),
                grad_query.astype(jnp.bfloat16),
                grad_key.astype(jnp.bfloat16),
                grad_value.astype(jnp.bfloat16),
            ),
            "dp",
            0,
            1,
        ),
        sum_at_owner(grad_out.astype(jnp.bfloat16), "dp", 1),
        *side_by_side(
            (gain_two_sum.astype(jnp.bfloat16), grad_up.astype(jnp.bfloat16)), "dp", 0, 1
        ),
        sum_at_owner(grad_down.astype(jnp.bfloat16), "dp", 1),
    )
    return (
        result.astype(jnp.bfloat16),
        grad_inputs.astype(jnp.bfloat16),
        summed[0],
        summed[1],
        summed[2],
        summed[3],
        summed[4],
        summed[5],
        summed[6],
        summed[7],
    )


def solution(mesh):
    return jax.shard_map(
        shards,
        mesh=mesh,
        in_specs=(
            P(("dp", "tensor"), None),
            P(("dp", "tensor"), None),
            P(),
            P(),
            P("dp"),
            P("dp", "tensor"),
            P("dp", "tensor"),
            P("dp", "tensor"),
            P("tensor", "dp"),
            P("dp"),
            P("dp", "tensor"),
            P("tensor", "dp"),
        ),
        out_specs=(
            P(("dp", "tensor"), None),
            P(("dp", "tensor"), None),
            P("dp"),
            P("dp", "tensor"),
            P("dp", "tensor"),
            P("dp", "tensor"),
            P("tensor", "dp"),
            P("dp"),
            P("dp", "tensor"),
            P("tensor", "dp"),
        ),
        check_vma=False,
    )
```

profile of v0, /device:TPU:0, one launch (start us, length us, event | category | flops | bytes accessed | tf_op | source)
XLA Modules:
  0.0 773.3 jit_solution(16327131825716059331)
XLA Ops:
  12.9 23.7 %all-reduce.5 = (bf16[768]{0:T(1024)(128)(2,1)S(1)}, bf16[768]{0:T(1024)(128)(2,1)}) all-reduce(bf16[768]{0:T(1024)(128)(2,1)S(1)} %dynamic-update-slice, bf16[768]{0:T(1024)(128)(2,1)S(1)} %dynamic-update-slice.1), channel_id=1, replica_groups=mesh['dp'=8,'tensor'=4] {'dp'}, use_global_device_ids=true, to_apply=%add.2 | all-reduce | flops 1536 | bytes 6144
  41.0 31.2 %all_gather.38 = bf16[768,192]{1,0:T(8,128)(2,1)S(1)} all-gather(bf16[96,192]{1,0:T(8,128)(2,1)} %param.22), channel_id=1, replica_groups=mesh['dp'=8,'tensor'=4] {'dp'}, dimensions={0}, use_global_device_ids=true | all-gather | bytes 331776 | tf_op jit(solution)/shard_map/all_gather | solution.py:81
  72.2 31.2 %all_gather.39 = bf16[768,192]{1,0:T(8,128)(2,1)S(1)} all-gather(bf16[96,192]{1,0:T(8,128)(2,1)} %param.23), channel_id=1, replica_groups=mesh['dp'=8,'tensor'=4] {'dp'}, dimensions={0}, use_global_device_ids=true | all-gather | bytes 331776 | tf_op jit(solution)/shard_map/all_gather | solution.py:82
  110.2 46.0 %all_gather.41 = bf16[192,768]{0,1:T(8,128)(2,1)} all-gather(bf16[192,96]{0,1:T(8,128)(2,1)S(1)} %copy.48), channel_id=1, replica_groups=mesh['dp'=8,'tensor'=4] {'dp'}, dimensions={1}, use_global_device_ids=true | all-gather | bytes 331776 | tf_op jit(solution)/shard_map/all_gather | solution.py:83
  156.2 31.0 %all_gather.40 = bf16[768,192]{1,0:T(8,128)(2,1)S(1)} all-gather(bf16[96,192]{1,0:T(8,128)(2,1)S(1)} %copy-done.35), channel_id=1, replica_groups=mesh['dp'=8,'tensor'=4] {'dp'}, dimensions={0}, use_global_device_ids=true | all-gather | bytes 331776 | tf_op jit(solution)/shard_map/all_gather | solution.py:80
  193.2 72.9 %while.29 = (s32[]{:T(128)}, bf16[2,640,192]{1,2,0:T(8,128)(2,1)}, f32[2,3,640]{2,1,0:T(4,128)S(1)}, s32[2]{0:T(128)S(1)}, bf16[2816,384]{0,1:T(8,128)(2,1)}, /*...) while((s32[]{:T(128)}, bf16[2,640,192]{1,2,0:T(8,128)(2,1)}, ...), condition=%wide.region_6.7_spmd.clone, body=%wide.region_3.6_spmd.clone.sunk | while | flops 1133730560 | bytes 66249560 | solution.py:166
  209.7 10.5 %fusion.137 = f32[3,640]{1,0:T(4,128)S(1)} fusion(f32[3,640,2176]{2,1,0:T(8,128)} %get-tuple-element.566, f32[3,640]{1,0:T(4,128)S(1)} %get-tuple-element.567, pred[640,2176]{1,0:T(8,128)(4,1)S(1)} %fusion.135), kind=kLoop, calls=%fused_computation.8.clone.1 | loop fusion | flops 16709760 | bytes 18119680 | tf_op jit(solution)/shard_map/while/body/eval_jaxpr/reduce_sum | solution.py:158
  245.9 10.5 %fusion.137 = f32[3,640]{1,0:T(4,128)S(1)} fusion(f32[3,640,2176]{2,1,0:T(8,128)} %get-tuple-element.566, f32[3,640]{1,0:T(4,128)S(1)} %get-tuple-element.567, pred[640,2176]{1,0:T(8,128)(4,1)S(1)} %fusion.135), kind=kLoop, calls=%fused_computation.8.clone.1 | loop fusion | flops 16709760 | bytes 18119680 | tf_op jit(solution)/shard_map/while/body/eval_jaxpr/reduce_sum | solution.py:158
  271.3 32.8 %reduce-scatter.5.cloned.1.call-done = bf16[320,768]{1,0:T(8,128)(2,1)} async-done(((bf16[1280,768]{1,0:T(8,128)(2,1)}), bf16[320,768]{1,0:T(8,128)(2,1)}) %reduce-scatter.5.cloned.1.call-update) | async-done | bytes 491536 | tf_op jit(solution)/shard_map/reduce_scatter | solution.py:168
  317.7 22.3 %all-gather.9.cloned.1.call-done = bf16[1280,768]{1,0:T(8,128)(2,1)} async-done(((bf16[320,768]{1,0:T(8,128)(2,1)}), bf16[1280,768]{1,0:T(8,128)(2,1)}) %all-gather.9.cloned.1.call-update) | async-done | bytes 1966096 | tf_op jit(solution)/shard_map/all_gather | solution.py:177
  345.5 38.4 %all-gather.13.cloned.1.call-done = bf16[768,768]{0,1:T(8,128)(2,1)} async-done(((bf16[768,96]{0,1:T(8,128)(2,1)}), bf16[768,768]{0,1:T(8,128)(2,1)}) %all-gather.13.cloned.1.call-update) | async-done | bytes 1179664 | tf_op jit(solution)/shard_map/all_gather | solution.py:86
  383.9 21.9 %all-gather.15.cloned.1.call-done = bf16[1280,768]{1,0:T(8,128)(2,1)} async-done(((bf16[320,768]{1,0:T(8,128)(2,1)}), bf16[1280,768]{1,0:T(8,128)(2,1)}) %all-gather.15.cloned.1.call-update) | async-done | bytes 1966096 | tf_op jit(solution)/shard_map/all_gather | solution.py:187
  405.7 13.1 %add_convert_fusion = (bf16[1280,768]{1,0:T(8,128)(2,1)S(1)}, f32[1280,768]{1,0:T(8,128)}) fusion(f32[1280,768]{1,0:T(8,128)} %fusion.64, bf16[1280,768]{1,0:T(8,128)(2,1)} %all-gather.15.cloned.1.call-done, bf16[768,768]{0,1:T(8,128)(2,1)} %all-gather.13.cloned.1.call-done), kind=kOutput, calls=%fused_computation.47 | convolution fusion | flops 1580728320 | bytes 12976128 | tf_op jit(solution)/shard_map/td,fd->tf/dot_general | solution.py:189
  424.6 30.7 %reduce-scatter.9.cloned.1.call-done = bf16[320,768]{1,0:T(8,128)(2,1)} async-done(((bf16[1280,768]{1,0:T(8,128)(2,1)}), bf16[320,768]{1,0:T(8,128)(2,1)}) %reduce-scatter.9.cloned.1.call-update) | async-done | bytes 491536 | tf_op jit(solution)/shard_map/reduce_scatter | solution.py:197
  460.0 21.5 %all-gather.17.cloned.1.call-done = bf16[1280,768]{1,0:T(8,128)(2,1)} async-done(((bf16[320,768]{1,0:T(8,128)(2,1)}), bf16[1280,768]{1,0:T(8,128)(2,1)}) %all-gather.17.cloned.1.call-update) | async-done | bytes 1966096 | tf_op jit(solution)/shard_map/all_gather | solution.py:207
  487.9 112.6 %while.30 = (s32[]{:T(128)}, bf16[1280,192]{0,1:T(8,128)(2,1)}, f32[2816,384]{0,1:T(8,128)}, bf16[2816,384]{0,1:T(8,128)(2,1)}, s32[2816]{0:T(1024)S(1)}, /*inde...) while((s32[]{:T(128)}, bf16[1280,192]{0,1:T(8,128)(2,1)}, ...), condition=%wide.region_14.15_spmd.clone, body=%wide.region_12.14_spmd.clone.sunk | while | flops 2727729920 | bytes 220916592 | solution.py:256
  503.7 15.1 %multiply_reduce_fusion.3 = (f32[3,640]{1,0:T(4,128)S(1)}, f32[3,640,2176]{2,1,0:T(8,128)}) fusion(f32[3,640,2176]{2,1,0:T(8,128)} %fusion.150, f32[3,640]{1,0:T(4,128)S(1)} %dynamic-slice_bitcast_fusion.2, bf16[640,3,64]{0,2,1:T(8,128)(2,1)S(1)} %bitcast.138, bf16[2176,3,64]{0,2,1:T(8,128)(2,1)S(1)} %bitcast.135, pred[640,2176]{1,0:T(8,128)(4,1)S(1)} %fusion.151), kind=kOutput, calls=%fused_computation.24.clone.1 | convolution fusion | flops 555661440 | bytes 35912704 | tf_op jit(solution)/shard_map/while/body/eval_jaxpr/qhd,khd->hqk/dot_general | solution.py:149
  518.8 11.4 %multiply_convert_fusion.4 = bf16[3,640,2176]{2,1,0:T(8,128)(2,1)S(1)} fusion(f32[3,640,2176]{2,1,0:T(8,128)} %get-tuple-element.583, f32[3,640,2176]{2,1,0:T(8,128)} %fusion.150, f32[3,640]{1,0:T(4,128)S(1)} %get-tuple-element.584), kind=kLoop, calls=%fused_computation.23.clone.1 | loop fusion | flops 12533760 | bytes 41786880 | tf_op jit(solution)/shard_map/while/body/eval_jaxpr/convert_element_type | solution.py:226
  559.9 15.1 %multiply_reduce_fusion.3 = (f32[3,640]{1,0:T(4,128)S(1)}, f32[3,640,2176]{2,1,0:T(8,128)}) fusion(f32[3,640,2176]{2,1,0:T(8,128)} %fusion.150, f32[3,640]{1,0:T(4,128)S(1)} %dynamic-slice_bitcast_fusion.2, bf16[640,3,64]{0,2,1:T(8,128)(2,1)S(1)} %bitcast.138, bf16[2176,3,64]{0,2,1:T(8,128)(2,1)S(1)} %bitcast.135, pred[640,2176]{1,0:T(8,128)(4,1)S(1)} %fusion.151), kind=kOutput, calls=%fused_computation.24.clone.1 | convolution fusion | flops 555661440 | bytes 35912704 | tf_op jit(solution)/shard_map/while/body/eval_jaxpr/qhd,khd->hqk/dot_general | solution.py:149
  575.0 11.4 %multiply_convert_fusion.4 = bf16[3,640,2176]{2,1,0:T(8,128)(2,1)S(1)} fusion(f32[3,640,2176]{2,1,0:T(8,128)} %get-tuple-element.583, f32[3,640,2176]{2,1,0:T(8,128)} %fusion.150, f32[3,640]{1,0:T(4,128)S(1)} %get-tuple-element.584), kind=kLoop, calls=%fused_computation.23.clone.1 | loop fusion | flops 12533760 | bytes 41786880 | tf_op jit(solution)/shard_map/while/body/eval_jaxpr/convert_element_type | solution.py:226
  606.7 27.3 %collective-permute-done.3 = bf16[256,384]{0,1:T(8,128)(2,1)S(1)} collective-permute-done((bf16[256,384]{0,1:T(8,128)(2,1)S(1)}, bf16[256,384]{0,1:T(8,128)(2,1)S(1)}, u32[]{:S(2)}, u32[]{:S(2)}) %collective-permute-start.3) | collective-permute-done | bytes 196640 | tf_op jit(solution)/shard_map/ppermute | solution.py:19
  667.3 11.4 %all-to-all-done.3 = bf16[8,768,96]{1,2,0:T(8,128)(2,1)} async-done(((bf16[8,768,96]{1,2,0:T(8,128)(2,1)}), bf16[8,768,96]{1,2,0:T(8,128)(2,1)}, u32[]{:S(2)}, u32[]{:S(2)}) %all-to-all-start.3) | async-done | bytes 1179680 | tf_op jit(solution)/shard_map/all_to_all | solution.py:30
  711.0 15.5 %all-to-all-done = bf16[8,96,577]{2,1,0:T(8,128)(2,1)S(1)} async-done(((bf16[8,96,577]{2,1,0:T(8,128)(2,1)}), bf16[8,96,577]{2,1,0:T(8,128)(2,1)S(1)}, u32[]{:S(2)}, u32[]{:S(2)}) %all-to-all-start) | async-done | bytes 886304 | tf_op jit(solution)/shard_map/all_to_all | solution.py:30
  739.5 24.3 %all-to-all-done.2 = bf16[8,96,769]{2,1,0:T(8,128)(2,1)S(1)} async-done(((bf16[8,96,769]{2,1,0:T(8,128)(2,1)}), bf16[8,96,769]{2,1,0:T(8,128)(2,1)S(1)}, u32[]{:S(2)}, u32[]{:S(2)}) %all-to-all-start.2) | async-done | bytes 1181216 | tf_op jit(solution)/shard_map/all_to_all | solution.py:30
  (266 shorter events, 257.6 us)
Async XLA Ops:
  8.0 95.4 %all-gather.7.cloned.1.call-start = ((), (), s32[]{:S(2)}) async-start(), calls=%async_computation.8 | async-start | bytes 2457600 | tf_op jit(solution)/shard_map/all_gather | solution.py:104
  39.2 264.9 %reduce-scatter.5.cloned.1.call-start = ((), (), s32[]{:S(2)}) async-start(), calls=%async_computation.9 | async-start | bytes 2457600 | tf_op jit(solution)/shard_map/reduce_scatter | solution.py:168
  103.4 52.9 %copy-start.21 = (bf16[768,192]{1,0:T(8,128)(2,1)}, bf16[768,192]{1,0:T(8,128)(2,1)S(1)}, u32[]{:S(2)}) copy-start(bf16[768,192]{1,0:T(8,128)(2,1)S(1)} %all_gather.39) | copy-start | bytes 884740
  103.4 52.9 %copy-start.35 = (bf16[96,192]{1,0:T(8,128)(2,1)S(1)}, bf16[96,192]{1,0:T(8,128)(2,1)}, u32[]{:S(2)}) copy-start(bf16[96,192]{1,0:T(8,128)(2,1)} %param.21) | copy-start | bytes 110596
  105.9 82.6 %copy-start.3 = (bf16[1280,768]{1,0:T(8,128)(2,1)S(1)}, bf16[1280,768]{1,0:T(8,128)(2,1)}, u32[]{:S(2)}) copy-start(bf16[1280,768]{1,0:T(8,128)(2,1)} %all-gather.7.cloned.1.call-done) | copy-start | bytes 5898244
  108.5 83.2 %collective-permute-start.1 = (bf16[1280,384]{0,1:T(8,128)(2,1)S(1)}, bf16[1280,384]{0,1:T(8,128)(2,1)S(1)}, u32[]{:S(2)}, u32[]{:S(2)}) collective-permute-start(bf16[1280,384]{0,1:T(8,128)(2,1)S(1)} %pad_maximum_fusion.1), channel_id=1, source_target_pairs={{0,4},{4,8},{8,12},{12,16},{16,20},{20,24},{24,28},{1,5},{5,9},{9,... | collective-permute-start | bytes 2949128 | tf_op jit(solution)/shard_map/ppermute | solution.py:19
  187.2 4.5 collective-permute-start
  270.5 47.2 %all-gather.11.cloned.1.call-start = ((), (), s32[]{:S(2)}) async-start(), calls=%async_computation.11 | async-start | bytes 1327104 | tf_op jit(solution)/shard_map/all_gather | solution.py:85
  271.1 69.0 %all-gather.9.cloned.1.call-start = ((), (), s32[]{:S(2)}) async-start(), calls=%async_computation.10 | async-start | bytes 2457600 | tf_op jit(solution)/shard_map/all_gather | solution.py:177
  271.3 186.2 %copy-start.29 = (f32[768]{0:T(1024)}, f32[768]{0:T(1024)S(1)}, u32[]{:S(2)}) copy-start(f32[768]{0:T(1024)S(1)} %convert_element_type.159) | copy-start | bytes 9220
  305.4 152.2 %copy-start.33 = (f32[320]{0:T(512)}, f32[320]{0:T(512)S(1)}, u32[]{:S(2)}) copy-start(f32[320]{0:T(512)S(1)} %add_rsqrt_fusion) | copy-start | bytes 3844
  307.4 76.4 %all-gather.13.cloned.1.call-start = ((), (), s32[]{:S(2)}) async-start(), calls=%async_computation.12 | async-start | bytes 1327104 | tf_op jit(solution)/shard_map/all_gather | solution.py:86
  308.0 97.7 %all-gather.15.cloned.1.call-start = ((), (), s32[]{:S(2)}) async-start(), calls=%async_computation.14 | async-start | bytes 2457600 | tf_op jit(solution)/shard_map/all_gather | solution.py:187
  308.7 146.6 %reduce-scatter.9.cloned.1.call-start = ((), (), s32[]{:S(2)}) async-start(), calls=%async_computation.15 | async-start | bytes 2457600 | tf_op jit(solution)/shard_map/reduce_scatter | solution.py:197
  424.6 57.0 %copy-start.25 = (bf16[192,768]{0,1:T(8,128)(2,1)S(1)}, bf16[192,768]{0,1:T(8,128)(2,1)}, u32[]{:S(2)}) copy-start(bf16[192,768]{0,1:T(8,128)(2,1)} %all_gather.41) | copy-start | bytes 884740
  424.6 57.0 %all-gather.17.cloned.1.call-start = ((), (), s32[]{:S(2)}) async-start(), calls=%async_computation.16 | async-start | bytes 2457600 | tf_op jit(solution)/shard_map/all_gather | solution.py:207
  459.8 225.5 %reduce-scatter.11.cloned.1.call-start = ((), (), s32[]{:S(2)}) async-start(), calls=%async_computation.17 | async-start | bytes 2457600 | tf_op jit(solution)/shard_map/reduce_scatter | solution.py:281
  603.1 30.9 %collective-permute-start.2 = (bf16[1280,384]{0,1:T(8,128)(2,1)S(1)}, bf16[1280,384]{0,1:T(8,128)(2,1)S(1)}, u32[]{:S(2)}, u32[]{:S(2)}) collective-permute-start(bf16[1280,384]{0,1:T(8,128)(2,1)S(1)} %slice.58), channel_id=1, source_target_pairs={{4,0},{8,4},{12,8},{16,12},{20,16},{24,20},{28,24},{5,1},{9,5},{13... | collective-permute-start | bytes 2949128 | tf_op jit(solution)/shard_map/ppermute | solution.py:19
  604.7 29.3 %collective-permute-start.3 = (bf16[256,384]{0,1:T(8,128)(2,1)S(1)}, bf16[256,384]{0,1:T(8,128)(2,1)S(1)}, u32[]{:S(2)}, u32[]{:S(2)}) collective-permute-start(bf16[256,384]{0,1:T(8,128)(2,1)S(1)} %slice.59), channel_id=1, source_target_pairs={{8,0},{12,4},{16,8},{20,12},{24,16},{28,20},{9,1},{13,5},{17,9},{2... | collective-permute-start | bytes 589832 | tf_op jit(solution)/shard_map/ppermute | solution.py:19
  646.0 32.7 %all-to-all-start.3 = ((bf16[8,768,96]{1,2,0:T(8,128)(2,1)}), bf16[8,768,96]{1,2,0:T(8,128)(2,1)}, u32[]{:S(2)}, u32[]{:S(2)}) async-start(bf16[8,768,96]{1,2,0:T(8,128)(2,1)} %bitcast.154), calls=%async_computation.7 | async-start | bytes 2359296 | tf_op jit(solution)/shard_map/all_to_all | solution.py:30
  650.3 84.6 %reduce-scatter.7.cloned.1.call-start = ((), (), s32[]{:S(2)}) async-start(), calls=%async_computation.13 | async-start | bytes 2457600 | tf_op jit(solution)/shard_map/reduce_scatter | solution.py:180
  678.7 17.6 %all-to-all-start.1 = ((bf16[8,192,96]{2,1,0:T(8,128)(2,1)}), bf16[8,192,96]{2,1,0:T(8,128)(2,1)}, u32[]{:S(2)}, u32[]{:S(2)}) async-start(bf16[8,192,96]{2,1,0:T(8,128)(2,1)} %bitcast.150), calls=%async_computation.5 | async-start | bytes 786432 | tf_op jit(solution)/shard_map/all_to_all | solution.py:30
  696.4 30.1 %all-to-all-start = ((bf16[8,96,577]{2,1,0:T(8,128)(2,1)}), bf16[8,96,577]{2,1,0:T(8,128)(2,1)S(1)}, u32[]{:S(2)}, u32[]{:S(2)}) async-start(bf16[8,96,577]{2,1,0:T(8,128)(2,1)} %pad_maximum_fusion.2), calls=%async_computation.4 | async-start | bytes 1966080 | tf_op jit(solution)/shard_map/all_to_all | solution.py:30
  727.4 36.4 %all-to-all-start.2 = ((bf16[8,96,769]{2,1,0:T(8,128)(2,1)}), bf16[8,96,769]{2,1,0:T(8,128)(2,1)S(1)}, u32[]{:S(2)}, u32[]{:S(2)}) async-start(bf16[8,96,769]{2,1,0:T(8,128)(2,1)} %pad_maximum_fusion), calls=%async_computation.6 | async-start | bytes 2752512 | tf_op jit(solution)/shard_map/all_to_all | solution.py:30
  (44 other events, 673.5 us)
Sparse Core Ops, SparseCore 0:
  39.3 19.0 all-gather.6
  270.6 33.4 reduce-scatter.4
  424.7 30.6 reduce-scatter.8
  639.3 28.7 reduce-scatter.10
  670.7 30.9 reduce-scatter.6
Sparse Core Ops, SparseCore 1:
  273.4 44.3 all-gather.10
  319.8 20.1 all-gather.8
  342.3 41.5 all-gather.12
  385.5 20.1 all-gather.14
  459.8 21.7 all-gather.16
where the time goes:
time: 779 us; the launch traced here: 773 us
  waiting for transfers between devices  259 us (33%)
  blocking collectives  170 us (22%)
  matrix products  150 us (19%)
  other arithmetic  107 us (14%)
  local copies, waits for them, and re-layouts  43.4 us (6%)
  starting transfers between devices  24.4 us (3%)
  between operations  17.2 us (2%)
    all_to_all x4, waiting for transfers between devices, sum_at_owner(): lax.all_to_all(tiles, axis, split_axis=0, concat_axis=0, tiled=True)  51.2 us
    dot_general x4, matrix products, scores_of(): jnp.einsum('qhd,khd->hqk', query_block, key_block, preferred_element_type...  46.3 us
    all_gather x1, blocking collectives, shards(): lax.all_gather(w_out, 'dp', axis=1, tiled=True)  46 us
    all_gather x1, waiting for transfers between devices, shards(): lax.all_gather(w_down, 'dp', axis=1, tiled=True)  38.4 us
    reduce_scatter x1, waiting for transfers between devices, shards(): lax.psum_scatter(jnp.dot(context, full_out, preferred_element_type=jnp.fl...  32.8 us
    all_gather x1, blocking collectives, shards(): lax.all_gather(w_value, 'dp', axis=0, tiled=True)  31.2 us
    all_gather x1, blocking collectives, shards(): lax.all_gather(w_key, 'dp', axis=0, tiled=True)  31.2 us
    all_gather x1, blocking collectives, shards(): lax.all_gather(w_query, 'dp', axis=0, tiled=True)  31 us
  transfers between devices with their start and end apart: 18, of which 12 were waited for; matrix products, arithmetic and copies ran while one was open for 8% of the time, Pallas kernels for 0%

commit v1 on v0

--- a/solution.py
+++ b/solution.py
@@ -1,12 +1,392 @@
+import functools
 import math
 
 import jax
 import jax.numpy as jnp
 from jax import lax
+from jax.experimental import pallas as pl
+from jax.experimental.pallas import tpu as pltpu
 from jax.sharding import PartitionSpec as P
 
+MESH = pl.DeviceIdType.MESH
+BF = jnp.bfloat16
+F32 = jnp.float32
 HD = 64
 WINDOW = 1536
+SEG = 256
+TREE = 5120
+LOG2E = 1.4426950408889634
+NEG = -1e30
+EPS = 1e-6
+
+
+def nt(a, b):
+    return lax.dot_general(a, b, (((1,), (1,)), ((), ())), preferred_element_type=F32)
+
+
+def nn(a, b):
+    return jnp.dot(a, b, preferred_element_type=F32)
+
+
+class Links:
+    def __init__(self, send, recv):
+        self.send, self.recv, self.used = send, recv, 0
+
+    def take(self, count):
+        base = self.used
+        self.used += count
+        return base
+
+    def copy(self, src, dst, send, recv, device):
+        return pltpu.make_async_remote_copy(
+            src_ref=src,
+            dst_ref=dst,
+            send_sem=self.send.at[send],
+            recv_sem=self.recv.at[recv],
+            device_id=device,
+            device_id_type=MESH,
+        )
+
+
+class Spread:
+    def __init__(self, links, base, dp, t, part):
+        self.dp, self.t = dp, t
+        self.out = [
+            links.copy(part(t), part(t), base, base, (dp, t ^ 1)),
+            links.copy(part(t), part(t), base + 1, base + 1, (dp, t ^ 2)),
+            links.copy(part(t ^ 2), part(t ^ 2), base + 2, base + 2, (dp, t ^ 1)),
+        ]
+        self.arrivals = [
+            links.copy(part(t ^ 1), part(t ^ 1), base, base, (dp, t ^ 1)),
+            links.copy(part(t ^ 2), part(t ^ 2), base + 1, base + 1, (dp, t ^ 2)),
+            links.copy(part(t ^ 3), part(t ^ 3), base + 2, base + 2, (dp, t ^ 1)),
+        ]
+
+    def start(self):
+        self.out[1].start()
+        self.out[0].start()
+
+    def forward(self):
+        self.arrivals[1].wait_recv()
+        self.out[2].start()
+
+    def wait(self):
+        self.arrivals[0].wait_recv()
+        self.arrivals[2].wait_recv()
+
+    def finish(self):
+        for copy in self.out:
+            copy.wait_send()
+
+
+class Gather:
+    def __init__(self, links, base, dp, t, slot):
+        self.links, self.base, self.dp, self.t, self.slot = links, base, dp, t, slot
+        self.z, self.y = dp // 2, dp % 2
+
+    def at(self, step):
+        z = lax.rem(self.z + step, 4)
+        return z, z * 2 + self.y
+
+    def along(self, step):
+        z, peer = self.at(step)
+        return self.links.copy(self.slot(self.dp), self.slot(self.dp), self.base + step - 1, self.base + self.z, (peer, self.t))
+
+    def came(self, step):
+        z, peer = self.at(step)
+        return self.links.copy(self.slot(peer), self.slot(peer), self.base + step - 1, self.base + z, (peer, self.t))
+
+    def across(self, step):
+        z, peer = self.at(step)
+        other = z * 2 + (1 - self.y)
+        return self.links.copy(self.slot(peer), self.slot(peer), self.base + 4 + step, self.base + 4 + z, (self.dp ^ 1, self.t))
+
+    def crossed(self, step):
+        z, peer = self.at(step)
+        other = z * 2 + (1 - self.y)
+        return self.links.copy(self.slot(other), self.slot(other), self.base + 4 + step, self.base + 4 + z, (self.dp ^ 1, self.t))
+
+    def start(self):
+        self.across(0).start()
+        for step in (1, 3, 2):
+            self.along(step).start()
+
+    def forward(self, step):
+        self.came(step).wait_recv()
+        self.across(step).start()
+
+    def wait(self):
+        for step in range(4):
+            self.crossed(step).wait_recv()
+
+    def finish(self):
+        for step in range(1, 4):
+            self.along(step).wait_send()
+        for step in range(4):
+            self.across(step).wait_send()
+
+
+def greet(dp, t):
+    barrier = pltpu.get_barrier_semaphore()
+    for step in range(1, 8):
+        pl.semaphore_signal(barrier, inc=1, device_id=(lax.rem(dp + step, 8), t), device_id_type=MESH)
+    for flip in (1, 2):
+        pl.semaphore_signal(barrier, inc=1, device_id=(dp, t ^ flip), device_id_type=MESH)
+    pl.semaphore_wait(barrier, 9)
+
+
+def head_mask(h, rows, width):
+    lane = lax.broadcasted_iota(jnp.int32, (rows, width), 1)
+    return (lane >= h * HD) & (lane < (h + 1) * HD)
+
+
+def block_bias(seg_ref, par_ref, block, back):
+    own = seg_ref[block * SEG]
+    one = par_ref[own]
+    two = par_ref[one]
+    far = block - back
+    near = seg_ref[jnp.maximum(far, 0) * SEG]
+    ok = ((near == own) | (near == one) | (near == two)) & (far >= 0)
+    return jnp.where(ok, jnp.float32(0.0), jnp.float32(NEG))
+
+
+def first_kernel(
+    seg_ref, par_ref, x_ref, cot_ref, wa_ref, wf_ref,
+    n1_ref, a_ref, f_ref, cot_all, wout_ref, q_ref, k_ref, v_ref, ct_ref, l_ref, gain_ref,
+    xe_ref, wq_ref, wk_ref, wv_ref, vt_ref, s_ref, e_ref, tri_ref, send, recv,
+):
+    dp, t = lax.axis_index("dp"), lax.axis_index("tensor")
+    rows = x_ref.shape[0]
+    token = 4 * rows
+    blocks = token // SEG
+    back = WINDOW // SEG
+    lag = WINDOW - token
+    per_tree = TREE // token
+    place = lax.rem(dp, per_tree)
+    links = Links(send, recv)
+    own = lambda p: xe_ref.at[pl.ds(WINDOW + p * rows, rows)]
+    halo = lambda p: xe_ref.at[pl.ds(lag + p * rows, rows)]
+    x_spread = Spread(links, links.take(3), dp, t, own)
+    halo_spread = Spread(links, links.take(3), dp, t, halo)
+    cot_spread = Spread(links, links.take(3), dp, t, lambda p: cot_all.at[pl.ds(p * rows, rows)])
+    wide = wout_ref.shape[0] // 4
+    wout_spread = Spread(links, links.take(3), dp, t, lambda p: wout_ref.at[pl.ds(p * wide, wide)])
+    a_gather = Gather(links, links.take(8), dp, t, lambda s: a_ref.at[s])
+    f_gather = Gather(links, links.take(8), dp, t, lambda s: f_ref.at[s])
+    h1 = links.take(1)
+    halo_out = links.copy(x_ref, halo(t), h1, h1, (lax.rem(dp + 1, 8), t))
+    halo_in = links.copy(x_ref, halo(t), h1, h1, (lax.rem(dp + 7, 8), t))
+    h2 = links.take(1)
+    far_src = xe_ref.at[pl.ds(WINDOW + token - lag, lag)]
+    far_dst = xe_ref.at[pl.ds(0, lag)]
+    far_out = links.copy(far_src, far_dst, h2, h2, (lax.rem(dp + 2, 8), t))
+    far_in = links.copy(far_src, far_dst, h2, h2, (lax.rem(dp + 6, 8), t))
+    c_base = links.take(3 * blocks)
+
+    def c_spread(i):
+        at = pl.multiple_of(i * SEG, SEG)
+        return Spread(
+            links, c_base + 3 * i, dp, t, lambda p: ct_ref.at[pl.ds(p * wide, wide), pl.ds(at, SEG)]
+        )
+
+    greet(dp, t)
+    a_ref[pl.ds(dp, 1)] = wa_ref[...][None]
+    a_gather.start()
+    xe_ref[pl.ds(WINDOW + t * rows, rows), :] = x_ref[...]
+    x_spread.start()
+
+    @pl.when(place < per_tree - 1)
+    def _():
+        halo_out.start()
+
+    @pl.when(place < 1)
+    def _():
+        xe_ref[pl.ds(lag, token), :] = jnp.zeros((token, xe_ref.shape[1]), BF)
+
+    @pl.when(place < 2)
+    def _():
+        xe_ref[pl.ds(0, lag), :] = jnp.zeros((lag, xe_ref.shape[1]), BF)
+
+    row = lax.broadcasted_iota(jnp.int32, (SEG, SEG), 0)
+    col = lax.broadcasted_iota(jnp.int32, (SEG, SEG), 1)
+    tri_ref[0] = jnp.where(row <= col, 0.0, NEG)
+    tri_ref[1] = jnp.where(row > col, 0.0, NEG)
+    cot_all[pl.ds(t * rows, rows), :] = cot_ref[...]
+    f_ref[pl.ds(dp, 1)] = wf_ref[...][None]
+    x_spread.forward()
+    for step in (1, 3, 2):
+        a_gather.forward(step)
+
+    @pl.when(place >= 1)
+    def _():
+        halo_in.wait_recv()
+        halo_spread.start()
+
+    x_spread.wait()
+
+    @pl.when(place < per_tree - 2)
+    def _():
+        far_out.start()
+
+    f_gather.start()
+    a_gather.wait()
+    cols = wq_ref.shape[1]
+    deep = wa_ref.shape[0] - 16
+    weights = a_ref[:, 0:deep, :].reshape(8 * deep, 4 * cols)
+    wq_ref[...] = weights[:, 0:cols]
+    wk_ref[...] = weights[:, cols : 2 * cols]
+    wv_ref[...] = weights[:, 2 * cols : 3 * cols]
+    wout_ref[pl.ds(t * wide, wide), :] = weights[:, 3 * cols : 4 * cols].T
+    gains = jnp.sum(a_ref[:, deep : deep + 16, :].astype(F32), axis=0)
+    gain_ref[...] = gains[0:8]
+
+    def norm_rows(at):
+        x = xe_ref[pl.ds(at, SEG), :].astype(F32)
+        r = lax.rsqrt(jnp.mean(x * x, axis=-1, keepdims=True) + EPS)
+        n = (x * r * gain_ref[0:1, :]).astype(BF)
+        n1_ref[pl.ds(at, SEG), :] = n
+        k_ref[pl.ds(at, SEG), :] = nn(n, wk_ref[...]).astype(BF)
+        v = nn(n, wv_ref[...]).astype(BF)
+        v_ref[pl.ds(at, SEG), :] = v
+        vt_ref[:, pl.ds(at, SEG)] = v.T
+        return n
+
+    def own_rows(i, _):
+        at = pl.multiple_of(i * SEG, SEG)
+        n = norm_rows(WINDOW + at)
+        q_ref[pl.ds(at, SEG), :] = (nn(n, wq_ref[...]).astype(BF).astype(F32) * HD**-0.5).astype(BF)
+        return 0
+
+    lax.fori_loop(0, blocks, own_rows, 0)
+
+    @pl.when(place >= 1)
+    def _():
+        halo_spread.forward()
+        halo_spread.wait()
+
+    wout_spread.start()
+    cot_spread.start()
+
+    @pl.when(place >= 2)
+    def _():
+        far_in.wait_recv()
+
+    def halo_rows(i, _):
+        norm_rows(pl.multiple_of(i * SEG, SEG))
+        return 0
+
+    lax.fori_loop(0, back, halo_rows, 0)
+
+    def attend(i, _):
+        at = pl.multiple_of(i * SEG, SEG)
+        block = dp * blocks + i
+        biases = [block_bias(seg_ref, par_ref, block, back - j) for j in range(back + 1)]
+        q = q_ref[pl.ds(at, SEG), :]
+        for h in range(3):
+            qm = jnp.where(head_mask(h, SEG, cols), q, jnp.zeros_like(q))
+            top = None
+            for j in range(back + 1):
+                s = nt(k_ref[pl.ds(at + j * SEG, SEG), :], qm)
+                if j == 0:
+                    s = s + tri_ref[1]
+                if j == back:
+                    s = s + tri_ref[0]
+                s_ref[h, j * SEG : (j + 1) * SEG, :] = s
+                best = jnp.max(s, axis=0, keepdims=True) + biases[j]
+                top = best if top is None else jnp.maximum(top, best)
+            top = top * LOG2E
+            total = None
+            for j in range(back + 1):
+                e = jnp.exp2(s_ref[h, j * SEG : (j + 1) * SEG, :] * LOG2E - (top - biases[j]))
+                part = jnp.sum(e, axis=0, keepdims=True)
+                total = part if total is None else total + part
+                e_ref[h, j * SEG : (j + 1) * SEG, :] = e.astype(BF)
+            o = nn(vt_ref[h * HD : (h + 1) * HD, pl.ds(at, (back + 1) * SEG)], e_ref[h])
+            ct_ref[pl.ds(t * wide + h * HD, HD), pl.ds(at, SEG)] = (o / total).astype(BF)
+            l_ref[h : h + 1, pl.ds(at, SEG)] = top + jnp.log(total) * LOG2E
+        c_spread(i).start()
+
+        @pl.when(i > 0)
+        def _():
+            c_spread(i - 1).forward()
+
+        @pl.when(i == 1)
+        def _():
+            for step in (1, 3, 2):
+                f_gather.forward(step)
+
+        return 0
+
+    lax.fori_loop(0, blocks, attend, 0)
+    c_spread(blocks - 1).forward()
+    for i in range(blocks):
+        c_spread(i).wait()
+    wout_spread.forward()
+    cot_spread.forward()
+    wout_spread.wait()
+    cot_spread.wait()
+    f_gather.wait()
+    for item in (x_spread, cot_spread, wout_spread, a_gather, f_gather):
+        item.finish()
+    for i in range(blocks):
+        c_spread(i).finish()
+
+    @pl.when(place >= 1)
+    def _():
+        halo_spread.finish()
+
+    @pl.when(place < per_tree - 1)
+    def _():
+        halo_out.wait_send()
+
+    @pl.when(place < per_tree - 2)
+    def _():
+        far_out.wait_send()
+
+
+def first_phase(x, cot, segments, parents, wa, wf):
+    rows, width = x.shape
+    token = 4 * rows
+    ext = token + WINDOW
+    cols = width // 4
+    blocks = token // SEG
+    keys = WINDOW + SEG
+    vmem = pl.BlockSpec(memory_space=pltpu.VMEM)
+    smem = pl.BlockSpec(memory_space=pltpu.SMEM)
+    copies = 3 * 4 + 2 * 8 + 2 + 3 * blocks
+    return pl.pallas_call(
+        first_kernel,
+        out_shape=[
+            jax.ShapeDtypeStruct((ext, width), BF),
+            jax.ShapeDtypeStruct((8,) + wa.shape, BF),
+            jax.ShapeDtypeStruct((8,) + wf.shape, BF),
+            jax.ShapeDtypeStruct((token, width), BF),
+            jax.ShapeDtypeStruct((width, width), BF),
+            jax.ShapeDtypeStruct((token, cols), BF),
+            jax.ShapeDtypeStruct((ext, cols), BF),
+            jax.ShapeDtypeStruct((ext, cols), BF),
+            jax.ShapeDtypeStruct((width, token), BF),
+            jax.ShapeDtypeStruct((8, token), F32),
+            jax.ShapeDtypeStruct((8, width), F32),
+        ],
+        in_specs=[smem, smem, vmem, vmem, vmem, vmem],
+        out_specs=[vmem] * 11,
+        scratch_shapes=[
+            pltpu.VMEM((ext, width), BF),
+            pltpu.VMEM((width, cols), BF),
+            pltpu.VMEM((width, cols), BF),
+            pltpu.VMEM((width, cols), BF),
+            pltpu.VMEM((cols, ext), BF),
+            pltpu.VMEM((3, keys, SEG), F32),
+            pltpu.VMEM((3, keys, SEG), BF),
+            pltpu.VMEM((2, SEG, SEG), F32),
+            pltpu.SemaphoreType.DMA((copies,)),
+            pltpu.SemaphoreType.DMA((copies,)),
+        ],
+        compiler_params=pltpu.CompilerParams(
+            collective_id=0, has_side_effects=True, vmem_limit_bytes=56 << 20
+        ),
+    )(segments, parents, x, cot, wa, wf)
 
 
 epsilon = 1e-06
@@ -319,9 +699,229 @@
     )
 
 
+def fast_shards(
+    layer_input, cotangent, segments, parents, norm1_gain, w_query, w_key, w_value, w_out, norm2_gain, w_up, w_down,
+):
+    dp = lax.axis_index("dp")
+    width = layer_input.shape[1]
+    gains = jnp.zeros((16, width), BF)
+    gains = lax.dynamic_update_slice(gains, norm1_gain[None], (0, dp * norm1_gain.shape[0]))
+    gains = lax.dynamic_update_slice(gains, norm2_gain[None], (1, dp * norm1_gain.shape[0]))
+    wa = jnp.concatenate([jnp.concatenate([w_query, w_key, w_value, w_out.T], axis=1), gains], axis=0)
+    wf = jnp.concatenate([w_up, w_down.T], axis=1)
+    n1, a_all, f_all, incoming_all, wout, queries, keys, values, ct, logs, gain = first_phase(
+        layer_input, cotangent, segments, parents, wa, wf
+    )
+    deep = w_query.shape[0]
+    weights = a_all[:, :deep].reshape(width, width)
+    full_query, full_key, full_value = weights[:, :192], weights[:, 192:384], weights[:, 384:576]
+    full_out = weights[:, 576:].T
+    ffn = f_all.reshape(width, -1)
+    full_up, full_down = ffn[:, :768], ffn[:, 768:].T
+    gain_one, gain_two = gain[0], gain[1]
+    row_count = layer_input.shape[0]
+    token_count = row_count * lax.axis_size("tensor")
+    position = lax.axis_index("dp") * token_count
+    head_width = full_query.shape[1]
+    head_count = head_width // HD
+    scaling = HD ** (-0.5)
+    block_rows = min(640, token_count)
+    block_count = token_count // block_rows
+    span = WINDOW + block_rows
+    hop_count = (WINDOW + token_count - 1) // token_count
+    inputs = layer_input.astype(jnp.float32)
+    factor_one = row_scale(inputs)
+    hat_one = inputs * factor_one
+    normed_all = n1[WINDOW:]
+    pair_all = jnp.concatenate([keys, values], axis=1)
+    seg_padded = jnp.concatenate([jnp.full((WINDOW,), -1, jnp.int32), segments])
+    seg_keys = lax.dynamic_slice_in_dim(seg_padded, position, WINDOW + token_count, 0)
+    seg_query = seg_keys[WINDOW:]
+    parent_one = parent_of(seg_query, parents)
+    parent_two = parent_of(parent_one, parents)
+    query_spots = jnp.arange(block_rows, dtype=jnp.int32)
+    key_spots = jnp.arange(span, dtype=jnp.int32)
+
+    def scores_of(offset):
+        query_block = lax.dynamic_slice_in_dim(queries, offset, block_rows, 0).reshape(
+            block_rows, head_count, HD
+        )
+        pair_block = lax.dynamic_slice_in_dim(pair_all, offset, span, 0)
+        key_block = pair_block[:, :head_width].reshape(span, head_count, HD)
+        value_block = pair_block[:, head_width:].reshape(span, head_count, HD)
+        own_seg = lax.dynamic_slice_in_dim(seg_query, offset, block_rows, 0)
+        up_one = lax.dynamic_slice_in_dim(parent_one, offset, block_rows, 0)
+        up_two = lax.dynamic_slice_in_dim(parent_two, offset, block_rows, 0)
+        near_seg = lax.dynamic_slice_in_dim(seg_keys, offset, span, 0)
+        gap = WINDOW + query_spots[:, None] - key_spots[None, :]
+        same_path = (
+            (near_seg[None, :] == own_seg[:, None])
+            | (near_seg[None, :] == up_one[:, None])
+            | (near_seg[None, :] == up_two[:, None])
+        )
+        allowed = (gap >= 0) & (gap < WINDOW) & same_path
+        raw = (
+            jnp.einsum("qhd,khd->hqk", query_block, key_block, preferred_element_type=jnp.float32)
+        )
+        return (jnp.where(allowed[None], raw, masked_score), query_block, key_block, value_block)
+
+    t = lax.axis_index("tensor")
+    context = lax.dynamic_slice_in_dim(ct, t * 192, 192, 0).T
+    logsum_blocks = (logs[:3] / LOG2E).reshape(3, block_count, block_rows).transpose(1, 0, 2)
+    middle = inputs + lax.psum_scatter(
+        jnp.dot(context, full_out, preferred_element_type=jnp.float32).astype(jnp.bfloat16),
+        "tensor",
+        scatter_dimension=0,
+        tiled=True,
+    ).astype(jnp.float32)
+    factor_two = row_scale(middle)
+    hat_two = middle * factor_two
+    normed_two = (hat_two * gain_two).astype(jnp.bfloat16)
+    normed_two_all = lax.all_gather(normed_two, "tensor", axis=0, tiled=True)
+    upper = jnp.dot(normed_two_all, full_up, preferred_element_type=jnp.float32)
+    active = gelu_exact(upper).astype(jnp.bfloat16)
+    result = middle + lax.psum_scatter(
+        jnp.dot(active, full_down, preferred_element_type=jnp.float32).astype(jnp.bfloat16),
+        "tensor",
+        scatter_dimension=0,
+        tiled=True,
+    ).astype(jnp.float32)
+    incoming = cotangent.astype(jnp.float32)
+    grad_down = jnp.einsum("tf,td->fd", active, incoming_all, preferred_element_type=jnp.float32)
+    grad_active = jnp.einsum(
+        "td,fd->tf", incoming_all, full_down, preferred_element_type=jnp.float32
+    )
+    unused_value, gelu_pull = jax.vjp(gelu_exact, upper)
+    grad_upper = gelu_pull(grad_active)[0].astype(jnp.bfloat16)
+    grad_up = jnp.einsum(
+        "tc,tf->cf", normed_two_all, grad_upper, preferred_element_type=jnp.float32
+    )
+    grad_normed_two = lax.psum_scatter(
+        jnp.einsum("tf,cf->tc", grad_upper, full_up, preferred_element_type=jnp.float32).astype(
+            jnp.bfloat16
+        ),
+        "tensor",
+        scatter_dimension=0,
+        tiled=True,
+    ).astype(jnp.float32)
+    through_two, gain_two_part = norm_backward(grad_normed_two, hat_two, factor_two, gain_two)
+    grad_middle = incoming + through_two
+    grad_middle_all = lax.all_gather(grad_middle.astype(jnp.bfloat16), "tensor", axis=0, tiled=True)
+    grad_out = jnp.einsum("tc,td->cd", context, grad_middle_all, preferred_element_type=jnp.float32)
+    grad_context = jnp.einsum(
+        "td,cd->tc", grad_middle_all, full_out, preferred_element_type=jnp.float32
+    ).astype(jnp.bfloat16)
+
+    def backward_block(block_index, carry):
+        grad_queries, grad_pairs = carry
+        offset = block_index * block_rows
+        scores, query_block, key_block, value_block = scores_of(offset)
+        logsum = lax.dynamic_index_in_dim(logsum_blocks, block_index, 0, keepdims=False)
+        probs = jnp.exp(scores - logsum[..., None])
+        grad_rows = lax.dynamic_slice_in_dim(grad_context, offset, block_rows, 0).reshape(
+            block_rows, head_count, HD
+        )
+        grad_probs = jnp.einsum(
+            "qhd,khd->hqk", grad_rows, value_block, preferred_element_type=jnp.float32
+        )
+        inner = jnp.sum(probs * grad_probs, axis=-1, keepdims=True)
+        grad_scores = (probs * (grad_probs - inner)).astype(jnp.bfloat16)
+        grad_query_block = (
+            jnp.einsum("hqk,khd->qhd", grad_scores, key_block, preferred_element_type=jnp.float32)
+            * scaling
+        )
+        grad_key_block = jnp.einsum("hqk,qhd->khd", grad_scores, query_block, preferred_element_type=jnp.float32)
+        grad_value_block = jnp.einsum(
+            "hqk,qhd->khd",
+            probs.astype(jnp.bfloat16),
+            grad_rows,
+            preferred_element_type=jnp.float32,
+        )
+        grad_queries = lax.dynamic_update_slice_in_dim(
+            grad_queries, grad_query_block.reshape(block_rows, head_width), offset, 0
+        )
+        update = jnp.concatenate(
+            [grad_key_block.reshape(span, head_width), grad_value_block.reshape(span, head_width)],
+            axis=1,
+        )
+        current = lax.dynamic_slice_in_dim(grad_pairs, offset, span, 0)
+        grad_pairs = lax.dynamic_update_slice_in_dim(grad_pairs, current + update, offset, 0)
+        return (grad_queries, grad_pairs)
+
+    start_carry = (
+        jnp.zeros((token_count, head_width), jnp.float32),
+        jnp.zeros((WINDOW + token_count, 2 * head_width), jnp.float32),
+    )
+    grad_queries, grad_pairs = lax.fori_loop(0, block_count, backward_block, start_carry)
+    grad_own = grad_pairs[WINDOW:]
+    for distance in range(1, hop_count + 1):
+        length = min(token_count, WINDOW - (distance - 1) * token_count)
+        first_row = WINDOW - (distance - 1) * token_count - length
+        piece = grad_pairs[first_row : first_row + length]
+        returned = from_behind(piece.astype(jnp.bfloat16), "dp", -distance).astype(piece.dtype)
+        grad_own = grad_own + jnp.pad(returned, ((token_count - length, 0), (0, 0)))
+    grad_keys = grad_own[:, :head_width].astype(jnp.bfloat16)
+    grad_values = grad_own[:, head_width:].astype(jnp.bfloat16)
+    grad_queries_low = grad_queries.astype(jnp.bfloat16)
+    grad_query = jnp.einsum(
+        "tc,tq->cq", normed_all, grad_queries_low, preferred_element_type=jnp.float32
+    )
+    grad_key = jnp.einsum("tc,tq->cq", normed_all, grad_keys, preferred_element_type=jnp.float32)
+    grad_value = jnp.einsum(
+        "tc,tq->cq", normed_all, grad_values, preferred_element_type=jnp.float32
+    )
+    part_query = jnp.einsum(
+        "tq,cq->tc", grad_queries_low, full_query, preferred_element_type=jnp.float32
+    )
+    part_key = jnp.einsum("tq,cq->tc", grad_keys, full_key, preferred_element_type=jnp.float32)
+    part_value = jnp.einsum(
+        "tq,cq->tc", grad_values, full_value, preferred_element_type=jnp.float32
+    )
+    grad_normed = lax.psum_scatter(
+        (part_query + part_key + part_value).astype(jnp.bfloat16),
+        "tensor",
+        scatter_dimension=0,
+        tiled=True,
+    ).astype(jnp.float32)
+    through_one, gain_one_part = norm_backward(grad_normed, hat_one, factor_one, gain_one)
+    grad_inputs = grad_middle + through_one
+    gain_one_sum, gain_two_sum = lax.psum((gain_one_part, gain_two_part), "tensor")
+    summed = (
+        *side_by_side(
+            (
+                gain_one_sum.astype(jnp.bfloat16),
+                grad_query.astype(jnp.bfloat16),
+                grad_key.astype(jnp.bfloat16),
+                grad_value.astype(jnp.bfloat16),
+            ),
+            "dp",
+            0,
+            1,
+        ),
+        sum_at_owner(grad_out.astype(jnp.bfloat16), "dp", 1),
+        *side_by_side(
+            (gain_two_sum.astype(jnp.bfloat16), grad_up.astype(jnp.bfloat16)), "dp", 0, 1
+        ),
+        sum_at_owner(grad_down.astype(jnp.bfloat16), "dp", 1),
+    )
+    return (
+        result.astype(jnp.bfloat16),
+        grad_inputs.astype(jnp.bfloat16),
+        summed[0],
+        summed[1],
+        summed[2],
+        summed[3],
+        summed[4],
+        summed[5],
+        summed[6],
+        summed[7],
+    )
+
+
 def solution(mesh):
+    fast = mesh.shape["dp"] == 8 and mesh.shape["tensor"] == 4
     return jax.shard_map(
-        shards,
+        fast_shards if fast else shards,
         mesh=mesh,
         in_specs=(
             P(("dp", "tensor"), None),

time: 779 us -> 545 us (0.70)
  blocking collectives: 170 us -> 6.36 us
  Pallas kernels: 0 us -> 86.3 us
  waiting for transfers between devices: 259 us -> 184 us
  other arithmetic: 107 us -> 68.3 us
  matrix products: 150 us -> 119 us
    all_gather x4 -> x0, blocking collectives: 139 us -> none  [the longest x1 46 us: shards(): lax.all_gather(w_out, 'dp', axis=1, tiled=True)]
    pallas_call x0 -> x1, Pallas kernels: none -> 86.3 us  [first_phase(): pl.pallas_call(first_kernel, out_shape=[jax.ShapeDtypeStruct((ext, width)...]
    all_gather x6 -> x2, waiting for transfers between devices: 113 us -> 39 us  [the longest x1 21.7 us: fast_shards(): normed_two_all = lax.all_gather(normed_two, 'tensor', axis=0, tiled=True)]
    dot_general x4 -> x2, matrix products: 46.3 us -> 4.74 us  [scores_of(): jnp.einsum('qhd,khd->hqk', query_block, key_block, preferred_element_type...]
    unnamed x1 -> x0, blocking collectives: 23.7 us -> none
    reduce_sum x2 -> x0, other arithmetic: 21 us -> none  [forward_block(): denominator = jnp.sum(exponent, axis=-1, keepdims=True)]
    dot_general x2, matrix products: 16.2 us -> 29.1 us  [backward_block(): jnp.einsum('qhd,khd->hqk', grad_rows, value_block, preferred_element_type...]
    dot_general x20 -> x15, matrix products: 76.3 us -> 64.4 us  [the longest x1 24.2 us: fast_shards(): upper = jnp.dot(normed_two_all, full_up, preferred_element_type=jnp.float32)]
  transfers between devices with their start and end apart: 18 -> 12, of which waited for: 12 -> 8; matrix products, arithmetic and copies ran while one was open for 8% -> 10% of each run, Pallas kernels for 0% -> 0%
where the time goes in v1:
time: 545 us; the launch traced here: 538 us
  waiting for transfers between devices  184 us (34%)
  matrix products  119 us (22%)
  Pallas kernels  86.3 us (16%)
  other arithmetic  68.3 us (13%)
  local copies, waits for them, and re-layouts  37.8 us (7%)
  starting transfers between devices  20.5 us (4%)
  between operations  14.8 us (3%)
  blocking collectives  6.36 us (1%)
    pallas_call x1, Pallas kernels, first_phase(): pl.pallas_call(first_kernel, out_shape=[jax.ShapeDtypeStruct((ext, width)...  86.3 us
    all_to_all x4, waiting for transfers between devices, sum_at_owner(): lax.all_to_all(tiles, axis, split_axis=0, concat_axis=0, tiled=True)  52.2 us
    reduce_scatter x1, waiting for transfers between devices, fast_shards(): lax.psum_scatter(jnp.dot(context, full_out, preferred_element_type=jnp.fl...  34.2 us
    reduce_scatter x1, waiting for transfers between devices, fast_shards(): lax.psum_scatter(jnp.einsum('tf,cf->tc', grad_upper, full_up, preferred_e...  30.7 us
    dot_general x2, matrix products, backward_block(): jnp.einsum('qhd,khd->hqk', grad_rows, value_block, preferred_element_type...  29.1 us
    ppermute x2, waiting for transfers between devices, from_behind(): return lax.ppermute(block, axis, route)  27.5 us
    dot_general x1, matrix products, fast_shards(): upper = jnp.dot(normed_two_all, full_up, preferred_element_type=jnp.float32)  24.2 us
    convert_element_type x2, other arithmetic, backward_block(): grad_scores = (probs * (grad_probs - inner)).astype(jnp.bfloat16)  24.2 us
  transfers between devices with their start and end apart: 12, of which 8 were waited for; matrix products, arithmetic and copies ran while one was open for 10% of the time, Pallas kernels for 0%

profile of v1, /device:TPU:0, one launch (start us, length us, event | category | flops | bytes accessed | tf_op | source)
XLA Modules:
  0.0 538.1 jit_solution(15054918839108180428)
XLA Ops:
  13.1 86.3 %shard_map.195 = (bf16[2816,768]{1,0:T(8,128)(2,1)}, bf16[8,112,768]{2,1,0:T(8,128)(2,1)}, bf16[8,96,1536]{2,1,0:T(8,128)(2,1)}, bf16[1280,768]{1,0:T(8,128)(2,1...) custom-call(s32[10240]{0:T(1024)} %seg_ref.1, ...), custom_call_target="tpu_custom_call" | custom-call | tf_op jit(solution)/shard_map/pallas_call | solution.py:357
  105.9 34.2 %reduce-scatter.5.cloned.1.call-done = bf16[320,768]{1,0:T(8,128)(2,1)} async-done(((bf16[1280,768]{1,0:T(8,128)(2,1)}), bf16[320,768]{1,0:T(8,128)(2,1)}) %reduce-scatter.5.cloned.1.call-update) | async-done | bytes 491536 | tf_op jit(solution)/shard_map/reduce_scatter | solution.py:771
  143.7 21.7 %all-gather.3.cloned.1.call-done = bf16[1280,768]{1,0:T(8,128)(2,1)} async-done(((bf16[320,768]{1,0:T(8,128)(2,1)}), bf16[1280,768]{1,0:T(8,128)(2,1)}) %all-gather.3.cloned.1.call-update) | async-done | bytes 1966096 | tf_op jit(solution)/shard_map/all_gather | solution.py:780
  165.5 24.2 %multiply_convert_fusion.1 = (bf16[1280,768]{1,0:T(8,128)(2,1)}, f32[1280,768]{1,0:T(8,128)S(1)}, f32[1280,768]{1,0:T(8,128)S(1)}) fusion(bf16[1280,768]{1,0:T(8,128)(2,1)} %all-gather.3.cloned.1.call-done, bf16[768,1536]{1,0:T(8,128)(2,1)} %bitcast.117), kind=kOutput, calls=%fused_computation.28 | convolution fusion | flops 1573847040 | bytes 12976128 | tf_op jit(solution)/shard_map/dot_general | solution.py:781
  196.7 30.7 %reduce-scatter.9.cloned.1.call-done = bf16[320,768]{1,0:T(8,128)(2,1)} async-done(((bf16[1280,768]{1,0:T(8,128)(2,1)}), bf16[320,768]{1,0:T(8,128)(2,1)}) %reduce-scatter.9.cloned.1.call-update) | async-done | bytes 491536 | tf_op jit(solution)/shard_map/reduce_scatter | solution.py:799
  237.1 17.3 %all-gather.5.cloned.1.call-done = bf16[1280,768]{1,0:T(8,128)(2,1)} async-done(((bf16[320,768]{1,0:T(8,128)(2,1)}), bf16[1280,768]{1,0:T(8,128)(2,1)}) %all-gather.5.cloned.1.call-update) | async-done | bytes 1966096 | tf_op jit(solution)/shard_map/all_gather | solution.py:809
  260.0 108.6 %while.16 = (s32[]{:T(128)}, bf16[1280,192]{0,1:T(8,128)(2,1)}, f32[2816,384]{0,1:T(8,128)}, bf16[2816,384]{1,0:T(8,128)(2,1)}, s32[2816]{0:T(1024)S(1)}, /*inde...) while((s32[]{:T(128)}, bf16[1280,192]{0,1:T(8,128)(2,1)}, ...), condition=%wide.region_10.11_spmd.clone, body=%wide.region_8.0_spmd.clone.sunk | while | flops 2739845888 | bytes 280904128 | solution.py:855
  261.6 4.8 fusion.132
  274.3 6.2 %fusion.133 = f32[3,64,2176]{2,1,0:T(8,128)} fusion(bf16[640,3,64]{0,2,1:T(8,128)(2,1)S(1)} %bitcast.99, f32[3,640,2176]{2,1,0:T(8,128)S(1)} %fusion.131, f32[3,640]{1,0:T(4,128)S(1)} %copy-done.8, pred[640,2176]{1,0:T(8,128)(4,1)S(1)} %fusion.132), kind=kOutput, calls=%fused_computation.6.clone.1 | convolution fusion | flops 547307520 | bytes 20028928 | tf_op jit(solution)/shard_map/while/body/eval_jaxpr/hqk,qhd->khd/dot_general | solution.py:834
  280.5 14.6 %multiply_reduce_fusion.3 = (f32[3,640]{1,0:T(4,128)S(1)}, f32[3,640,2176]{2,1,0:T(8,128)}) fusion(f32[3,640,2176]{2,1,0:T(8,128)} %copy-done, f32[3,640]{1,0:T(4,128)S(1)} %copy-done.8, pred[640,2176]{1,0:T(8,128)(4,1)S(1)} %fusion.132, bf16[640,3,64]{0,2,1:T(8,128)(2,1)S(1)} %bitcast.100, bf16[2176,3,64]{0,2,1:T(8,128)(2,1)S(1)} %bitcast.97), kind=kOutput, calls=%fused_computation.3.clone.1 | convolution fusion | flops 551483520 | bytes 35912704 | tf_op jit(solution)/shard_map/while/body/eval_jaxpr/qhd,khd->hqk/dot_general | solution.py:824
  295.1 12.1 %multiply_convert_fusion.4 = bf16[3,640,2176]{2,1,0:T(8,128)(2,1)S(1)} fusion(f32[3,640,2176]{2,1,0:T(8,128)} %get-tuple-element.479, f32[3,640,2176]{2,1,0:T(8,128)} %copy-done, f32[3,640]{1,0:T(4,128)S(1)} %get-tuple-element.480, f32[3,640]{1,0:T(4,128)S(1)} %copy-done.8, pred[640,2176]{1,0:T(8,128)(4,1)S(1)} %fusion.132), kind=kLoop, calls=%fused_computation.2.clone.1 | loop fusion | flops 20889600 | bytes 43187200 | tf_op jit(solution)/shard_map/while/body/eval_jaxpr/convert_element_type | solution.py:828
  315.6 4.8 fusion.132
  328.3 6.2 %fusion.133 = f32[3,64,2176]{2,1,0:T(8,128)} fusion(bf16[640,3,64]{0,2,1:T(8,128)(2,1)S(1)} %bitcast.99, f32[3,640,2176]{2,1,0:T(8,128)S(1)} %fusion.131, f32[3,640]{1,0:T(4,128)S(1)} %copy-done.8, pred[640,2176]{1,0:T(8,128)(4,1)S(1)} %fusion.132), kind=kOutput, calls=%fused_computation.6.clone.1 | convolution fusion | flops 547307520 | bytes 20028928 | tf_op jit(solution)/shard_map/while/body/eval_jaxpr/hqk,qhd->khd/dot_general | solution.py:834
  334.5 14.6 %multiply_reduce_fusion.3 = (f32[3,640]{1,0:T(4,128)S(1)}, f32[3,640,2176]{2,1,0:T(8,128)}) fusion(f32[3,640,2176]{2,1,0:T(8,128)} %copy-done, f32[3,640]{1,0:T(4,128)S(1)} %copy-done.8, pred[640,2176]{1,0:T(8,128)(4,1)S(1)} %fusion.132, bf16[640,3,64]{0,2,1:T(8,128)(2,1)S(1)} %bitcast.100, bf16[2176,3,64]{0,2,1:T(8,128)(2,1)S(1)} %bitcast.97), kind=kOutput, calls=%fused_computation.3.clone.1 | convolution fusion | flops 551483520 | bytes 35912704 | tf_op jit(solution)/shard_map/while/body/eval_jaxpr/qhd,khd->hqk/dot_general | solution.py:824
  349.1 12.1 %multiply_convert_fusion.4 = bf16[3,640,2176]{2,1,0:T(8,128)(2,1)S(1)} fusion(f32[3,640,2176]{2,1,0:T(8,128)} %get-tuple-element.479, f32[3,640,2176]{2,1,0:T(8,128)} %copy-done, f32[3,640]{1,0:T(4,128)S(1)} %get-tuple-element.480, f32[3,640]{1,0:T(4,128)S(1)} %copy-done.8, pred[640,2176]{1,0:T(8,128)(4,1)S(1)} %fusion.132), kind=kLoop, calls=%fused_computation.2.clone.1 | loop fusion | flops 20889600 | bytes 43187200 | tf_op jit(solution)/shard_map/while/body/eval_jaxpr/convert_element_type | solution.py:828
  374.6 27.5 %collective-permute-done.1 = bf16[256,384]{0,1:T(8,128)(2,1)S(1)} collective-permute-done((bf16[256,384]{0,1:T(8,128)(2,1)S(1)}, bf16[256,384]{0,1:T(8,128)(2,1)S(1)}, u32[]{:S(2)}, u32[]{:S(2)}) %collective-permute-start.1) | collective-permute-done | bytes 196640 | tf_op jit(solution)/shard_map/ppermute | solution.py:399
  407.0 4.3 convolution_convert_fusion.4
  415.1 4.9 convolution_convert_fusion.2
  431.3 12.0 %all-to-all-done.3 = bf16[8,768,96]{1,2,0:T(8,128)(2,1)S(1)} async-done(((bf16[8,768,96]{1,2,0:T(8,128)(2,1)}), bf16[8,768,96]{1,2,0:T(8,128)(2,1)S(1)}, u32[]{:S(2)}, u32[]{:S(2)}) %all-to-all-start.3) | async-done | bytes 1179680 | tf_op jit(solution)/shard_map/all_to_all | solution.py:410
  453.6 6.4 %all-reduce.2 = (bf16[768]{0:T(1024)(128)(2,1)S(1)}, bf16[768]{0:T(1024)(128)(2,1)S(1)}) all-reduce(f32[768]{0:T(1024)S(1)} %get-tuple-element.359, f32[768]{0:T(1024)S(1)} %copy-done.44), channel_id=1, replica_groups=mesh['dp'=8,'tensor'=4] {'tensor'}, use_global_device_ids=true, to_apply=%region_14.15 | all-reduce | flops 1536 | bytes 9216 | tf_op jit(solution)/shard_map/psum | solution.py:888
  462.0 6.1 %all-to-all-start = ((bf16[8,96,577]{2,1,0:T(8,128)(2,1)}), bf16[8,96,577]{2,1,0:T(8,128)(2,1)S(1)}, u32[]{:S(2)}, u32[]{:S(2)}) async-start(bf16[8,96,577]{2,1,0:T(8,128)(2,1)} %pad_maximum_fusion.2), calls=%async_computation.4 | async-start | bytes 1966080 | tf_op jit(solution)/shard_map/all_to_all | solution.py:410
  468.1 5.0 convolution_convert_fusion.5
  476.5 15.6 %all-to-all-done = bf16[8,96,577]{2,1,0:T(8,128)(2,1)S(1)} async-done(((bf16[8,96,577]{2,1,0:T(8,128)(2,1)}), bf16[8,96,577]{2,1,0:T(8,128)(2,1)S(1)}, u32[]{:S(2)}, u32[]{:S(2)}) %all-to-all-start) | async-done | bytes 886304 | tf_op jit(solution)/shard_map/all_to_all | solution.py:410
  504.7 24.6 %all-to-all-done.2 = bf16[8,96,769]{2,1,0:T(8,128)(2,1)S(1)} async-done(((bf16[8,96,769]{2,1,0:T(8,128)(2,1)}), bf16[8,96,769]{2,1,0:T(8,128)(2,1)S(1)}, u32[]{:S(2)}, u32[]{:S(2)}) %all-to-all-start.2) | async-done | bytes 1181216 | tf_op jit(solution)/shard_map/all_to_all | solution.py:410
  (267 shorter events, 125.9 us)
Async XLA Ops:
  7.2 132.9 %reduce-scatter.5.cloned.1.call-start = ((), (), s32[]{:S(2)}) async-start(), calls=%async_computation.8 | async-start | bytes 2457600 | tf_op jit(solution)/shard_map/reduce_scatter | solution.py:771
  99.4 40.7 %copy-start.4 = (bf16[320,768]{1,0:T(8,128)(2,1)S(1)}, bf16[320,768]{1,0:T(8,128)(2,1)}, u32[]{:S(2)}) copy-start(bf16[320,768]{1,0:T(8,128)(2,1)} %x_ref.1) | copy-start | bytes 1474564
  100.8 153.6 %copy-start.9 = (bf16[8,96,768]{2,1,0:T(8,128)(2,1)}, bf16[8,96,768]{2,1,0:T(8,128)(2,1)S(1)}, u32[]{:S(2)}) copy-start(bf16[8,96,768]{2,1,0:T(8,128)(2,1)S(1)} %slice.69) | copy-start | bytes 3538948
  104.5 61.0 %all-gather.3.cloned.1.call-start = ((), (), s32[]{:S(2)}) async-start(), calls=%async_computation.9 | async-start | bytes 2457600 | tf_op jit(solution)/shard_map/all_gather | solution.py:780
  105.9 123.7 %copy-start.34 = (f32[768]{0:T(1024)}, f32[768]{0:T(1024)S(1)}, u32[]{:S(2)}) copy-start(f32[768]{0:T(1024)S(1)} %get-tuple-element.363) | copy-start | bytes 9220
  141.4 88.2 %copy-start.38 = (f32[320]{0:T(512)}, f32[320]{0:T(512)S(1)}, u32[]{:S(2)}) copy-start(f32[320]{0:T(512)S(1)} %add_rsqrt_fusion.1) | copy-start | bytes 3844
  143.4 84.0 %reduce-scatter.9.cloned.1.call-start = ((), (), s32[]{:S(2)}) async-start(), calls=%async_computation.11 | async-start | bytes 2457600 | tf_op jit(solution)/shard_map/reduce_scatter | solution.py:799
  193.5 33.9 %copy-start.6 = (bf16[320,768]{1,0:T(8,128)(2,1)S(1)}, bf16[320,768]{1,0:T(8,128)(2,1)}, u32[]{:S(2)}) copy-start(bf16[320,768]{1,0:T(8,128)(2,1)} %reduce-scatter.5.cloned.1.call-done) | copy-start | bytes 1474564
  193.5 36.6 %copy-start.16 = (bf16[320,768]{1,0:T(8,128)(2,1)S(1)}, bf16[320,768]{1,0:T(8,128)(2,1)}, u32[]{:S(2)}) copy-start(bf16[320,768]{1,0:T(8,128)(2,1)} %cot_ref.1) | copy-start | bytes 1474564
  196.6 35.9 %copy-start.24 = (bf16[1280,192]{1,0:T(8,128)(2,1)S(1)}, bf16[1280,192]{1,0:T(8,128)(2,1)}, u32[]{:S(2)}) copy-start(bf16[1280,192]{1,0:T(8,128)(2,1)} %get-tuple-element.344) | copy-start | bytes 1474564
  196.6 36.1 %copy-start.27 = (s32[10240]{0:T(1024)S(1)}, s32[10240]{0:T(1024)}, u32[]{:S(2)}) copy-start(s32[10240]{0:T(1024)} %seg_ref.1) | copy-start | bytes 122884
  196.6 36.3 %copy-start.47 = (s32[26]{0:T(128)S(1)}, s32[26]{0:T(128)}, u32[]{:S(2)}) copy-start(s32[26]{0:T(128)} %par_ref.1) | copy-start | bytes 316
  196.6 57.8 %all-gather.5.cloned.1.call-start = ((), (), s32[]{:S(2)}) async-start(), calls=%async_computation.12 | async-start | bytes 2457600 | tf_op jit(solution)/shard_map/all_gather | solution.py:809
  232.4 219.1 %reduce-scatter.11.cloned.1.call-start = ((), (), s32[]{:S(2)}) async-start(), calls=%async_computation.13 | async-start | bytes 2457600 | tf_op jit(solution)/shard_map/reduce_scatter | solution.py:880
  371.3 30.9 %collective-permute-start = (bf16[1280,384]{0,1:T(8,128)(2,1)S(1)}, bf16[1280,384]{0,1:T(8,128)(2,1)S(1)}, u32[]{:S(2)}, u32[]{:S(2)}) collective-permute-start(bf16[1280,384]{0,1:T(8,128)(2,1)S(1)} %slice.92), channel_id=1, source_target_pairs={{4,0},{8,4},{12,8},{16,12},{20,16},{24,20},{28,24},{5,1},{9,5},{13... | collective-permute-start | bytes 2949128 | tf_op jit(solution)/shard_map/ppermute | solution.py:399
  372.6 29.6 %collective-permute-start.1 = (bf16[256,384]{0,1:T(8,128)(2,1)S(1)}, bf16[256,384]{0,1:T(8,128)(2,1)S(1)}, u32[]{:S(2)}, u32[]{:S(2)}) collective-permute-start(bf16[256,384]{0,1:T(8,128)(2,1)S(1)} %slice.93), channel_id=1, source_target_pairs={{8,0},{12,4},{16,8},{20,12},{24,16},{28,20},{9,1},{13,5},{17,9},{2... | collective-permute-start | bytes 589832 | tf_op jit(solution)/shard_map/ppermute | solution.py:399
  411.3 32.0 %all-to-all-start.3 = ((bf16[8,768,96]{1,2,0:T(8,128)(2,1)}), bf16[8,768,96]{1,2,0:T(8,128)(2,1)S(1)}, u32[]{:S(2)}, u32[]{:S(2)}) async-start(bf16[8,768,96]{1,2,0:T(8,128)(2,1)} %bitcast.15), calls=%async_computation.7 | async-start | bytes 2359296 | tf_op jit(solution)/shard_map/all_to_all | solution.py:410
  415.0 84.9 %reduce-scatter.7.cloned.1.call-start = ((), (), s32[]{:S(2)}) async-start(), calls=%async_computation.10 | async-start | bytes 2457600 | tf_op jit(solution)/shard_map/reduce_scatter | solution.py:783
  420.0 31.5 %copy-start.43 = (f32[320]{0:T(512)}, f32[320]{0:T(512)S(1)}, u32[]{:S(2)}) copy-start(f32[320]{0:T(512)S(1)} %add_rsqrt_fusion) | copy-start | bytes 3844
  443.3 18.7 %all-to-all-start.1 = ((bf16[8,192,96]{2,1,0:T(8,128)(2,1)}), bf16[8,192,96]{2,1,0:T(8,128)(2,1)}, u32[]{:S(2)}, u32[]{:S(2)}) async-start(bf16[8,192,96]{2,1,0:T(8,128)(2,1)} %bitcast.55), calls=%async_computation.5 | async-start | bytes 786432 | tf_op jit(solution)/shard_map/all_to_all | solution.py:410
  462.0 30.0 %all-to-all-start = ((bf16[8,96,577]{2,1,0:T(8,128)(2,1)}), bf16[8,96,577]{2,1,0:T(8,128)(2,1)S(1)}, u32[]{:S(2)}, u32[]{:S(2)}) async-start(bf16[8,96,577]{2,1,0:T(8,128)(2,1)} %pad_maximum_fusion.2), calls=%async_computation.4 | async-start | bytes 1966080 | tf_op jit(solution)/shard_map/all_to_all | solution.py:410
  473.1 26.9 %copy-start.39 = (f32[320]{0:T(512)S(1)}, f32[320]{0:T(512)}, u32[]{:S(2)}) copy-start(f32[320]{0:T(512)} %copy-done.38) | copy-start | bytes 3844
  473.1 26.9 %copy-start.42 = (f32[320]{0:T(512)S(1)}, f32[320]{0:T(512)}, u32[]{:S(2)}) copy-start(f32[320]{0:T(512)} %copy-done.41) | copy-start | bytes 3844
  493.0 36.4 %all-to-all-start.2 = ((bf16[8,96,769]{2,1,0:T(8,128)(2,1)}), bf16[8,96,769]{2,1,0:T(8,128)(2,1)S(1)}, u32[]{:S(2)}, u32[]{:S(2)}) async-start(bf16[8,96,769]{2,1,0:T(8,128)(2,1)} %pad_maximum_fusion.1), calls=%async_computation.6 | async-start | bytes 2752512 | tf_op jit(solution)/shard_map/all_to_all | solution.py:410
  (65 other events, 351.8 us)
Sparse Core Ops, SparseCore 0:
  104.6 35.4 reduce-scatter.4
  143.6 21.8 all-gather.2
  196.7 30.6 reduce-scatter.8
  232.5 21.8 all-gather.4
  407.2 28.7 reduce-scatter.10
  438.6 30.8 reduce-scatter.6

commit v2 on v0

--- a/solution.py
+++ b/solution.py
@@ -1,12 +1,861 @@
+import functools
 import math
 
 import jax
 import jax.numpy as jnp
 from jax import lax
+from jax.experimental import pallas as pl
+from jax.experimental.pallas import tpu as pltpu
 from jax.sharding import PartitionSpec as P
 
+MESH = pl.DeviceIdType.MESH
+BF = jnp.bfloat16
+F32 = jnp.float32
 HD = 64
 WINDOW = 1536
+SEG = 256
+TREE = 5120
+LOG2E = 1.4426950408889634
+NEG = -1e30
+EPS = 1e-6
+
+
+def nt(a, b):
+    return lax.dot_general(a, b, (((1,), (1,)), ((), ())), preferred_element_type=F32)
+
+
+def nn(a, b):
+    return jnp.dot(a, b, preferred_element_type=F32)
+
+
+def tn(a, b):
+    return lax.dot_general(a, b, (((0,), (0,)), ((), ())), preferred_element_type=F32)
+
+
+class Links:
+    def __init__(self, send, recv):
+        self.send, self.recv, self.used = send, recv, 0
+
+    def take(self, count):
+        base = self.used
+        self.used += count
+        return base
+
+    def copy(self, src, dst, send, recv, device):
+        return pltpu.make_async_remote_copy(
+            src_ref=src,
+            dst_ref=dst,
+            send_sem=self.send.at[send],
+            recv_sem=self.recv.at[recv],
+            device_id=device,
+            device_id_type=MESH,
+        )
+
+
+class Spread:
+    def __init__(self, links, base, dp, t, part):
+        self.links, self.base, self.dp, self.t, self.part = links, base, dp, t, part
+
+    def leave(self, i):
+        flip, what = ((1, 0), (2, 0), (1, 2))[i]
+        ref = self.part(self.t ^ what)
+        return self.links.copy(ref, ref, self.base + i, self.base + i, (self.dp, self.t ^ flip))
+
+    def come(self, i):
+        flip, what = ((1, 1), (2, 2), (1, 3))[i]
+        ref = self.part(self.t ^ what)
+        return self.links.copy(ref, ref, self.base + i, self.base + i, (self.dp, self.t ^ flip))
+
+    def start(self):
+        self.leave(1).start()
+        self.leave(0).start()
+
+    def forward(self):
+        self.come(1).wait_recv()
+        self.leave(2).start()
+
+    def wait(self):
+        self.come(0).wait_recv()
+        self.come(2).wait_recv()
+
+    def finish(self):
+        for i in range(3):
+            self.leave(i).wait_send()
+
+
+class Gather:
+    def __init__(self, links, base, dp, t, slot):
+        self.links, self.base, self.dp, self.t, self.slot = links, base, dp, t, slot
+        self.z, self.y = dp // 2, dp % 2
+
+    def at(self, step):
+        z = lax.rem(self.z + step, 4)
+        return z, z * 2 + self.y
+
+    def along(self, step):
+        z, peer = self.at(step)
+        return self.links.copy(self.slot(self.dp), self.slot(self.dp), self.base + step - 1, self.base + self.z, (peer, self.t))
+
+    def came(self, step):
+        z, peer = self.at(step)
+        return self.links.copy(self.slot(peer), self.slot(peer), self.base + step - 1, self.base + z, (peer, self.t))
+
+    def across(self, step):
+        z, peer = self.at(step)
+        return self.links.copy(self.slot(peer), self.slot(peer), self.base + 4 + step, self.base + 4 + z, (self.dp ^ 1, self.t))
+
+    def crossed(self, step):
+        z, peer = self.at(step)
+        other = z * 2 + (1 - self.y)
+        return self.links.copy(self.slot(other), self.slot(other), self.base + 4 + step, self.base + 4 + z, (self.dp ^ 1, self.t))
+
+    def start(self):
+        self.across(0).start()
+        for step in (1, 3, 2):
+            self.along(step).start()
+
+    def forward(self, step):
+        self.came(step).wait_recv()
+        self.across(step).start()
+
+    def wait(self):
+        for step in range(4):
+            self.crossed(step).wait_recv()
+
+    def finish(self):
+        for step in range(1, 4):
+            self.along(step).wait_send()
+        for step in range(4):
+            self.across(step).wait_send()
+
+
+def greet(dp, t):
+    barrier = pltpu.get_barrier_semaphore()
+    for step in range(1, 8):
+        pl.semaphore_signal(barrier, inc=1, device_id=(lax.rem(dp + step, 8), t), device_id_type=MESH)
+    for flip in (1, 2, 3):
+        pl.semaphore_signal(barrier, inc=1, device_id=(dp, t ^ flip), device_id_type=MESH)
+    pl.semaphore_wait(barrier, 10)
+
+
+def head_mask(h, rows, width):
+    lane = lax.broadcasted_iota(jnp.int32, (rows, width), 1)
+    return (lane >= h * HD) & (lane < (h + 1) * HD)
+
+
+def block_bias(seg_ref, par_ref, block, back):
+    own = seg_ref[block * SEG]
+    one = par_ref[own]
+    two = par_ref[one]
+    far = block - back
+    near = seg_ref[jnp.maximum(far, 0) * SEG]
+    ok = ((near == own) | (near == one) | (near == two)) & (far >= 0)
+    return jnp.where(ok, jnp.float32(0.0), jnp.float32(NEG))
+
+
+def first_kernel(
+    seg_ref, par_ref, x_ref, cot_ref, wa_ref, wf_ref,
+    n1_ref, n2_ref, mid_ref, f_ref, cot_all, wout_ref, q_ref, k_ref, v_ref, ct_ref, l_ref, gain_ref, wq_ref, wk_ref, wv_ref,
+    a_ref, xe_ref, vt_ref, s_ref, e_ref, tri_ref, mids_ref, send, recv,
+):
+    dp, t = lax.axis_index("dp"), lax.axis_index("tensor")
+    rows = x_ref.shape[0]
+    token = 4 * rows
+    blocks = token // SEG
+    back = WINDOW // SEG
+    lag = WINDOW - token
+    per_tree = TREE // token
+    place = lax.rem(dp, per_tree)
+    links = Links(send, recv)
+    own = lambda p: xe_ref.at[pl.ds(WINDOW + p * rows, rows)]
+    halo = lambda p: xe_ref.at[pl.ds(lag + p * rows, rows)]
+    x_spread = Spread(links, links.take(3), dp, t, own)
+    halo_spread = Spread(links, links.take(3), dp, t, halo)
+    cot_spread = Spread(links, links.take(3), dp, t, lambda p: cot_all.at[pl.ds(p * rows, rows)])
+    wide = wout_ref.shape[0] // 4
+    wout_spread = Spread(links, links.take(3), dp, t, lambda p: wout_ref.at[pl.ds(p * wide, wide)])
+    a_gather = Gather(links, links.take(8), dp, t, lambda s: a_ref.at[s])
+    f_gather = Gather(links, links.take(8), dp, t, lambda s: f_ref.at[s])
+    h1 = links.take(1)
+    h2 = links.take(1)
+    halo_copy = lambda: links.copy(x_ref, halo(t), h1, h1, (lax.rem(dp + 1, 8), t))
+    far_copy = lambda: links.copy(
+        xe_ref.at[pl.ds(WINDOW + token - lag, lag)], xe_ref.at[pl.ds(0, lag)], h2, h2, (lax.rem(dp + 2, 8), t)
+    )
+    c_base = links.take(3 * blocks)
+
+    def c_spread(i):
+        at = pl.multiple_of(i * SEG, SEG)
+        return Spread(
+            links, c_base + 3 * i, dp, t, lambda p: ct_ref.at[pl.ds(p * wide, wide), pl.ds(at, SEG)]
+        )
+
+    greet(dp, t)
+    a_ref[pl.ds(dp, 1)] = wa_ref[...][None]
+    a_gather.start()
+    xe_ref[pl.ds(WINDOW + t * rows, rows), :] = x_ref[...]
+    x_spread.start()
+
+    @pl.when(place < per_tree - 1)
+    def _():
+        halo_copy().start()
+
+    @pl.when(place < 1)
+    def _():
+        xe_ref[pl.ds(lag, token), :] = jnp.zeros((token, xe_ref.shape[1]), BF)
+
+    @pl.when(place < 2)
+    def _():
+        xe_ref[pl.ds(0, lag), :] = jnp.zeros((lag, xe_ref.shape[1]), BF)
+
+    row = lax.broadcasted_iota(jnp.int32, (SEG, SEG), 0)
+    col = lax.broadcasted_iota(jnp.int32, (SEG, SEG), 1)
+    tri_ref[0] = jnp.where(row <= col, 0.0, NEG)
+    tri_ref[1] = jnp.where(row > col, 0.0, NEG)
+    cot_all[pl.ds(t * rows, rows), :] = cot_ref[...]
+    f_ref[pl.ds(dp, 1)] = wf_ref[...][None]
+    x_spread.forward()
+    for step in (1, 3, 2):
+        a_gather.forward(step)
+
+    @pl.when(place >= 1)
+    def _():
+        halo_copy().wait_recv()
+        halo_spread.start()
+
+    x_spread.wait()
+
+    @pl.when(place < per_tree - 2)
+    def _():
+        far_copy().start()
+
+    f_gather.start()
+    a_gather.wait()
+    cols = wq_ref.shape[1]
+    deep = wa_ref.shape[0] - 16
+    weights = a_ref[:, 0:deep, :].reshape(8 * deep, 4 * wide)
+    for j, ref in enumerate((wq_ref, wk_ref, wv_ref)):
+        ref[...] = jnp.concatenate(
+            [weights[:, j * wide : (j + 1) * wide], jnp.zeros((8 * deep, cols - wide), BF)], axis=1
+        )
+    wout_ref[pl.ds(t * wide, wide), :] = weights[:, 3 * wide : 4 * wide].T
+    gains = jnp.sum(a_ref[:, deep : deep + 16, :].astype(F32), axis=0)
+    gain_ref[...] = gains[0:8]
+
+    def norm_rows(at):
+        x = xe_ref[pl.ds(at, SEG), :].astype(F32)
+        r = lax.rsqrt(jnp.mean(x * x, axis=-1, keepdims=True) + EPS)
+        n = (x * r * gain_ref[0:1, :]).astype(BF)
+        k_ref[pl.ds(at, SEG), :] = nn(n, wk_ref[...]).astype(BF)
+        v = nn(n, wv_ref[...]).astype(BF)
+        v_ref[pl.ds(at, SEG), :] = v
+        vt_ref[:, pl.ds(at, SEG)] = v.T
+        return n
+
+    def own_rows(i, _):
+        at = pl.multiple_of(i * SEG, SEG)
+        n = norm_rows(WINDOW + at)
+        n1_ref[pl.ds(at, SEG), :] = n
+        q_ref[pl.ds(at, SEG), :] = (nn(n, wq_ref[...]).astype(BF).astype(F32) * HD**-0.5).astype(BF)
+        return 0
+
+    lax.fori_loop(0, blocks, own_rows, 0)
+
+    @pl.when(place >= 1)
+    def _():
+        halo_spread.forward()
+        halo_spread.wait()
+
+    wout_spread.start()
+    cot_spread.start()
+
+    @pl.when(place >= 2)
+    def _():
+        far_copy().wait_recv()
+
+    def halo_rows(i, _):
+        norm_rows(pl.multiple_of(i * SEG, SEG))
+        return 0
+
+    lax.fori_loop(0, back, halo_rows, 0)
+
+    def attend(i, _):
+        at = pl.multiple_of(i * SEG, SEG)
+        block = dp * blocks + i
+        biases = [block_bias(seg_ref, par_ref, block, back - j) for j in range(back + 1)]
+        q = q_ref[pl.ds(at, SEG), :]
+        for h in range(3):
+            qm = jnp.where(head_mask(h, SEG, cols), q, jnp.zeros_like(q))
+            top = None
+            for j in range(back + 1):
+                s = nt(k_ref[pl.ds(at + j * SEG, SEG), :], qm)
+                if j == 0:
+                    s = s + tri_ref[1]
+                if j == back:
+                    s = s + tri_ref[0]
+                s_ref[h, j * SEG : (j + 1) * SEG, :] = s
+                best = jnp.max(s, axis=0, keepdims=True) + biases[j]
+                top = best if top is None else jnp.maximum(top, best)
+            top = top * LOG2E
+            total = None
+            for j in range(back + 1):
+                e = jnp.exp2(s_ref[h, j * SEG : (j + 1) * SEG, :] * LOG2E - (top - biases[j]))
+                part = jnp.sum(e, axis=0, keepdims=True)
+                total = part if total is None else total + part
+                e_ref[h, j * SEG : (j + 1) * SEG, :] = e.astype(BF)
+            o = nn(vt_ref[h * HD : (h + 1) * HD, pl.ds(at, (back + 1) * SEG)], e_ref[h])
+            ct_ref[pl.ds(t * wide + h * HD, HD), pl.ds(at, SEG)] = (o / total).astype(BF)
+            l_ref[h : h + 1, pl.ds(at, SEG)] = top + jnp.log(total) * LOG2E
+        c_spread(i).start()
+
+        @pl.when(i > 0)
+        def _():
+            c_spread(i - 1).forward()
+
+        @pl.when(i == 1)
+        def _():
+            for step in (1, 3, 2):
+                f_gather.forward(step)
+
+        return 0
+
+    lax.fori_loop(0, blocks, attend, 0)
+    c_spread(blocks - 1).forward()
+    wout_spread.forward()
+    wout_spread.wait()
+
+    def middle(i, _):
+        at = pl.multiple_of(i * SEG, SEG)
+        c_spread(i).wait()
+        m = xe_ref[pl.ds(WINDOW + at, SEG), :].astype(F32) + tn(ct_ref[:, pl.ds(at, SEG)], wout_ref[...])
+        mids_ref[pl.ds(at, SEG), :] = m
+        r = lax.rsqrt(jnp.mean(m * m, axis=-1, keepdims=True) + EPS)
+        n2_ref[pl.ds(at, SEG), :] = (m * r * gain_ref[1:2, :]).astype(BF)
+        return 0
+
+    lax.fori_loop(0, blocks, middle, 0)
+    mid_ref[...] = mids_ref[pl.ds(t * rows, rows), :]
+    cot_spread.forward()
+    cot_spread.wait()
+    f_gather.wait()
+    for item in (x_spread, cot_spread, wout_spread, a_gather, f_gather):
+        item.finish()
+    for i in range(blocks):
+        c_spread(i).finish()
+
+    @pl.when(place >= 1)
+    def _():
+        halo_spread.finish()
+
+    @pl.when(place < per_tree - 1)
+    def _():
+        halo_copy().wait_send()
+
+    @pl.when(place < per_tree - 2)
+    def _():
+        far_copy().wait_send()
+
+
+def first_phase(x, cot, segments, parents, wa, wf):
+    rows, width = x.shape
+    token = 4 * rows
+    ext = token + WINDOW
+    wide = width // 4
+    cols = 256 * pl.cdiv(wide, 256)
+    blocks = token // SEG
+    keys = WINDOW + SEG
+    vmem = pl.BlockSpec(memory_space=pltpu.VMEM)
+    smem = pl.BlockSpec(memory_space=pltpu.SMEM)
+    copies = 3 * 4 + 2 * 8 + 2 + 3 * blocks
+    shape = jax.ShapeDtypeStruct
+    return pl.pallas_call(
+        first_kernel,
+        out_shape=[
+            shape((token, width), BF),
+            shape((token, width), BF),
+            shape((rows, width), F32),
+            shape((8,) + wf.shape, BF),
+            shape((token, width), BF),
+            shape((width, width), BF),
+            shape((token, cols), BF),
+            shape((ext, cols), BF),
+            shape((ext, cols), BF),
+            shape((width, token), BF),
+            shape((8, token), F32),
+            shape((8, width), F32),
+            shape((width, cols), BF),
+            shape((width, cols), BF),
+            shape((width, cols), BF),
+        ],
+        in_specs=[smem, smem, vmem, vmem, vmem, vmem],
+        out_specs=[vmem] * 15,
+        scratch_shapes=[
+            pltpu.VMEM((8,) + wa.shape, BF),
+            pltpu.VMEM((ext, width), BF),
+            pltpu.VMEM((cols, ext), BF),
+            pltpu.VMEM((3, keys, SEG), F32),
+            pltpu.VMEM((3, keys, SEG), BF),
+            pltpu.VMEM((2, SEG, SEG), F32),
+            pltpu.VMEM((token, width), F32),
+            pltpu.SemaphoreType.DMA((copies,)),
+            pltpu.SemaphoreType.DMA((copies,)),
+        ],
+        compiler_params=pltpu.CompilerParams(
+            collective_id=0, has_side_effects=True, vmem_limit_bytes=60 << 20
+        ),
+    )(segments, parents, x, cot, wa, wf)
+
+
+class Fold:
+    def __init__(self, links, base, dp, t, buf):
+        self.links, self.base, self.dp, self.t, self.buf = links, base, dp, t, buf
+
+    def copy(self, i):
+        flip = (1, 2, 1)[i]
+        return self.links.copy(
+            self.buf.at[i], self.buf.at[3 + i], self.base + i, self.base + i, (self.dp, self.t ^ flip)
+        )
+
+    def put(self, i, value):
+        if i == 1:
+            self.copy(0).wait_recv()
+            value = value + self.buf[3].astype(F32)
+        self.buf[i] = value.astype(BF)
+
+    def total(self, value):
+        self.copy(1).wait_recv()
+        self.copy(2).wait_recv()
+        return value + self.buf[5].astype(F32) + self.buf[4].astype(F32)
+
+    def finish(self):
+        for i in range(3):
+            self.copy(i).wait_send()
+
+
+class Settle:
+    def __init__(self, links, base, dp, t, slots, deep, from_y, from_z):
+        self.links, self.base, self.dp, self.t = links, base, dp, t
+        self.slots, self.deep, self.from_y, self.from_z = slots, deep, from_y, from_z
+        self.z, self.y = dp // 2, lax.rem(dp, 2)
+
+    def rows(self, z, y):
+        return pl.ds(pl.multiple_of((z * 2 + y) * self.deep, self.deep), self.deep)
+
+    def across(self, step):
+        z = lax.rem(self.z + step, 4)
+        return self.links.copy(
+            self.slots.at[self.rows(z, 1 - self.y)],
+            self.from_y.at[step],
+            self.base + step,
+            self.base + step,
+            (self.dp ^ 1, self.t),
+        )
+
+    def along(self, step):
+        z = lax.rem(self.z + step, 4)
+        return self.links.copy(
+            self.slots.at[self.rows(z, self.y)],
+            self.from_z.at[step - 1],
+            self.base + 3 + step,
+            self.base + 3 + step,
+            (z * 2 + self.y, self.t),
+        )
+
+    def start(self):
+        for step in (2, 1, 3, 0):
+            self.across(step).start()
+
+    def pass_on(self, step):
+        self.across(step).wait_recv()
+        z = lax.rem(self.z + step, 4)
+        at = self.rows(z, self.y)
+        self.slots[at, :] = (self.slots[at, :].astype(F32) + self.from_y[step].astype(F32)).astype(BF)
+        self.along(step).start()
+
+    def total(self):
+        self.across(0).wait_recv()
+        value = self.slots[self.rows(self.z, self.y), :].astype(F32) + self.from_y[0].astype(F32)
+        for step in (1, 2, 3):
+            self.along(step).wait_recv()
+            value = value + self.from_z[step - 1].astype(F32)
+        return value
+
+    def finish(self):
+        for step in range(4):
+            self.across(step).wait_send()
+        for step in (1, 2, 3):
+            self.along(step).wait_send()
+
+
+def second_kernel(
+    seg_ref, par_ref, x_ref, cot_ref, wa_ref, wf_ref,
+    n1_ref, n2_ref, mid_ref, f_ref, cot_all, wout_ref, q_ref, k_ref, v_ref, ct_ref, l_ref, gain_ref, wq_ref, wk_ref, wv_ref,
+    out_ref, ing_ref, gqkv_ref, gout_ref, gup_ref, gdown_ref, gs_ref,
+    a_ref, gu_ref, down_own, gn_own, down_buf, gn_buf, gn1_buf, gmb_ref, gmid_ref,
+    gf_ref, gfy_ref, gfz_ref, ga_ref, gay_ref, gaz_ref, wo_ref, kt_ref, dqt_ref, halo_ref, back_ref, own_ref, acc_ref,
+    gq_ref, gk_ref, gv_ref, tri_ref, delta_ref, gain_buf, send, recv,
+):
+    dp, t = lax.axis_index("dp"), lax.axis_index("tensor")
+    rows, width = x_ref.shape
+    token = 4 * rows
+    blocks = token // SEG
+    back = WINDOW // SEG
+    lag = WINDOW - token
+    per_tree = TREE // token
+    place = lax.rem(dp, per_tree)
+    wide = width // 4
+    cols = q_ref.shape[1]
+    deep = wf_ref.shape[0]
+    hidden = wf_ref.shape[1] // 2
+    links = Links(send, recv)
+    down_fold = Fold(links, links.take(3), dp, t, down_buf)
+    gn_fold = Fold(links, links.take(3), dp, t, gn_buf)
+    gn1_fold = Fold(links, links.take(3), dp, t, gn1_buf)
+    gmb_spread = Spread(links, links.take(3), dp, t, lambda p: gmb_ref.at[pl.ds(p * rows, rows)])
+    f_settle = Settle(links, links.take(7), dp, t, gf_ref, deep, gfy_ref, gfz_ref)
+    a_settle = Settle(links, links.take(7), dp, t, ga_ref, deep, gay_ref, gaz_ref)
+    hb = links.take(5)
+
+    def back_copy(i):
+        at = pl.ds(lag + (t ^ (3 - i)) * rows, rows)
+        return links.copy(halo_ref.at[at], back_ref.at[at], hb + i, hb + i, (lax.rem(dp + 7, 8), t))
+
+    def far_copy():
+        at = pl.ds(0, lag)
+        return links.copy(halo_ref.at[at], back_ref.at[at], hb + 4, hb + 4, (lax.rem(dp + 6, 8), t))
+
+    gb = links.take(3)
+
+    def gain_copy(i):
+        return links.copy(gain_buf.at[0], gain_buf.at[i + 1], gb + i, gb + i, (dp, t ^ (i + 1)))
+
+    greet(dp, t)
+    up = f_ref[:, :, 0:hidden].reshape(width, hidden)
+    down_t = f_ref[:, :, hidden : 2 * hidden].reshape(width, hidden)
+
+    def feed(k, _):
+        at = (t ^ (3 - k)) * rows
+        u = nn(n2_ref[pl.ds(at, rows), :], up)
+        cdf = 0.5 * (1.0 + lax.erf(u * 0.7071067811865476))
+        act = (u * cdf).astype(BF)
+        a_ref[pl.ds(at, rows), :] = act
+        slope = cdf + u * jnp.exp2(u * u * (-0.5 * LOG2E)) * 0.3989422804014327
+        gu = (nn(cot_all[pl.ds(at, rows), :], down_t) * slope).astype(BF)
+        gu_ref[pl.ds(at, rows), :] = gu
+        gn_own[...] = nt(gu, up)
+        down_own[...] = nt(act, down_t)
+        for i in range(3):
+
+            @pl.when(k == i)
+            def _():
+                gn_fold.put(i, gn_own[...])
+                gn_fold.copy(i).start()
+                down_fold.put(i, down_own[...])
+                if i != 1:
+                    down_fold.copy(i).start()
+
+        return 0
+
+    lax.fori_loop(0, 4, feed, 0)
+
+    def ffn_grads(j, _):
+        at = pl.multiple_of(j * 256, 256)
+        gf_ref[pl.ds(at, 256), 0:hidden] = tn(n2_ref[:, pl.ds(at, 256)], gu_ref[...]).astype(BF)
+        gf_ref[pl.ds(at, 256), hidden : 2 * hidden] = tn(cot_all[:, pl.ds(at, 256)], a_ref[...]).astype(BF)
+        return 0
+
+    lax.fori_loop(0, width // 256, ffn_grads, 0)
+    f_settle.start()
+
+    gn2 = gn_fold.total(gn_own[...])
+    mid = mid_ref[...]
+    r2 = lax.rsqrt(jnp.mean(mid * mid, axis=-1, keepdims=True) + EPS)
+    hat2 = mid * r2
+    scaled = gn2 * gain_ref[1:2, :]
+    inner = jnp.mean(scaled * hat2, axis=-1, keepdims=True)
+    gmid = cot_ref[...].astype(F32) + r2 * (scaled - hat2 * inner)
+    gmid_ref[...] = gmid
+    gmb_ref[pl.ds(t * rows, rows), :] = gmid.astype(BF)
+    gmb_spread.start()
+
+    row = lax.broadcasted_iota(jnp.int32, (SEG, SEG), 0)
+    col = lax.broadcasted_iota(jnp.int32, (SEG, SEG), 1)
+    tri_ref[0] = jnp.where(row <= col, 0.0, NEG)
+    tri_ref[1] = jnp.where(row > col, 0.0, NEG)
+    tri_ref[2] = jnp.zeros((SEG, SEG), F32)
+    wo_ref[0:wide, :] = wout_ref[pl.ds(t * wide, wide), :]
+    wo_ref[wide:cols, :] = jnp.zeros((cols - wide, width), BF)
+
+    def turn_keys(i, _):
+        at = pl.multiple_of(i * SEG, SEG)
+        kt_ref[:, pl.ds(at, SEG)] = k_ref[pl.ds(at, SEG), :].T
+        return 0
+
+    lax.fori_loop(0, blocks + back, turn_keys, 0)
+    dqt_ref[...] = jnp.zeros_like(dqt_ref)
+
+    def mask_queries(i, _):
+        at = pl.multiple_of(i * SEG, SEG)
+        q = q_ref[pl.ds(at, SEG), :]
+        for h in range(3):
+            a_ref[pl.ds(at, SEG), h * cols : (h + 1) * cols] = jnp.where(head_mask(h, SEG, cols), q, jnp.zeros_like(q))
+        return 0
+
+    lax.fori_loop(0, blocks, mask_queries, 0)
+    gmb_spread.forward()
+    for step in (2, 1, 3):
+        f_settle.pass_on(step)
+    gmb_spread.wait()
+    down_fold.copy(1).start()
+
+    def context_grads(i, _):
+        at = pl.multiple_of(i * SEG, SEG)
+        gc = nt(gmb_ref[pl.ds(at, SEG), :], wo_ref[...])
+        low = gc.astype(BF)
+        gct = low.astype(F32).T
+        for h in range(3):
+            gu_ref[pl.ds(at, SEG), h * cols : (h + 1) * cols] = jnp.where(
+                head_mask(h, SEG, cols), low, jnp.zeros_like(low)
+            )
+            c = ct_ref[pl.ds(t * wide + h * HD, HD), pl.ds(at, SEG)].astype(F32)
+            delta_ref[h : h + 1, pl.ds(at, SEG)] = jnp.sum(gct[h * HD : (h + 1) * HD] * c, axis=0, keepdims=True)
+        return 0
+
+    lax.fori_loop(0, blocks, context_grads, 0)
+    qm_ref, gm_ref = a_ref, gu_ref
+
+    def key_block(kb, _):
+        kat = pl.multiple_of(kb * SEG, SEG)
+        acc_ref[...] = jnp.zeros_like(acc_ref)
+
+        def pair(qb, _):
+            qat = pl.multiple_of(qb * SEG, SEG)
+            bias = block_bias(seg_ref, par_ref, dp * blocks + qb, back + qb - kb)
+            tri = tri_ref[jnp.where(kb == qb, 1, jnp.where(kb == qb + back, 0, 2))]
+            keys = k_ref[pl.ds(kat, SEG), :]
+            values = v_ref[pl.ds(kat, SEG), :]
+            dk = dv = None
+            for h in range(3):
+                qm = qm_ref[pl.ds(qat, SEG), h * cols : (h + 1) * cols]
+                gm = gm_ref[pl.ds(qat, SEG), h * cols : (h + 1) * cols]
+                p = jnp.exp2(nt(keys, qm) * LOG2E + tri - (l_ref[h : h + 1, pl.ds(qat, SEG)] - bias))
+                ds = (p * (nt(values, gm) - delta_ref[h : h + 1, pl.ds(qat, SEG)])).astype(BF)
+                dv_h = nn(p.astype(BF), gm)
+                dk_h = nn(ds, qm)
+                dv = dv_h if dv is None else dv + dv_h
+                dk = dk_h if dk is None else dk + dk_h
+                dqt_ref[h * HD : (h + 1) * HD, pl.ds(qat, SEG)] += nn(
+                    kt_ref[h * HD : (h + 1) * HD, pl.ds(kat, SEG)], ds
+                )
+            acc_ref[0] += dk
+            acc_ref[1] += dv
+            return 0
+
+        lax.fori_loop(jnp.maximum(kb - back, 0), jnp.minimum(kb + 1, blocks), pair, 0)
+        both = jnp.concatenate([acc_ref[0, :, 0:wide], acc_ref[1, :, 0:wide]], axis=1)
+
+        @pl.when(kb < back)
+        def _():
+            halo_ref[pl.ds(kat, SEG), :] = both.astype(BF)
+
+        @pl.when(kb >= back)
+        def _():
+            own_ref[pl.ds(kat - WINDOW, SEG), :] = both
+
+        @pl.when((kb == back - 1) & (place >= 1))
+        def _():
+            for i in range(4):
+                back_copy(i).start()
+
+        @pl.when((kb == back - 1) & (place >= 2))
+        def _():
+            far_copy().start()
+
+        return 0
+
+    lax.fori_loop(0, blocks + back, key_block, 0)
+
+    def turn_queries(i, _):
+        at = pl.multiple_of(i * SEG, SEG)
+        gq_ref[pl.ds(at, SEG), :] = (dqt_ref[:, pl.ds(at, SEG)] * HD**-0.5).astype(BF).T
+        return 0
+
+    lax.fori_loop(0, blocks, turn_queries, 0)
+    gout = nn(ct_ref[pl.ds(t * wide, wide), :], gmb_ref[...]).astype(BF).T
+    out_ref[...] = (mid_ref[...] + down_fold.total(down_own[...])).astype(BF)
+
+    @pl.when(place < per_tree - 2)
+    def _():
+        far_copy().wait_recv()
+        at = token - lag
+        own_ref[at:token, :] = own_ref[at:token, :] + back_ref[0:lag, :].astype(F32)
+
+    def outer(k, _):
+        at = (t ^ (3 - k)) * rows
+
+        @pl.when(place < per_tree - 1)
+        def _():
+            for i in range(4):
+
+                @pl.when(k == i)
+                def _():
+                    back_copy(i).wait_recv()
+
+            own_ref[pl.ds(at, rows), :] = own_ref[pl.ds(at, rows), :] + back_ref[pl.ds(lag + at, rows), :].astype(F32)
+
+        both = own_ref[pl.ds(at, rows), :].astype(BF)
+        gk_ref[pl.ds(at, rows), :] = both[:, 0:wide]
+        gv_ref[pl.ds(at, rows), :] = both[:, wide : 2 * wide]
+        gn_own[...] = (
+            nt(gq_ref[pl.ds(at, rows), :], wq_ref[:, 0:wide])
+            + nt(gk_ref[pl.ds(at, rows), :], wk_ref[:, 0:wide])
+            + nt(gv_ref[pl.ds(at, rows), :], wv_ref[:, 0:wide])
+        )
+        for i in range(3):
+
+            @pl.when(k == i)
+            def _():
+                gn1_fold.put(i, gn_own[...])
+                gn1_fold.copy(i).start()
+
+        return 0
+
+    lax.fori_loop(0, 4, outer, 0)
+
+    ga_ref[:, 3 * wide : 4 * wide] = gout
+    for j, ref in enumerate((gq_ref, gk_ref, gv_ref)):
+        ga_ref[:, j * wide : (j + 1) * wide] = tn(n1_ref[...], ref[...]).astype(BF)
+    a_settle.start()
+    gf = f_settle.total()
+    gup_ref[...] = gf[:, 0:hidden]
+    gdown_ref[...] = gf[:, hidden : 2 * hidden].T
+    for step in (2, 1, 3):
+        a_settle.pass_on(step)
+
+    gn1 = gn1_fold.total(gn_own[...])
+    x = x_ref[...].astype(F32)
+    r1 = lax.rsqrt(jnp.mean(x * x, axis=-1, keepdims=True) + EPS)
+    hat1 = x * r1
+    scaled = gn1 * gain_ref[0:1, :]
+    inner = jnp.mean(scaled * hat1, axis=-1, keepdims=True)
+    ing_ref[...] = (gmid_ref[...] + r1 * (scaled - hat1 * inner)).astype(BF)
+
+    ga = a_settle.total()
+    gqkv_ref[...] = ga[:, 0 : 3 * wide]
+    gout_ref[...] = ga[:, 3 * wide : 4 * wide].T
+    one = jnp.sum(ga[:, 0 : 3 * wide] * wa_ref[0:deep, 0 : 3 * wide].astype(F32), axis=1, keepdims=True)
+    two = jnp.sum(gup_ref[...] * wf_ref[:, 0:hidden].astype(F32), axis=1, keepdims=True)
+    lane = lax.broadcasted_iota(jnp.int32, (deep, 128), 1)
+    gain_buf[0] = jnp.where(lane < 64, one, two)
+    for i in range(3):
+        gain_copy(i).start()
+    total = gain_buf[0]
+    for i in range(3):
+        gain_copy(i).wait_recv()
+        total = total + gain_buf[i + 1]
+    gs_ref[...] = total
+    for i in range(3):
+        gain_copy(i).wait_send()
+    for item in (down_fold, gn_fold, gn1_fold, gmb_spread, f_settle, a_settle):
+        item.finish()
+
+    @pl.when(place >= 1)
+    def _():
+        for i in range(4):
+            back_copy(i).wait_send()
+
+    @pl.when(place >= 2)
+    def _():
+        far_copy().wait_send()
+
+
+def second_phase(x, cot, segments, parents, wa, wf, firsts):
+    rows, width = x.shape
+    token = 4 * rows
+    ext = token + WINDOW
+    wide = width // 4
+    cols = 256 * pl.cdiv(wide, 256)
+    deep, hidden = wf.shape[0], wf.shape[1] // 2
+    vmem = pl.BlockSpec(memory_space=pltpu.VMEM)
+    smem = pl.BlockSpec(memory_space=pltpu.SMEM)
+    copies = 4 * 3 + 2 * 7 + 5 + 3
+    shape = jax.ShapeDtypeStruct
+    return pl.pallas_call(
+        second_kernel,
+        out_shape=[
+            shape((rows, width), BF),
+            shape((rows, width), BF),
+            shape((deep, 3 * wide), F32),
+            shape((wide, deep), F32),
+            shape((deep, hidden), F32),
+            shape((hidden, deep), F32),
+            shape((deep, 128), F32),
+        ],
+        in_specs=[smem, smem] + [vmem] * 19,
+        out_specs=[vmem] * 7,
+        scratch_shapes=[
+            pltpu.VMEM((token, hidden), BF),
+            pltpu.VMEM((token, hidden), BF),
+            pltpu.VMEM((rows, width), F32),
+            pltpu.VMEM((rows, width), F32),
+            pltpu.VMEM((6, rows, width), BF),
+            pltpu.VMEM((6, rows, width), BF),
+            pltpu.VMEM((6, rows, width), BF),
+            pltpu.VMEM((token, width), BF),
+            pltpu.VMEM((rows, width), F32),
+            pltpu.VMEM((width, 2 * hidden), BF),
+            pltpu.VMEM((4, deep, 2 * hidden), BF),
+            pltpu.VMEM((3, deep, 2 * hidden), BF),
+            pltpu.VMEM((width, width), BF),
+            pltpu.VMEM((4, deep, width), BF),
+            pltpu.VMEM((3, deep, width), BF),
+            pltpu.VMEM((cols, width), BF),
+            pltpu.VMEM((cols, ext), BF),
+            pltpu.VMEM((wide, token), F32),
+            pltpu.VMEM((WINDOW, 2 * wide), BF),
+            pltpu.VMEM((WINDOW, 2 * wide), BF),
+            pltpu.VMEM((token, 2 * wide), F32),
+            pltpu.VMEM((2, SEG, cols), F32),
+            pltpu.VMEM((token, wide), BF),
+            pltpu.VMEM((token, wide), BF),
+            pltpu.VMEM((token, wide), BF),
+            pltpu.VMEM((3, SEG, SEG), F32),
+            pltpu.VMEM((8, token), F32),
+            pltpu.VMEM((4, deep, 128), F32),
+            pltpu.SemaphoreType.DMA((copies,)),
+            pltpu.SemaphoreType.DMA((copies,)),
+        ],
+        compiler_params=pltpu.CompilerParams(
+            collective_id=1, has_side_effects=True, vmem_limit_bytes=63 << 20
+        ),
+    )(segments, parents, x, cot, wa, wf, *firsts)
+
+
+def fast_shards(
+    layer_input, cotangent, segments, parents, norm1_gain, w_query, w_key, w_value, w_out, norm2_gain, w_up, w_down,
+):
+    dp = lax.axis_index("dp")
+    width = layer_input.shape[1]
+    wide = width // 4
+    gains = jnp.zeros((16, width), BF)
+    gains = lax.dynamic_update_slice(gains, norm1_gain[None], (0, dp * norm1_gain.shape[0]))
+    gains = lax.dynamic_update_slice(gains, norm2_gain[None], (1, dp * norm1_gain.shape[0]))
+    wa = jnp.concatenate([jnp.concatenate([w_query, w_key, w_value, w_out.T], axis=1), gains], axis=0)
+    wf = jnp.concatenate([w_up, w_down.T], axis=1)
+    firsts = first_phase(layer_input, cotangent, segments, parents, wa, wf)
+    out, ing, gqkv, gout, gup, gdown, gs = second_phase(layer_input, cotangent, segments, parents, wa, wf, firsts)
+    return (
+        out,
+        ing,
+        gs[:, 0] / norm1_gain.astype(F32),
+        gqkv[:, 0:wide],
+        gqkv[:, wide : 2 * wide],
+        gqkv[:, 2 * wide :],
+        gout,
+        gs[:, 64] / norm2_gain.astype(F32),
+        gup,
+        gdown,
+    )
 
 
 epsilon = 1e-06
@@ -320,8 +1169,9 @@
 
 
 def solution(mesh):
+    fast = mesh.shape["dp"] == 8 and mesh.shape["tensor"] == 4
     return jax.shard_map(
-        shards,
+        fast_shards if fast else shards,
         mesh=mesh,
         in_specs=(
             P(("dp", "tensor"), None),

time: 779 us -> 225 us (0.29)
  waiting for transfers between devices: 259 us -> 0 us
  Pallas kernels: 0 us -> 206 us
  blocking collectives: 170 us -> 0 us
  matrix products: 150 us -> 0 us
  other arithmetic: 107 us -> 3.86 us
  local copies, waits for them, and re-layouts: 43.4 us -> 11.2 us
  starting transfers between devices: 24.4 us -> 0 us
  between operations: 17.2 us -> 0.76 us
    pallas_call x0 -> x2, Pallas kernels: none -> 206 us  [the longest x1 120 us: second_phase(): pl.pallas_call(second_kernel, out_shape=[shape((rows, width), BF), shape(...]
    dot_general x32 -> x0, matrix products: 150 us -> none  [the longest x4 46.3 us: scores_of(): jnp.einsum('qhd,khd->hqk', query_block, key_block, preferred_element_type...]
    all_gather x4 -> x0, blocking collectives: 139 us -> none  [the longest x1 46 us: shards(): lax.all_gather(w_out, 'dp', axis=1, tiled=True)]
    all_gather x6 -> x0, waiting for transfers between devices: 113 us -> none  [the longest x1 38.4 us: shards(): lax.all_gather(w_down, 'dp', axis=1, tiled=True)]
    reduce_scatter x4 -> x0, waiting for transfers between devices: 63.5 us -> none  [the longest x1 32.8 us: shards(): lax.psum_scatter(jnp.dot(context, full_out, preferred_element_type=jnp.fl...]
    all_to_all x4 -> x0, waiting for transfers between devices: 51.2 us -> none  [sum_at_owner(): lax.all_to_all(tiles, axis, split_axis=0, concat_axis=0, tiled=True)]
    convert_element_type x9 -> x0, other arithmetic: 36 us -> none  [the longest x2 22.8 us: backward_block(): grad_scores = (probs * (grad_probs - inner)).astype(jnp.bfloat16)]
    reduce_sum x12 -> x0, other arithmetic: 31.6 us -> none  [the longest x2 21 us: forward_block(): denominator = jnp.sum(exponent, axis=-1, keepdims=True)]
  transfers between devices with their start and end apart: 18 -> 0, of which waited for: 12 -> 0; matrix products, arithmetic and copies ran while one was open for 8% -> 0% of each run, Pallas kernels for 0% -> 0%
where the time goes in v2:
time: 225 us; the launch traced here: 222 us
  Pallas kernels  206 us (92%)
  local copies, waits for them, and re-layouts  11.2 us (5%)
  other arithmetic  3.86 us (2%)
    pallas_call x1, Pallas kernels, second_phase(): pl.pallas_call(second_kernel, out_shape=[shape((rows, width), BF), shape(...  120 us
    pallas_call x1, Pallas kernels, first_phase(): pl.pallas_call(first_kernel, out_shape=[shape((token, width), BF), shape(...  86.3 us
    unnamed x16, local copies, waits for them, and re-layouts  6.75 us

profile of v2, /device:TPU:0, one launch (start us, length us, event | category | flops | bytes accessed | tf_op | source)
XLA Modules:
  0.0 222.2 jit_solution(15917489525861220873)
XLA Ops:
  0.7 0.8 dynamic_update_slice.6
  1.5 0.8 dynamic_update_slice.7
  2.3 0.9 copy.24
  3.2 1.6 pad_maximum_fusion.1.wa_ref
  4.8 1.7 pad_maximum_fusion.wf_ref
  6.5 86.3 %shard_map.195 = (bf16[1280,768]{1,0:T(8,128)(2,1)}, bf16[1280,768]{1,0:T(8,128)(2,1)}, f32[320,768]{1,0:T(8,128)}, bf16[8,96,1536]{2,1,0:T(8,128)(2,1)}, bf16[1...) custom-call(s32[10240]{0:T(1024)} %seg_ref.3, ...), custom_call_target="tpu_custom_call" | custom-call | tf_op jit(solution)/shard_map/pallas_call | solution.py:371
  92.8 0.0 copy-start.3
  92.8 0.0 copy-start.4
  92.9 120.1 %shard_map.196 = (bf16[320,768]{1,0:T(8,128)(2,1)}, bf16[320,768]{1,0:T(8,128)(2,1)}, f32[96,576]{1,0:T(8,128)}, f32[192,96]{1,0:T(8,128)}, f32[96,768]{1,0:T(8,...) custom-call(s32[10240]{0:T(1024)} %seg_ref.3, s32[26]{0:T(128)} %par_ref.3, bf16[320,768]{1,0:T(8,128)(2,1)} %x_ref.3, ...), custom_call_target="tpu_custom_call" | custom-call | tf_op jit(solution)/shard_map/pallas_call | solution.py:783
  212.9 0.0 copy-start
  212.9 0.0 copy-start.2
  212.9 0.0 copy-start.1
  212.9 1.1 slice_reduce_fusion
  214.0 0.0 copy-done.3
  214.0 0.0 copy-done.4
  214.0 0.5 convert_divide_fusion
  214.6 1.9 copy.25
  216.4 1.8 fusion
  218.2 1.8 copy.32
  220.1 0.0 copy-done
  220.1 0.8 copy.33
  220.8 0.0 copy-done.2
  220.8 0.6 copy.34
  221.5 0.7 copy.35
  (2 shorter events, 0.0 us)
Async XLA Ops:
  92.8 121.2 %copy-start.3 = (bf16[96]{0:T(256)(128)(2,1)S(1)}, bf16[96]{0:T(256)(128)(2,1)}, u32[]{:S(2)}) copy-start(bf16[96]{0:T(256)(128)(2,1)} %param.16) | copy-start | bytes 580
  92.8 121.2 %copy-start.4 = (bf16[96]{0:T(256)(128)(2,1)S(1)}, bf16[96]{0:T(256)(128)(2,1)}, u32[]{:S(2)}) copy-start(bf16[96]{0:T(256)(128)(2,1)} %param.21) | copy-start | bytes 580
  212.9 7.1 %copy-start = (bf16[320,768]{1,0:T(8,128)(2,1)S(1)}, bf16[320,768]{1,0:T(8,128)(2,1)}, u32[]{:S(2)}) copy-start(bf16[320,768]{1,0:T(8,128)(2,1)} %get-tuple-element.92) | copy-start | bytes 1474564
  212.9 7.9 %copy-start.2 = (f32[192,96]{1,0:T(8,128)S(1)}, f32[192,96]{1,0:T(8,128)}, u32[]{:S(2)}) copy-start(f32[192,96]{1,0:T(8,128)} %get-tuple-element.97) | copy-start | bytes 221188
  212.9 8.6 %copy-start.1 = (f32[96,768]{1,0:T(8,128)S(1)}, f32[96,768]{1,0:T(8,128)}, u32[]{:S(2)}) copy-start(f32[96,768]{1,0:T(8,128)} %get-tuple-element.99) | copy-start | bytes 884740

commit v3 on v0

--- a/solution.py
+++ b/solution.py
@@ -1,12 +1,817 @@
+import functools
 import math
 
 import jax
 import jax.numpy as jnp
 from jax import lax
+from jax.experimental import pallas as pl
+from jax.experimental.pallas import tpu as pltpu
 from jax.sharding import PartitionSpec as P
 
+MESH = pl.DeviceIdType.MESH
+BF = jnp.bfloat16
+F32 = jnp.float32
 HD = 64
 WINDOW = 1536
+SEG = 256
+TREE = 5120
+LOG2E = 1.4426950408889634
+NEG = -1e30
+EPS = 1e-6
+
+
+def nt(a, b):
+    return lax.dot_general(a, b, (((1,), (1,)), ((), ())), preferred_element_type=F32)
+
+
+def nn(a, b):
+    return jnp.dot(a, b, preferred_element_type=F32)
+
+
+def tn(a, b):
+    return lax.dot_general(a, b, (((0,), (0,)), ((), ())), preferred_element_type=F32)
+
+
+class Links:
+    def __init__(self, send, recv):
+        self.send, self.recv, self.used = send, recv, 0
+
+    def take(self, count):
+        base = self.used
+        self.used += count
+        return base
+
+    def copy(self, src, dst, send, recv, device):
+        return pltpu.make_async_remote_copy(
+            src_ref=src,
+            dst_ref=dst,
+            send_sem=self.send.at[send],
+            recv_sem=self.recv.at[recv],
+            device_id=device,
+            device_id_type=MESH,
+        )
+
+
+class Spread:
+    def __init__(self, links, base, dp, t, part):
+        self.links, self.base, self.dp, self.t, self.part = links, base, dp, t, part
+
+    def leave(self, i):
+        flip, what = ((1, 0), (2, 0), (1, 2))[i]
+        ref = self.part(self.t ^ what)
+        return self.links.copy(ref, ref, self.base + i, self.base + i, (self.dp, self.t ^ flip))
+
+    def come(self, i):
+        flip, what = ((1, 1), (2, 2), (1, 3))[i]
+        ref = self.part(self.t ^ what)
+        return self.links.copy(ref, ref, self.base + i, self.base + i, (self.dp, self.t ^ flip))
+
+    def start(self):
+        self.leave(1).start()
+        self.leave(0).start()
+
+    def forward(self):
+        self.come(1).wait_recv()
+        self.leave(2).start()
+
+    def wait(self):
+        self.come(0).wait_recv()
+        self.come(2).wait_recv()
+
+    def finish(self):
+        for i in range(3):
+            self.leave(i).wait_send()
+
+
+class Gather:
+    def __init__(self, links, base, dp, t, slot):
+        self.links, self.base, self.dp, self.t, self.slot = links, base, dp, t, slot
+        self.z, self.y = dp // 2, dp % 2
+
+    def at(self, step):
+        z = lax.rem(self.z + step, 4)
+        return z, z * 2 + self.y
+
+    def along(self, step):
+        z, peer = self.at(step)
+        return self.links.copy(self.slot(self.dp), self.slot(self.dp), self.base + step - 1, self.base + self.z, (peer, self.t))
+
+    def came(self, step):
+        z, peer = self.at(step)
+        return self.links.copy(self.slot(peer), self.slot(peer), self.base + step - 1, self.base + z, (peer, self.t))
+
+    def across(self, step):
+        z, peer = self.at(step)
+        return self.links.copy(self.slot(peer), self.slot(peer), self.base + 4 + step, self.base + 4 + z, (self.dp ^ 1, self.t))
+
+    def crossed(self, step):
+        z, peer = self.at(step)
+        other = z * 2 + (1 - self.y)
+        return self.links.copy(self.slot(other), self.slot(other), self.base + 4 + step, self.base + 4 + z, (self.dp ^ 1, self.t))
+
+    def start(self):
+        self.across(0).start()
+        for step in (1, 3, 2):
+            self.along(step).start()
+
+    def forward(self, step):
+        self.came(step).wait_recv()
+        self.across(step).start()
+
+    def wait(self):
+        for step in range(4):
+            self.crossed(step).wait_recv()
+
+    def finish(self):
+        for step in range(1, 4):
+            self.along(step).wait_send()
+        for step in range(4):
+            self.across(step).wait_send()
+
+
+def head_mask(h, rows, width):
+    lane = lax.broadcasted_iota(jnp.int32, (rows, width), 1)
+    return (lane >= h * HD) & (lane < (h + 1) * HD)
+
+
+def block_bias(seg_ref, par_ref, block, back):
+    own = seg_ref[block * SEG]
+    one = par_ref[own]
+    two = par_ref[one]
+    far = block - back
+    near = seg_ref[jnp.maximum(far, 0) * SEG]
+    ok = ((near == own) | (near == one) | (near == two)) & (far >= 0)
+    return jnp.where(ok, jnp.float32(0.0), jnp.float32(NEG))
+
+
+class Fold:
+    def __init__(self, links, base, dp, t, buf):
+        self.links, self.base, self.dp, self.t, self.buf = links, base, dp, t, buf
+
+    def copy(self, i):
+        flip = (1, 2, 1)[i]
+        return self.links.copy(
+            self.buf.at[i], self.buf.at[3 + i], self.base + i, self.base + i, (self.dp, self.t ^ flip)
+        )
+
+    def put(self, i, value):
+        if i == 1:
+            self.copy(0).wait_recv()
+            value = value + self.buf[3].astype(F32)
+        self.buf[i] = value.astype(BF)
+
+    def total(self, value):
+        self.copy(1).wait_recv()
+        self.copy(2).wait_recv()
+        return value + self.buf[5].astype(F32) + self.buf[4].astype(F32)
+
+    def finish(self):
+        for i in range(3):
+            self.copy(i).wait_send()
+
+
+class Settle:
+    def __init__(self, links, base, dp, t, slots, deep, from_y, from_z):
+        self.links, self.base, self.dp, self.t = links, base, dp, t
+        self.slots, self.deep, self.from_y, self.from_z = slots, deep, from_y, from_z
+        self.z, self.y = dp // 2, lax.rem(dp, 2)
+
+    def rows(self, z, y):
+        return pl.ds(pl.multiple_of((z * 2 + y) * self.deep, self.deep), self.deep)
+
+    def across(self, step):
+        z = lax.rem(self.z + step, 4)
+        return self.links.copy(
+            self.slots.at[self.rows(z, 1 - self.y)],
+            self.from_y.at[step],
+            self.base + step,
+            self.base + step,
+            (self.dp ^ 1, self.t),
+        )
+
+    def along(self, step):
+        z = lax.rem(self.z + step, 4)
+        return self.links.copy(
+            self.slots.at[self.rows(z, self.y)],
+            self.from_z.at[step - 1],
+            self.base + 3 + step,
+            self.base + 3 + step,
+            (z * 2 + self.y, self.t),
+        )
+
+    def start(self):
+        for step in (2, 1, 3, 0):
+            self.across(step).start()
+
+    def pass_on(self, step):
+        self.across(step).wait_recv()
+        z = lax.rem(self.z + step, 4)
+        at = self.rows(z, self.y)
+        self.slots[at, :] = (self.slots[at, :].astype(F32) + self.from_y[step].astype(F32)).astype(BF)
+        self.along(step).start()
+
+    def total(self):
+        self.across(0).wait_recv()
+        value = self.slots[self.rows(self.z, self.y), :].astype(F32) + self.from_y[0].astype(F32)
+        for step in (1, 2, 3):
+            self.along(step).wait_recv()
+            value = value + self.from_z[step - 1].astype(F32)
+        return value
+
+    def finish(self):
+        for step in range(4):
+            self.across(step).wait_send()
+        for step in (1, 2, 3):
+            self.along(step).wait_send()
+
+
+def kernel(
+    seg_ref, par_ref, x_ref, cot_ref, g1_ref, wq_in, wk_in, wv_in, wo_in, g2_ref, wu_in, wd_in,
+    out_ref, ing_ref, gg1_ref, gq_out, gk_out, gv_out, gout_ref, gg2_ref, gup_ref, gdown_ref,
+    xe_ref, n1_ref, n2_ref, mid_ref, gmid_ref, w_ref, f_ref, cot_all, wout_ref, wo_ref, wq_ref, wk_ref, wv_ref,
+    q_ref, k_ref, v_ref, turn_ref, ct_ref, l_ref, gain_ref, delta_ref, pool_ref, e_ref, tri_ref,
+    a_ref, gu_ref, down_own, gn_own, down_buf, gn_buf, gmb_ref,
+    gfy_ref, gfz_ref, gay_ref, gaz_ref, dqt_ref, halo_ref, back_ref, gain_buf, send, recv,
+):
+    dp, t = lax.axis_index("dp"), lax.axis_index("tensor")
+    rows, width = x_ref.shape
+    token = 4 * rows
+    ext = token + WINDOW
+    blocks = token // SEG
+    back = WINDOW // SEG
+    lag = WINDOW - token
+    per_tree = TREE // token
+    place = lax.rem(dp, per_tree)
+    wide = width // 4
+    cols = q_ref.shape[1]
+    deep = wu_in.shape[0]
+    hidden = wu_in.shape[1]
+    links = Links(send, recv)
+    spread = lambda part: Spread(links, links.take(3), dp, t, part)
+    x_spread = spread(lambda p: xe_ref.at[pl.ds(WINDOW + p * rows, rows)])
+    halo = lambda p: xe_ref.at[pl.ds(lag + p * rows, rows)]
+    halo_spread = spread(halo)
+    cot_spread = spread(lambda p: cot_all.at[pl.ds(p * rows, rows)])
+    wout_spread = spread(lambda p: wout_ref.at[pl.ds(p * wide, wide)])
+    gmb_spread = spread(lambda p: gmb_ref.at[pl.ds(p * rows, rows)])
+    slot = deep + 16
+    a_gather = Gather(links, links.take(8), dp, t, lambda s: w_ref.at[pl.ds(pl.multiple_of(s * slot, 16), slot)])
+    f_slot = lambda s: pl.ds(pl.multiple_of(s * deep, deep), deep)
+    u_gather = Gather(links, links.take(8), dp, t, lambda s: f_ref.at[f_slot(s), pl.ds(0, hidden)])
+    d_gather = Gather(links, links.take(8), dp, t, lambda s: f_ref.at[f_slot(s), pl.ds(hidden, hidden)])
+    h1 = links.take(1)
+    h2 = links.take(1)
+    halo_copy = lambda: links.copy(x_ref, halo(t), h1, h1, (lax.rem(dp + 1, 8), t))
+    far_copy = lambda: links.copy(
+        xe_ref.at[pl.ds(WINDOW + token - lag, lag)], xe_ref.at[pl.ds(0, lag)], h2, h2, (lax.rem(dp + 2, 8), t)
+    )
+    c_base = links.take(3 * blocks)
+
+    def c_spread(i):
+        at = pl.multiple_of(i * SEG, SEG)
+        return Spread(links, c_base + 3 * i, dp, t, lambda p: ct_ref.at[pl.ds(p * wide, wide), pl.ds(at, SEG)])
+
+    down_fold = Fold(links, links.take(3), dp, t, down_buf)
+    gn_fold = Fold(links, links.take(3), dp, t, gn_buf)
+    gn1_fold = Fold(links, links.take(3), dp, t, gn_buf)
+    f_settle = Settle(links, links.take(7), dp, t, f_ref, deep, gfy_ref, gfz_ref)
+    a_settle = Settle(links, links.take(7), dp, t, w_ref, deep, gay_ref, gaz_ref)
+    hb = links.take(5)
+
+    def back_copy(i):
+        at = pl.ds(lag + (t ^ (3 - i)) * rows, rows)
+        return links.copy(halo_ref.at[at], back_ref.at[at], hb + i, hb + i, (lax.rem(dp + 7, 8), t))
+
+    def far_back():
+        at = pl.ds(0, lag)
+        return links.copy(halo_ref.at[at], back_ref.at[at], hb + 4, hb + 4, (lax.rem(dp + 6, 8), t))
+
+    gb = links.take(3)
+
+    def gain_copy(i):
+        return links.copy(gain_buf.at[0], gain_buf.at[i + 1], gb + i, gb + i, (dp, t ^ (i + 1)))
+
+    barrier = pltpu.get_barrier_semaphore()
+    for step in range(1, 8):
+        pl.semaphore_signal(barrier, inc=1, device_id=(lax.rem(dp + step, 8), t), device_id_type=MESH)
+    for flip in (1, 2, 3):
+        pl.semaphore_signal(barrier, inc=1, device_id=(dp, t ^ flip), device_id_type=MESH)
+
+    base = pl.multiple_of(dp * slot, 16)
+    w_ref[pl.ds(base, deep), :] = jnp.concatenate(
+        [wq_in[...], wk_in[...], wv_in[...], wo_in[...].astype(F32).T.astype(BF)], axis=1
+    )
+    lane = lax.broadcasted_iota(jnp.int32, (deep, width), 1)
+    line = lax.broadcasted_iota(jnp.int32, (deep, width), 0)
+    put = jnp.where(lane == line + dp * deep, 1.0, 0.0).astype(BF)
+    two = jnp.concatenate([g1_ref[...], g2_ref[...], jnp.zeros((14, deep), BF)], axis=0)
+    w_ref[pl.ds(base + deep, 16), :] = nn(two, put).astype(BF)
+    xe_ref[pl.ds(WINDOW + t * rows, rows), :] = x_ref[...]
+    pl.semaphore_wait(barrier, 10)
+    x_spread.start()
+
+    @pl.when(place < per_tree - 1)
+    def _():
+        halo_copy().start()
+
+    a_gather.start()
+    f_ref[f_slot(dp), 0:hidden] = wu_in[...]
+    f_ref[f_slot(dp), hidden : 2 * hidden] = wd_in[...].astype(F32).T.astype(BF)
+    cot_all[pl.ds(t * rows, rows), :] = cot_ref[...]
+
+    @pl.when(place < 1)
+    def _():
+        xe_ref[pl.ds(lag, token), :] = jnp.zeros((token, width), BF)
+
+    @pl.when(place < 2)
+    def _():
+        xe_ref[pl.ds(0, lag), :] = jnp.zeros((lag, width), BF)
+
+    row = lax.broadcasted_iota(jnp.int32, (SEG, SEG), 0)
+    col = lax.broadcasted_iota(jnp.int32, (SEG, SEG), 1)
+    tri_ref[0] = jnp.where(row <= col, 0.0, NEG)
+    tri_ref[1] = jnp.where(row > col, 0.0, NEG)
+    a_gather.forward(1)
+    x_spread.forward()
+    a_gather.forward(3)
+    a_gather.forward(2)
+
+    @pl.when(place >= 1)
+    def _():
+        halo_copy().wait_recv()
+        halo_spread.start()
+
+    x_spread.wait()
+
+    @pl.when(place < per_tree - 2)
+    def _():
+        far_copy().start()
+
+    u_gather.start()
+    a_gather.wait()
+    weights = w_ref[...].reshape(8, slot, width)[:, 0:deep].reshape(width, width)
+    for j, ref in enumerate((wq_ref, wk_ref, wv_ref)):
+        ref[...] = jnp.concatenate(
+            [weights[:, j * wide : (j + 1) * wide], jnp.zeros((width, cols - wide), BF)], axis=1
+        )
+    wo_ref[0:wide, :] = weights[:, 3 * wide : 4 * wide].T
+    wo_ref[wide:cols, :] = jnp.zeros((cols - wide, width), BF)
+    wout_ref[pl.ds(t * wide, wide), :] = wo_ref[0:wide, :]
+    gain_ref[...] = jnp.sum(w_ref[...].reshape(8, slot, width)[:, deep:slot].astype(F32), axis=0)[0:8]
+
+    def norm_rows(at):
+        x = xe_ref[pl.ds(at, SEG), :].astype(F32)
+        r = lax.rsqrt(jnp.mean(x * x, axis=-1, keepdims=True) + EPS)
+        n = (x * r * gain_ref[0:1, :]).astype(BF)
+        k_ref[pl.ds(at, SEG), :] = nn(n, wk_ref[...]).astype(BF)
+        v = nn(n, wv_ref[...]).astype(BF)
+        v_ref[pl.ds(at, SEG), :] = v
+        turn_ref[:, pl.ds(at, SEG)] = v.T
+        return n
+
+    def own_rows(i, _):
+        at = pl.multiple_of(i * SEG, SEG)
+        n = norm_rows(WINDOW + at)
+        n1_ref[pl.ds(at, SEG), :] = n
+        q_ref[pl.ds(at, SEG), :] = (nn(n, wq_ref[...]).astype(BF).astype(F32) * HD**-0.5).astype(BF)
+        return 0
+
+    lax.fori_loop(0, blocks, own_rows, 0)
+
+    @pl.when(place >= 1)
+    def _():
+        halo_spread.forward()
+        halo_spread.wait()
+
+    wout_spread.start()
+    cot_spread.start()
+
+    @pl.when(place >= 2)
+    def _():
+        far_copy().wait_recv()
+
+    def halo_rows(i, _):
+        norm_rows(pl.multiple_of(i * SEG, SEG))
+        return 0
+
+    lax.fori_loop(0, back, halo_rows, 0)
+    span = (back + 1) * SEG
+
+    def scores(i, h):
+        at = pl.multiple_of(i * SEG, SEG)
+        q = q_ref[pl.ds(at, SEG), :]
+        qm = jnp.where(head_mask(h, SEG, cols), q, jnp.zeros_like(q))
+        pool_ref[h * span : (h + 1) * span, :] = nt(k_ref[pl.ds(at, span), :], qm)
+
+    scores(0, 0)
+
+    def attend(i, _):
+        at = pl.multiple_of(i * SEG, SEG)
+        biases = [block_bias(seg_ref, par_ref, dp * blocks + i, back - j) for j in range(back + 1)]
+        for h in range(3):
+            if h < 2:
+                scores(i, h + 1)
+            else:
+                scores(jnp.minimum(i + 1, blocks - 1), 0)
+            top = None
+            for j in range(back + 1):
+                here = pl.ds(h * span + j * SEG, SEG)
+                s = pool_ref[here, :]
+                if j == 0 or j == back:
+                    s = s + tri_ref[1 if j == 0 else 0]
+                    pool_ref[here, :] = s
+                best = jnp.max(s, axis=0, keepdims=True) + biases[j]
+                top = best if top is None else jnp.maximum(top, best)
+            top = top * LOG2E
+            total = None
+            for j in range(back + 1):
+                e = jnp.exp2(pool_ref[pl.ds(h * span + j * SEG, SEG), :] * LOG2E - (top - biases[j]))
+                part = jnp.sum(e, axis=0, keepdims=True)
+                total = part if total is None else total + part
+                e_ref[h, j * SEG : (j + 1) * SEG, :] = e.astype(BF)
+            o = nn(turn_ref[h * HD : (h + 1) * HD, pl.ds(at, span)], e_ref[h])
+            ct_ref[pl.ds(t * wide + h * HD, HD), pl.ds(at, SEG)] = (o / total).astype(BF)
+            l_ref[h : h + 1, pl.ds(at, SEG)] = top + jnp.log(total) * LOG2E
+        c_spread(i).start()
+
+        @pl.when(i == 0)
+        def _():
+            for step in (1, 3, 2):
+                u_gather.forward(step)
+            d_gather.start()
+
+        @pl.when(i > 0)
+        def _():
+            c_spread(i - 1).forward()
+
+        return 0
+
+    lax.fori_loop(0, blocks, attend, 0)
+    c_spread(blocks - 1).forward()
+    for step in (1, 3, 2):
+        d_gather.forward(step)
+    wout_spread.forward()
+    wout_spread.wait()
+
+    def middle(i, _):
+        at = pl.multiple_of(i * SEG, SEG)
+        c_spread(i).wait()
+        m = xe_ref[pl.ds(WINDOW + at, SEG), :].astype(F32) + tn(ct_ref[:, pl.ds(at, SEG)], wout_ref[...])
+        for j in range(width // 256):
+            pool_ref[pl.ds(j * token + at, SEG), :] = m[:, j * 256 : (j + 1) * 256]
+        r = lax.rsqrt(jnp.mean(m * m, axis=-1, keepdims=True) + EPS)
+        n2_ref[pl.ds(at, SEG), :] = (m * r * gain_ref[1:2, :]).astype(BF)
+        return 0
+
+    lax.fori_loop(0, blocks, middle, 0)
+    for j in range(width // 256):
+        mid_ref[:, j * 256 : (j + 1) * 256] = pool_ref[pl.ds(j * token + t * rows, rows), :]
+    cot_spread.forward()
+    cot_spread.wait()
+    u_gather.wait()
+    d_gather.wait()
+
+    def feed(k, _):
+        at = (t ^ (3 - k)) * rows
+        up = f_ref[:, 0:hidden]
+        down_t = f_ref[:, hidden : 2 * hidden]
+        u = nn(n2_ref[pl.ds(at, rows), :], up)
+        cdf = 0.5 * (1.0 + lax.erf(u * 0.7071067811865476))
+        act = (u * cdf).astype(BF)
+        a_ref[pl.ds(at, rows), :] = act
+        slope = cdf + u * jnp.exp2(u * u * (-0.5 * LOG2E)) * 0.3989422804014327
+        gu = (nn(cot_all[pl.ds(at, rows), :], down_t) * slope).astype(BF)
+        gu_ref[pl.ds(at, rows), :] = gu
+        gn_own[...] = nt(gu, up)
+        down_own[...] = nt(act, down_t)
+        for i in range(3):
+
+            @pl.when(k == i)
+            def _():
+                gn_fold.put(i, gn_own[...])
+                gn_fold.copy(i).start()
+                down_fold.put(i, down_own[...])
+                if i != 1:
+                    down_fold.copy(i).start()
+
+        return 0
+
+    lax.fori_loop(0, 4, feed, 0)
+    for item in (x_spread, cot_spread, wout_spread, a_gather, u_gather, d_gather):
+        item.finish()
+    for i in range(blocks):
+        c_spread(i).finish()
+
+    @pl.when(place >= 1)
+    def _():
+        halo_spread.finish()
+
+    @pl.when(place < per_tree - 1)
+    def _():
+        halo_copy().wait_send()
+
+    @pl.when(place < per_tree - 2)
+    def _():
+        far_copy().wait_send()
+
+    def ffn_grads(j, _):
+        at = pl.multiple_of(j * 256, 256)
+        f_ref[pl.ds(at, 256), 0:hidden] = tn(n2_ref[:, pl.ds(at, 256)], gu_ref[...]).astype(BF)
+        f_ref[pl.ds(at, 256), hidden : 2 * hidden] = tn(cot_all[:, pl.ds(at, 256)], a_ref[...]).astype(BF)
+        return 0
+
+    lax.fori_loop(0, width // 256, ffn_grads, 0)
+    f_settle.start()
+
+    gn2 = gn_fold.total(gn_own[...])
+    mid = mid_ref[...]
+    r2 = lax.rsqrt(jnp.mean(mid * mid, axis=-1, keepdims=True) + EPS)
+    hat2 = mid * r2
+    scaled = gn2 * gain_ref[1:2, :]
+    inner = jnp.mean(scaled * hat2, axis=-1, keepdims=True)
+    gmid = cot_ref[...].astype(F32) + r2 * (scaled - hat2 * inner)
+    gmid_ref[...] = gmid
+    gmb_ref[pl.ds(t * rows, rows), :] = gmid.astype(BF)
+    gmb_spread.start()
+    gn_fold.finish()
+
+    def turn_keys(i, _):
+        at = pl.multiple_of(i * SEG, SEG)
+        turn_ref[:, pl.ds(at, SEG)] = k_ref[pl.ds(at, SEG), :].T
+        return 0
+
+    lax.fori_loop(0, blocks + back, turn_keys, 0)
+
+    def mask_queries(i, _):
+        at = pl.multiple_of(i * SEG, SEG)
+        q = q_ref[pl.ds(at, SEG), :]
+        for h in range(3):
+            a_ref[pl.ds(at, SEG), h * cols : (h + 1) * cols] = jnp.where(head_mask(h, SEG, cols), q, jnp.zeros_like(q))
+        return 0
+
+    lax.fori_loop(0, blocks, mask_queries, 0)
+    gmb_spread.forward()
+    gmb_spread.wait()
+    down_fold.copy(1).start()
+
+    def context_grads(i, _):
+        at = pl.multiple_of(i * SEG, SEG)
+        low = nt(gmb_ref[pl.ds(at, SEG), :], wo_ref[...]).astype(BF)
+        gct = low.astype(F32).T
+        for h in range(3):
+            gu_ref[pl.ds(at, SEG), h * cols : (h + 1) * cols] = jnp.where(
+                head_mask(h, SEG, cols), low, jnp.zeros_like(low)
+            )
+            c = ct_ref[pl.ds(t * wide + h * HD, HD), pl.ds(at, SEG)].astype(F32)
+            delta_ref[h : h + 1, pl.ds(at, SEG)] = jnp.sum(gct[h * HD : (h + 1) * HD] * c, axis=0, keepdims=True)
+        return 0
+
+    lax.fori_loop(0, blocks, context_grads, 0)
+    qm_ref, gm_ref = a_ref, gu_ref
+
+    def piece(i, lo, hi, first):
+        at, n = i * SEG, hi - lo
+        keys = pl.ds(lo * SEG, n * SEG)
+        values = pl.ds(ext + lo * SEG, n * SEG)
+        for h in range(3):
+            head = slice(h * cols, (h + 1) * cols)
+            turned = slice(h * HD, (h + 1) * HD)
+            qm, gm = qm_ref[at : at + SEG, head], gm_ref[at : at + SEG, head]
+            s = nt(k_ref[keys, :], qm)
+            g = nt(v_ref[keys, :], gm)
+            logsum, delta = l_ref[h : h + 1, at : at + SEG], delta_ref[h : h + 1, at : at + SEG]
+            for j in range(n):
+                bias = block_bias(seg_ref, par_ref, dp * blocks + i, back + i - lo - j)
+                part = slice(j * SEG, (j + 1) * SEG)
+                x = s[part] * LOG2E
+                if lo + j == i:
+                    x = x + tri_ref[1]
+                if lo + j == i + back:
+                    x = x + tri_ref[0]
+                p = jnp.exp2(x - (logsum - bias))
+                e_ref[h, part, :] = p.astype(BF)
+                xe_ref[part, head] = (p * (g[part] - delta)).astype(BF)
+            dv = nn(e_ref[h, 0 : n * SEG, :], gm)
+            ds = xe_ref[0 : n * SEG, head]
+            dk = nn(ds, qm)
+            dq = nn(turn_ref[turned, keys], ds)
+            if first and h == 0:
+                pool_ref[values, :] = dv
+                pool_ref[keys, :] = dk
+            else:
+                pool_ref[values, :] += dv
+                pool_ref[keys, :] += dk
+            if lo < back:
+                dqt_ref[turned, at : at + SEG] = dq
+            else:
+                dqt_ref[turned, at : at + SEG] += dq
+
+    for i in range(blocks):
+        piece(i, i, back, i == 0)
+    for i in range(back):
+        at = pl.ds(i * SEG, SEG)
+        halo_ref[at, :] = jnp.concatenate(
+            [pool_ref[at, 0:wide], pool_ref[pl.ds(ext + i * SEG, SEG), 0:wide]], axis=1
+        ).astype(BF)
+
+    @pl.when(place >= 1)
+    def _():
+        for i in range(4):
+            back_copy(i).start()
+
+    @pl.when(place >= 2)
+    def _():
+        far_back().start()
+
+    for step in (2, 1, 3):
+        f_settle.pass_on(step)
+    for i in range(blocks - 1, -1, -1):
+        piece(i, back, back + i + 1, i == blocks - 1)
+
+    def turn_queries(i, _):
+        at = pl.multiple_of(i * SEG, SEG)
+        q_ref[pl.ds(at, SEG), 0:wide] = (dqt_ref[:, pl.ds(at, SEG)] * HD**-0.5).astype(BF).T
+        return 0
+
+    lax.fori_loop(0, blocks, turn_queries, 0)
+    gout = nn(ct_ref[pl.ds(t * wide, wide), :], gmb_ref[...]).astype(BF).T
+    out_ref[...] = (mid_ref[...] + down_fold.total(down_own[...])).astype(BF)
+
+    @pl.when(place < per_tree - 2)
+    def _():
+        far_back().wait_recv()
+        for j in range(2):
+            at = pl.ds(j * ext + WINDOW + token - lag, lag)
+            pool_ref[at, 0:wide] += back_ref[0:lag, j * wide : (j + 1) * wide].astype(F32)
+
+    def outer(k, _):
+        at = (t ^ (3 - k)) * rows
+
+        @pl.when(place < per_tree - 1)
+        def _():
+            for i in range(4):
+
+                @pl.when(k == i)
+                def _():
+                    back_copy(i).wait_recv()
+
+            for j in range(2):
+                here = pl.ds(j * ext + WINDOW + at, rows)
+                pool_ref[here, 0:wide] += back_ref[pl.ds(lag + at, rows), j * wide : (j + 1) * wide].astype(F32)
+
+        gq = q_ref[pl.ds(at, rows), 0:wide]
+        gk = pool_ref[pl.ds(WINDOW + at, rows), 0:wide].astype(BF)
+        gv = pool_ref[pl.ds(ext + WINDOW + at, rows), 0:wide].astype(BF)
+        k_ref[pl.ds(at, rows), 0:wide] = gk
+        v_ref[pl.ds(at, rows), 0:wide] = gv
+        gn_own[...] = nt(gq, wq_ref[:, 0:wide]) + nt(gk, wk_ref[:, 0:wide]) + nt(gv, wv_ref[:, 0:wide])
+        for i in range(3):
+
+            @pl.when(k == i)
+            def _():
+                gn1_fold.put(i, gn_own[...])
+                gn1_fold.copy(i).start()
+
+        return 0
+
+    lax.fori_loop(0, 4, outer, 0)
+
+    grads = [tn(n1_ref[...], ref[0:token, 0:wide]).astype(BF) for ref in (q_ref, k_ref, v_ref)]
+    w_ref[0:width, :] = jnp.concatenate(grads + [gout], axis=1)
+    a_settle.start()
+    gf = f_settle.total()
+    gup_ref[...] = gf[:, 0:hidden]
+    gdown_ref[...] = gf[:, hidden : 2 * hidden].T
+    two_sum = jnp.sum(gf[:, 0:hidden] * wu_in[...].astype(F32), axis=1, keepdims=True)
+    for step in (2, 1, 3):
+        a_settle.pass_on(step)
+
+    gn1 = gn1_fold.total(gn_own[...])
+    x = x_ref[...].astype(F32)
+    r1 = lax.rsqrt(jnp.mean(x * x, axis=-1, keepdims=True) + EPS)
+    hat1 = x * r1
+    scaled = gn1 * gain_ref[0:1, :]
+    inner = jnp.mean(scaled * hat1, axis=-1, keepdims=True)
+    ing_ref[...] = (gmid_ref[...] + r1 * (scaled - hat1 * inner)).astype(BF)
+
+    ga = a_settle.total()
+    one_sum = None
+    for j, (ref, own) in enumerate(((gq_out, wq_in), (gk_out, wk_in), (gv_out, wv_in))):
+        part = ga[:, j * wide : (j + 1) * wide]
+        ref[...] = part
+        part = jnp.sum(part * own[...].astype(F32), axis=1, keepdims=True)
+        one_sum = part if one_sum is None else one_sum + part
+    gout_ref[...] = ga[:, 3 * wide : 4 * wide].T
+    lane = lax.broadcasted_iota(jnp.int32, (deep, 128), 1)
+    gain_buf[0] = jnp.where(lane < 64, one_sum, two_sum)
+    for i in range(3):
+        gain_copy(i).start()
+    total = gain_buf[0]
+    for i in range(3):
+        gain_copy(i).wait_recv()
+        total = total + gain_buf[i + 1]
+    turned = total.T
+    gg1_ref[...] = turned[0:1] / g1_ref[...].astype(F32)
+    gg2_ref[...] = turned[64:65] / g2_ref[...].astype(F32)
+    for i in range(3):
+        gain_copy(i).wait_send()
+    for item in (down_fold, gn1_fold, gmb_spread, f_settle, a_settle):
+        item.finish()
+
+    @pl.when(place >= 1)
+    def _():
+        for i in range(4):
+            back_copy(i).wait_send()
+
+    @pl.when(place >= 2)
+    def _():
+        far_back().wait_send()
+
+
+def fast_shards(
+    layer_input, cotangent, segments, parents, norm1_gain, w_query, w_key, w_value, w_out, norm2_gain, w_up, w_down,
+):
+    rows, width = layer_input.shape
+    token = 4 * rows
+    ext = token + WINDOW
+    wide = width // 4
+    cols = 256 * pl.cdiv(wide, 256)
+    deep, hidden = w_up.shape
+    blocks = token // SEG
+    span = WINDOW + SEG
+    shape = jax.ShapeDtypeStruct
+    vmem = pl.BlockSpec(memory_space=pltpu.VMEM)
+    smem = pl.BlockSpec(memory_space=pltpu.SMEM)
+    copies = 5 * 3 + 3 * 8 + 2 + 3 * blocks + 3 * 3 + 2 * 7 + 5 + 3
+    results = pl.pallas_call(
+        kernel,
+        out_shape=[
+            shape((rows, width), BF),
+            shape((rows, width), BF),
+            shape((1, deep), F32),
+            shape((deep, wide), F32),
+            shape((deep, wide), F32),
+            shape((deep, wide), F32),
+            shape((wide, deep), F32),
+            shape((1, deep), F32),
+            shape((deep, hidden), F32),
+            shape((hidden, deep), F32),
+        ],
+        in_specs=[smem, smem] + [vmem] * 10,
+        out_specs=[vmem] * 10,
+        scratch_shapes=[
+            pltpu.VMEM((ext, width), BF),
+            pltpu.VMEM((token, width), BF),
+            pltpu.VMEM((token, width), BF),
+            pltpu.VMEM((rows, width), F32),
+            pltpu.VMEM((rows, width), F32),
+            pltpu.VMEM((8 * (deep + 16), width), BF),
+            pltpu.VMEM((width, 2 * hidden), BF),
+            pltpu.VMEM((token, width), BF),
+            pltpu.VMEM((width, width), BF),
+            pltpu.VMEM((cols, width), BF),
+            pltpu.VMEM((width, cols), BF),
+            pltpu.VMEM((width, cols), BF),
+            pltpu.VMEM((width, cols), BF),
+            pltpu.VMEM((token, cols), BF),
+            pltpu.VMEM((ext, cols), BF),
+            pltpu.VMEM((ext, cols), BF),
+            pltpu.VMEM((cols, ext), BF),
+            pltpu.VMEM((width, token), BF),
+            pltpu.VMEM((8, token), F32),
+            pltpu.VMEM((8, width), F32),
+            pltpu.VMEM((8, token), F32),
+            pltpu.VMEM((2 * ext, SEG), F32),
+            pltpu.VMEM((3, span, SEG), BF),
+            pltpu.VMEM((2, SEG, SEG), F32),
+            pltpu.VMEM((token, hidden), BF),
+            pltpu.VMEM((token, hidden), BF),
+            pltpu.VMEM((rows, width), F32),
+            pltpu.VMEM((rows, width), F32),
+            pltpu.VMEM((6, rows, width), BF),
+            pltpu.VMEM((6, rows, width), BF),
+            pltpu.VMEM((token, width), BF),
+            pltpu.VMEM((4, deep, 2 * hidden), BF),
+            pltpu.VMEM((3, deep, 2 * hidden), BF),
+            pltpu.VMEM((4, deep, width), BF),
+            pltpu.VMEM((3, deep, width), BF),
+            pltpu.VMEM((wide, token), F32),
+            pltpu.VMEM((WINDOW, 2 * wide), BF),
+            pltpu.VMEM((WINDOW, 2 * wide), BF),
+            pltpu.VMEM((4, deep, 128), F32),
+            pltpu.SemaphoreType.DMA((copies,)),
+            pltpu.SemaphoreType.DMA((copies,)),
+        ],
+        compiler_params=pltpu.CompilerParams(
+            collective_id=0, has_side_effects=True, vmem_limit_bytes=64 << 20
+        ),
+    )(
+        segments, parents, layer_input, cotangent, norm1_gain[None], w_query, w_key, w_value, w_out,
+        norm2_gain[None], w_up, w_down,
+    )
+    results = list(results)
+    results[2], results[7] = results[2][0], results[7][0]
+    return tuple(results)
 
 
 epsilon = 1e-06
@@ -320,8 +1125,9 @@
 
 
 def solution(mesh):
+    fast = mesh.shape["dp"] == 8 and mesh.shape["tensor"] == 4
     return jax.shard_map(
-        shards,
+        fast_shards if fast else shards,
         mesh=mesh,
         in_specs=(
             P(("dp", "tensor"), None),

time: 779 us -> 203 us (0.26)
  waiting for transfers between devices: 259 us -> 0 us
  Pallas kernels: 0 us -> 191 us
  blocking collectives: 170 us -> 0 us
  matrix products: 150 us -> 0 us
  other arithmetic: 107 us -> 0 us
  local copies, waits for them, and re-layouts: 43.4 us -> 9.99 us
  starting transfers between devices: 24.4 us -> 0 us
  between operations: 17.2 us -> 0.67 us
    pallas_call x0 -> x1, Pallas kernels: none -> 191 us  [fast_shards(): pl.pallas_call(kernel, out_shape=[shape((rows, width), BF), shape((rows,...]
    dot_general x32 -> x0, matrix products: 150 us -> none  [the longest x4 46.3 us: scores_of(): jnp.einsum('qhd,khd->hqk', query_block, key_block, preferred_element_type...]
    all_gather x4 -> x0, blocking collectives: 139 us -> none  [the longest x1 46 us: shards(): lax.all_gather(w_out, 'dp', axis=1, tiled=True)]
    all_gather x6 -> x0, waiting for transfers between devices: 113 us -> none  [the longest x1 38.4 us: shards(): lax.all_gather(w_down, 'dp', axis=1, tiled=True)]
    reduce_scatter x4 -> x0, waiting for transfers between devices: 63.5 us -> none  [the longest x1 32.8 us: shards(): lax.psum_scatter(jnp.dot(context, full_out, preferred_element_type=jnp.fl...]
    all_to_all x4 -> x0, waiting for transfers between devices: 51.2 us -> none  [sum_at_owner(): lax.all_to_all(tiles, axis, split_axis=0, concat_axis=0, tiled=True)]
    convert_element_type x9 -> x0, other arithmetic: 36 us -> none  [the longest x2 22.8 us: backward_block(): grad_scores = (probs * (grad_probs - inner)).astype(jnp.bfloat16)]
    reduce_sum x12 -> x0, other arithmetic: 31.6 us -> none  [the longest x2 21 us: forward_block(): denominator = jnp.sum(exponent, axis=-1, keepdims=True)]
  transfers between devices with their start and end apart: 18 -> 0, of which waited for: 12 -> 0; matrix products, arithmetic and copies ran while one was open for 8% -> 0% of each run, Pallas kernels for 0% -> 0%
where the time goes in v3:
time: 203 us; the launch traced here: 201 us
  Pallas kernels  191 us (94%)
  local copies, waits for them, and re-layouts  9.99 us (5%)
    pallas_call x1, Pallas kernels, fast_shards(): pl.pallas_call(kernel, out_shape=[shape((rows, width), BF), shape((rows,...  191 us
    unnamed x29, local copies, waits for them, and re-layouts  9.99 us

profile of v3, /device:TPU:0, one launch (start us, length us, event | category | flops | bytes accessed | tf_op | source)
XLA Modules:
  0.0 201.3 jit_solution(8228164450959250716)
XLA Ops:
  0.6 1.7 copy.22.wd_in
  2.4 190.7 %shard_map.195 = (bf16[320,768]{1,0:T(8,128)(2,1)}, bf16[320,768]{1,0:T(8,128)(2,1)}, f32[1,96]{1,0:T(1,128)}, f32[96,192]{1,0:T(8,128)}, f32[96,192]{1,0:T(8,12...) custom-call(s32[10240]{0:T(1024)} %seg_ref.1, ...), custom_call_target="tpu_custom_call" | custom-call | tf_op jit(solution)/shard_map/pallas_call | solution.py:746
  193.1 0.0 copy-start.1
  193.1 1.9 copy.23
  195.0 0.0 copy-done.1
  195.0 0.0 copy-start
  195.0 0.8 copy.33
  195.8 0.4 copy-done
  196.2 0.0 copy-start.8
  196.2 0.8 copy.34
  197.0 0.0 copy-done.8
  197.0 0.5 copy.35
  197.5 0.0 copy-done.6
  197.5 0.6 copy.36
  198.1 0.0 copy-done.5
  198.2 0.6 copy.37
  198.8 0.0 copy-done.4
  198.8 0.6 copy.38
  199.4 0.0 copy-done.3
  199.4 0.6 copy.39
  200.1 0.0 copy-done.7
  200.1 0.5 copy.40
  200.6 0.0 copy-done.2
  200.6 0.7 copy.41
  (6 shorter events, 0.0 us)
Async XLA Ops:
  193.1 1.9 copy-start.1
  195.0 1.2 copy-start
  196.2 0.8 copy-start.8
  196.2 1.3 copy-start.6
  196.2 1.9 copy-start.5
  197.5 1.3 copy-start.4
  197.5 1.9 copy-start.3
  198.1 2.5 %copy-start.2 = (f32[96,768]{1,0:T(8,128)S(1)}, f32[96,768]{1,0:T(8,128)}, u32[]{:S(2)}) copy-start(f32[96,768]{1,0:T(8,128)} %get-tuple-element.58) | copy-start | bytes 884740
  199.4 0.7 copy-start.7

commit v4 on v3

--- a/solution.py
+++ b/solution.py
@@ -145,25 +145,25 @@
 
 
 class Fold:
-    def __init__(self, links, base, dp, t, buf):
-        self.links, self.base, self.dp, self.t, self.buf = links, base, dp, t, buf
+    def __init__(self, links, base, dp, t, out, into):
+        self.links, self.base, self.dp, self.t, self.out, self.into = links, base, dp, t, out, into
 
     def copy(self, i):
         flip = (1, 2, 1)[i]
         return self.links.copy(
-            self.buf.at[i], self.buf.at[3 + i], self.base + i, self.base + i, (self.dp, self.t ^ flip)
+            self.out(i), self.into(i), self.base + i, self.base + i, (self.dp, self.t ^ flip)
         )
 
     def put(self, i, value):
         if i == 1:
             self.copy(0).wait_recv()
-            value = value + self.buf[3].astype(F32)
-        self.buf[i] = value.astype(BF)
+            value = value + self.into(0)[...].astype(F32)
+        self.out(i)[...] = value.astype(BF)
 
     def total(self, value):
         self.copy(1).wait_recv()
         self.copy(2).wait_recv()
-        return value + self.buf[5].astype(F32) + self.buf[4].astype(F32)
+        return value + self.into(2)[...].astype(F32) + self.into(1)[...].astype(F32)
 
     def finish(self):
         for i in range(3):
@@ -231,7 +231,7 @@
     xe_ref, n1_ref, n2_ref, mid_ref, gmid_ref, w_ref, f_ref, cot_all, wout_ref, wo_ref, wq_ref, wk_ref, wv_ref,
     q_ref, k_ref, v_ref, turn_ref, ct_ref, l_ref, gain_ref, delta_ref, pool_ref, e_ref, tri_ref,
     a_ref, gu_ref, down_own, gn_own, down_buf, gn_buf, gmb_ref,
-    gfy_ref, gfz_ref, gay_ref, gaz_ref, dqt_ref, halo_ref, back_ref, gain_buf, send, recv,
+    gfy_ref, gfz_ref, go_ref, goy_ref, goz_ref, gay_ref, gaz_ref, dqt_ref, near_buf, far_buf, gt_buf, gd_buf, send, recv,
 ):
     dp, t = lax.axis_index("dp"), lax.axis_index("tensor")
     rows, width = x_ref.shape
@@ -249,19 +249,26 @@
     links = Links(send, recv)
     spread = lambda part: Spread(links, links.take(3), dp, t, part)
     x_spread = spread(lambda p: xe_ref.at[pl.ds(WINDOW + p * rows, rows)])
-    halo = lambda p: xe_ref.at[pl.ds(lag + p * rows, rows)]
-    halo_spread = spread(halo)
+    part = rows // 2
+    halo_half = lambda p, j: xe_ref.at[pl.ds(lag + p * rows + j * part, part)]
+    halo_spreads = [spread(lambda p, j=j: halo_half(p, j)) for j in range(2)]
     cot_spread = spread(lambda p: cot_all.at[pl.ds(p * rows, rows)])
     wout_spread = spread(lambda p: wout_ref.at[pl.ds(p * wide, wide)])
-    gmb_spread = spread(lambda p: gmb_ref.at[pl.ds(p * rows, rows)])
+    gmb_spreads = [spread(lambda p, j=j: gmb_ref.at[pl.ds(p * rows + j * part, part)]) for j in range(2)]
     slot = deep + 16
-    a_gather = Gather(links, links.take(8), dp, t, lambda s: w_ref.at[pl.ds(pl.multiple_of(s * slot, 16), slot)])
+    a_slot = lambda s: pl.ds(pl.multiple_of(s * slot, 16), slot)
+    half = width // 2
+    a_gathers = [
+        Gather(links, links.take(8), dp, t, lambda s, j=j: w_ref.at[a_slot(s), pl.ds(j * half, half)]) for j in range(2)
+    ]
     f_slot = lambda s: pl.ds(pl.multiple_of(s * deep, deep), deep)
     u_gather = Gather(links, links.take(8), dp, t, lambda s: f_ref.at[f_slot(s), pl.ds(0, hidden)])
     d_gather = Gather(links, links.take(8), dp, t, lambda s: f_ref.at[f_slot(s), pl.ds(hidden, hidden)])
-    h1 = links.take(1)
+    h1 = links.take(2)
     h2 = links.take(1)
-    halo_copy = lambda: links.copy(x_ref, halo(t), h1, h1, (lax.rem(dp + 1, 8), t))
+    halo_copy = lambda j: links.copy(
+        x_ref.at[pl.ds(j * part, part)], halo_half(t, j), h1 + j, h1 + j, (lax.rem(dp + 1, 8), t)
+    )
     far_copy = lambda: links.copy(
         xe_ref.at[pl.ds(WINDOW + token - lag, lag)], xe_ref.at[pl.ds(0, lag)], h2, h2, (lax.rem(dp + 2, 8), t)
     )
@@ -271,25 +278,42 @@
         at = pl.multiple_of(i * SEG, SEG)
         return Spread(links, c_base + 3 * i, dp, t, lambda p: ct_ref.at[pl.ds(p * wide, wide), pl.ds(at, SEG)])
 
-    down_fold = Fold(links, links.take(3), dp, t, down_buf)
-    gn_fold = Fold(links, links.take(3), dp, t, gn_buf)
-    gn1_fold = Fold(links, links.take(3), dp, t, gn_buf)
+    down_fold = Fold(links, links.take(3), dp, t, lambda i: down_buf.at[i], lambda i: down_buf.at[3 + i])
+    gn_folds = [
+        Fold(
+            links,
+            links.take(3),
+            dp,
+            t,
+            lambda i, j=j: gn_buf.at[i, pl.ds(j * part, part)],
+            lambda i, j=j: gn_buf.at[3 + i, pl.ds(j * part, part)],
+        )
+        for j in range(2)
+    ]
+    gn1_fold = Fold(links, links.take(3), dp, t, lambda i: gn_buf.at[i], lambda i: gn_buf.at[3 + i])
+    halo_fold = Fold(
+        links,
+        links.take(3),
+        dp,
+        t,
+        lambda i: cot_all.at[pl.ds(i * rows, rows)],
+        lambda i: n2_ref.at[pl.ds(i * rows, rows)],
+    )
     f_settle = Settle(links, links.take(7), dp, t, f_ref, deep, gfy_ref, gfz_ref)
-    a_settle = Settle(links, links.take(7), dp, t, w_ref, deep, gay_ref, gaz_ref)
-    hb = links.take(5)
-
-    def back_copy(i):
-        at = pl.ds(lag + (t ^ (3 - i)) * rows, rows)
-        return links.copy(halo_ref.at[at], back_ref.at[at], hb + i, hb + i, (lax.rem(dp + 7, 8), t))
-
-    def far_back():
-        at = pl.ds(0, lag)
-        return links.copy(halo_ref.at[at], back_ref.at[at], hb + 4, hb + 4, (lax.rem(dp + 6, 8), t))
-
+    o_settle = Settle(links, links.take(7), dp, t, go_ref, deep, goy_ref, goz_ref)
+    a_settle = Settle(links, links.take(7), dp, t, w_ref.at[:, pl.ds(0, gay_ref.shape[2])], deep, gay_ref, gaz_ref)
+    b1 = links.take(1)
+    b2 = links.take(1)
+    near_back = lambda: links.copy(cot_all.at[pl.ds(3 * rows, rows)], near_buf, b1, b1, (lax.rem(dp + 7, 8), t))
+    far_back = lambda: links.copy(far_buf.at[0], far_buf.at[1], b2, b2, (lax.rem(dp + 6, 8), t))
     gb = links.take(3)
+    gd = links.take(7)
 
     def gain_copy(i):
-        return links.copy(gain_buf.at[0], gain_buf.at[i + 1], gb + i, gb + i, (dp, t ^ (i + 1)))
+        return links.copy(gt_buf.at[0], gt_buf.at[i + 1], gb + i, gb + i, (dp, t ^ (i + 1)))
+
+    def gain_over(i):
+        return links.copy(gd_buf.at[0], gd_buf.at[i + 1], gd + i, gd + i, (lax.rem(dp + i + 1, 8), t))
 
     barrier = pltpu.get_barrier_semaphore()
     for step in range(1, 8):
@@ -308,15 +332,15 @@
     w_ref[pl.ds(base + deep, 16), :] = nn(two, put).astype(BF)
     xe_ref[pl.ds(WINDOW + t * rows, rows), :] = x_ref[...]
     pl.semaphore_wait(barrier, 10)
+    a_gathers[0].start()
     x_spread.start()
 
     @pl.when(place < per_tree - 1)
     def _():
-        halo_copy().start()
-
-    a_gather.start()
+        halo_copy(0).start()
+
     f_ref[f_slot(dp), 0:hidden] = wu_in[...]
-    f_ref[f_slot(dp), hidden : 2 * hidden] = wd_in[...].astype(F32).T.astype(BF)
+    f_ref[f_slot(dp), hidden : 2 * hidden] = wd_in[...]
     cot_all[pl.ds(t * rows, rows), :] = cot_ref[...]
 
     @pl.when(place < 1)
@@ -331,15 +355,29 @@
     col = lax.broadcasted_iota(jnp.int32, (SEG, SEG), 1)
     tri_ref[0] = jnp.where(row <= col, 0.0, NEG)
     tri_ref[1] = jnp.where(row > col, 0.0, NEG)
-    a_gather.forward(1)
+    for step in (1, 3, 2):
+        a_gathers[0].forward(step)
+    a_gathers[1].start()
+
+    @pl.when(place < per_tree - 1)
+    def _():
+        halo_copy(0).wait_send()
+        halo_copy(1).start()
+
+    @pl.when(place >= 1)
+    def _():
+        halo_copy(0).wait_recv()
+        halo_spreads[0].start()
+
     x_spread.forward()
-    a_gather.forward(3)
-    a_gather.forward(2)
+    for step in (1, 3, 2):
+        a_gathers[1].forward(step)
 
     @pl.when(place >= 1)
     def _():
-        halo_copy().wait_recv()
-        halo_spread.start()
+        halo_copy(1).wait_recv()
+        halo_spreads[1].start()
+        halo_spreads[0].forward()
 
     x_spread.wait()
 
@@ -347,8 +385,9 @@
     def _():
         far_copy().start()
 
+    for item in a_gathers:
+        item.wait()
     u_gather.start()
-    a_gather.wait()
     weights = w_ref[...].reshape(8, slot, width)[:, 0:deep].reshape(width, width)
     for j, ref in enumerate((wq_ref, wk_ref, wv_ref)):
         ref[...] = jnp.concatenate(
@@ -357,6 +396,7 @@
     wo_ref[0:wide, :] = weights[:, 3 * wide : 4 * wide].T
     wo_ref[wide:cols, :] = jnp.zeros((cols - wide, width), BF)
     wout_ref[pl.ds(t * wide, wide), :] = wo_ref[0:wide, :]
+    wout_spread.start()
     gain_ref[...] = jnp.sum(w_ref[...].reshape(8, slot, width)[:, deep:slot].astype(F32), axis=0)[0:8]
 
     def norm_rows(at):
@@ -380,10 +420,11 @@
 
     @pl.when(place >= 1)
     def _():
-        halo_spread.forward()
-        halo_spread.wait()
-
-    wout_spread.start()
+        halo_spreads[1].forward()
+        for item in halo_spreads:
+            item.wait()
+            item.finish()
+
     cot_spread.start()
 
     @pl.when(place >= 2)
@@ -391,7 +432,8 @@
         far_copy().wait_recv()
 
     def halo_rows(i, _):
-        norm_rows(pl.multiple_of(i * SEG, SEG))
+        at = pl.multiple_of(i * SEG, SEG)
+        xe_ref[pl.ds(at, SEG), :] = norm_rows(at)
         return 0
 
     lax.fori_loop(0, back, halo_rows, 0)
@@ -488,8 +530,10 @@
 
             @pl.when(k == i)
             def _():
-                gn_fold.put(i, gn_own[...])
-                gn_fold.copy(i).start()
+                for j in range(2):
+                    gn_folds[j].put(i, gn_own[j * part : (j + 1) * part, :])
+                    if i != 1 or j == 0:
+                        gn_folds[j].copy(i).start()
                 down_fold.put(i, down_own[...])
                 if i != 1:
                     down_fold.copy(i).start()
@@ -497,43 +541,47 @@
         return 0
 
     lax.fori_loop(0, 4, feed, 0)
-    for item in (x_spread, cot_spread, wout_spread, a_gather, u_gather, d_gather):
+    gn_folds[1].copy(1).start()
+    for item in (x_spread, cot_spread, wout_spread, *a_gathers, u_gather, d_gather):
         item.finish()
     for i in range(blocks):
         c_spread(i).finish()
 
-    @pl.when(place >= 1)
-    def _():
-        halo_spread.finish()
-
     @pl.when(place < per_tree - 1)
     def _():
-        halo_copy().wait_send()
+        halo_copy(1).wait_send()
 
     @pl.when(place < per_tree - 2)
     def _():
         far_copy().wait_send()
+
+    ones = jnp.ones((8, hidden), BF)
 
     def ffn_grads(j, _):
         at = pl.multiple_of(j * 256, 256)
-        f_ref[pl.ds(at, 256), 0:hidden] = tn(n2_ref[:, pl.ds(at, 256)], gu_ref[...]).astype(BF)
+        g = tn(n2_ref[:, pl.ds(at, 256)], gu_ref[...])
+        gt_buf[0, :, pl.ds(at, 256)] = nt(ones, (g * f_ref[pl.ds(at, 256), 0:hidden].astype(F32)).astype(BF))
+        f_ref[pl.ds(at, 256), 0:hidden] = g.astype(BF)
         f_ref[pl.ds(at, 256), hidden : 2 * hidden] = tn(cot_all[:, pl.ds(at, 256)], a_ref[...]).astype(BF)
         return 0
 
     lax.fori_loop(0, width // 256, ffn_grads, 0)
     f_settle.start()
 
-    gn2 = gn_fold.total(gn_own[...])
-    mid = mid_ref[...]
-    r2 = lax.rsqrt(jnp.mean(mid * mid, axis=-1, keepdims=True) + EPS)
-    hat2 = mid * r2
-    scaled = gn2 * gain_ref[1:2, :]
-    inner = jnp.mean(scaled * hat2, axis=-1, keepdims=True)
-    gmid = cot_ref[...].astype(F32) + r2 * (scaled - hat2 * inner)
-    gmid_ref[...] = gmid
-    gmb_ref[pl.ds(t * rows, rows), :] = gmid.astype(BF)
-    gmb_spread.start()
-    gn_fold.finish()
+    for j in range(2):
+        here = slice(j * part, (j + 1) * part)
+        gn2 = gn_folds[j].total(gn_own[here, :])
+        mid = mid_ref[here, :]
+        r2 = lax.rsqrt(jnp.mean(mid * mid, axis=-1, keepdims=True) + EPS)
+        hat2 = mid * r2
+        scaled = gn2 * gain_ref[1:2, :]
+        inner = jnp.mean(scaled * hat2, axis=-1, keepdims=True)
+        gmid = cot_ref[here, :].astype(F32) + r2 * (scaled - hat2 * inner)
+        gmid_ref[here, :] = gmid
+        gmb_ref[pl.ds(t * rows + j * part, part), :] = gmid.astype(BF)
+        gmb_spreads[j].start()
+    for item in gn_folds:
+        item.finish()
 
     def turn_keys(i, _):
         at = pl.multiple_of(i * SEG, SEG)
@@ -550,9 +598,10 @@
         return 0
 
     lax.fori_loop(0, blocks, mask_queries, 0)
-    gmb_spread.forward()
-    gmb_spread.wait()
-    down_fold.copy(1).start()
+    for item in gmb_spreads:
+        item.forward()
+    for item in gmb_spreads:
+        item.wait()
 
     def context_grads(i, _):
         at = pl.multiple_of(i * SEG, SEG)
@@ -567,6 +616,8 @@
         return 0
 
     lax.fori_loop(0, blocks, context_grads, 0)
+    go_ref[...] = nn(ct_ref[pl.ds(t * wide, wide), :], gmb_ref[...]).astype(BF).T
+    o_settle.start()
     qm_ref, gm_ref = a_ref, gu_ref
 
     def piece(i, lo, hi, first):
@@ -590,9 +641,9 @@
                     x = x + tri_ref[0]
                 p = jnp.exp2(x - (logsum - bias))
                 e_ref[h, part, :] = p.astype(BF)
-                xe_ref[part, head] = (p * (g[part] - delta)).astype(BF)
+                xe_ref[WINDOW + j * SEG : WINDOW + (j + 1) * SEG, head] = (p * (g[part] - delta)).astype(BF)
             dv = nn(e_ref[h, 0 : n * SEG, :], gm)
-            ds = xe_ref[0 : n * SEG, head]
+            ds = xe_ref[WINDOW : WINDOW + n * SEG, head]
             dk = nn(ds, qm)
             dq = nn(turn_ref[turned, keys], ds)
             if first and h == 0:
@@ -601,32 +652,71 @@
             else:
                 pool_ref[values, :] += dv
                 pool_ref[keys, :] += dk
-            if lo < back:
+            if lo == i:
                 dqt_ref[turned, at : at + SEG] = dq
             else:
                 dqt_ref[turned, at : at + SEG] += dq
 
-    for i in range(blocks):
-        piece(i, i, back, i == 0)
-    for i in range(back):
-        at = pl.ds(i * SEG, SEG)
-        halo_ref[at, :] = jnp.concatenate(
-            [pool_ref[at, 0:wide], pool_ref[pl.ds(ext + i * SEG, SEG), 0:wide]], axis=1
-        ).astype(BF)
-
-    @pl.when(place >= 1)
-    def _():
-        for i in range(4):
-            back_copy(i).start()
+    def outer(at, k, fold, with_query):
+        gk = pool_ref[pl.ds(at, rows), 0:wide].astype(BF)
+        gv = pool_ref[pl.ds(ext + at, rows), 0:wide].astype(BF)
+        k_ref[pl.ds(at, rows), 0:wide] = gk
+        v_ref[pl.ds(at, rows), 0:wide] = gv
+        part = nt(gk, wk_ref[:, 0:wide]) + nt(gv, wv_ref[:, 0:wide])
+        if with_query:
+            part = part + nt(q_ref[pl.ds(at - WINDOW, rows), 0:wide], wq_ref[:, 0:wide])
+        gn_own[...] = part
+        if with_query:
+
+            @pl.when((place < per_tree - 2) & (t ^ (3 - k) == 3))
+            def _():
+                far_back().wait_recv()
+                gn_own[rows - lag :, :] += far_buf[1].astype(F32)
+
+        for i in range(3):
+
+            @pl.when(k == i)
+            def _():
+                fold.put(i, gn_own[...])
+                fold.copy(i).start()
+
+    piece(0, 0, 3, True)
+    piece(0, 3, back, True)
+    for i in range(1, blocks):
+        piece(i, i, back, False)
 
     @pl.when(place >= 2)
     def _():
+        gk = pool_ref[0:lag, 0:wide].astype(BF)
+        gv = pool_ref[ext : ext + lag, 0:wide].astype(BF)
+        far_buf[0] = (nt(gk, wk_ref[:, 0:wide]) + nt(gv, wv_ref[:, 0:wide])).astype(BF)
         far_back().start()
+
+    k_ref[0:lag, 0:wide] = pool_ref[0:lag, 0:wide].astype(BF)
+    v_ref[0:lag, 0:wide] = pool_ref[ext : ext + lag, 0:wide].astype(BF)
+
+    def halo_outer(k, _):
+        outer(lag + (t ^ (3 - k)) * rows, k, halo_fold, False)
+        return 0
+
+    lax.fori_loop(0, 4, halo_outer, 0)
+    for i in range(blocks - 1, 1, -1):
+        piece(i, back, back + i + 1, i == blocks - 1)
 
     for step in (2, 1, 3):
         f_settle.pass_on(step)
-    for i in range(blocks - 1, -1, -1):
-        piece(i, back, back + i + 1, i == blocks - 1)
+    for step in (2, 1, 3):
+        o_settle.pass_on(step)
+    for i in range(1, -1, -1):
+        piece(i, back, back + i + 1, False)
+
+    cot_all[3 * rows : 4 * rows, :] = halo_fold.total(gn_own[...]).astype(BF)
+
+    @pl.when(place >= 1)
+    def _():
+        near_back().start()
+
+    down_fold.copy(1).start()
 
     def turn_queries(i, _):
         at = pl.multiple_of(i * SEG, SEG)
@@ -634,59 +724,51 @@
         return 0
 
     lax.fori_loop(0, blocks, turn_queries, 0)
-    gout = nn(ct_ref[pl.ds(t * wide, wide), :], gmb_ref[...]).astype(BF).T
+
+    def own_outer(k, _):
+        outer(WINDOW + (t ^ (3 - k)) * rows, k, gn1_fold, True)
+        return 0
+
+    lax.fori_loop(0, 4, own_outer, 0)
+    grads = [
+        tn(n1_ref[...], q_ref[:, 0:wide]),
+        tn(xe_ref[0:WINDOW, :], k_ref[0:WINDOW, 0:wide]) + tn(n1_ref[...], k_ref[WINDOW:, 0:wide]),
+        tn(xe_ref[0:WINDOW, :], v_ref[0:WINDOW, 0:wide]) + tn(n1_ref[...], v_ref[WINDOW:, 0:wide]),
+    ]
+    w_ref[0:width, 0 : 3 * wide] = jnp.concatenate([g.astype(BF) for g in grads], axis=1)
+    a_settle.start()
+    terms = sum(g * w[:, 0:wide].astype(F32) for g, w in zip(grads, (wq_ref, wk_ref, wv_ref)))
+    first_row = lax.broadcasted_iota(jnp.int32, (8, width), 0) == 0
+    gt_buf[0] = jnp.where(first_row, nt(ones[:, 0:wide], terms.astype(BF)), gt_buf[0])
+    for i in range(3):
+        gain_copy(i).start()
     out_ref[...] = (mid_ref[...] + down_fold.total(down_own[...])).astype(BF)
-
-    @pl.when(place < per_tree - 2)
-    def _():
-        far_back().wait_recv()
-        for j in range(2):
-            at = pl.ds(j * ext + WINDOW + token - lag, lag)
-            pool_ref[at, 0:wide] += back_ref[0:lag, j * wide : (j + 1) * wide].astype(F32)
-
-    def outer(k, _):
-        at = (t ^ (3 - k)) * rows
-
-        @pl.when(place < per_tree - 1)
-        def _():
-            for i in range(4):
-
-                @pl.when(k == i)
-                def _():
-                    back_copy(i).wait_recv()
-
-            for j in range(2):
-                here = pl.ds(j * ext + WINDOW + at, rows)
-                pool_ref[here, 0:wide] += back_ref[pl.ds(lag + at, rows), j * wide : (j + 1) * wide].astype(F32)
-
-        gq = q_ref[pl.ds(at, rows), 0:wide]
-        gk = pool_ref[pl.ds(WINDOW + at, rows), 0:wide].astype(BF)
-        gv = pool_ref[pl.ds(ext + WINDOW + at, rows), 0:wide].astype(BF)
-        k_ref[pl.ds(at, rows), 0:wide] = gk
-        v_ref[pl.ds(at, rows), 0:wide] = gv
-        gn_own[...] = nt(gq, wq_ref[:, 0:wide]) + nt(gk, wk_ref[:, 0:wide]) + nt(gv, wv_ref[:, 0:wide])
-        for i in range(3):
-
-            @pl.when(k == i)
-            def _():
-                gn1_fold.put(i, gn_own[...])
-                gn1_fold.copy(i).start()
-
-        return 0
-
-    lax.fori_loop(0, 4, outer, 0)
-
-    grads = [tn(n1_ref[...], ref[0:token, 0:wide]).astype(BF) for ref in (q_ref, k_ref, v_ref)]
-    w_ref[0:width, :] = jnp.concatenate(grads + [gout], axis=1)
-    a_settle.start()
+    total = gt_buf[0]
+    for i in range(3):
+        gain_copy(i).wait_recv()
+        total = total + gt_buf[i + 1]
+    gd_buf[0] = total
+    for i in range(7):
+        gain_over(i).start()
     gf = f_settle.total()
     gup_ref[...] = gf[:, 0:hidden]
-    gdown_ref[...] = gf[:, hidden : 2 * hidden].T
-    two_sum = jnp.sum(gf[:, 0:hidden] * wu_in[...].astype(F32), axis=1, keepdims=True)
+    gdown_ref[...] = gf[:, hidden : 2 * hidden]
+    gout_ref[...] = o_settle.total().T
     for step in (2, 1, 3):
         a_settle.pass_on(step)
 
     gn1 = gn1_fold.total(gn_own[...])
+
+    @pl.when(place < per_tree - 1)
+    def _():
+        near_back().wait_recv()
+        gn_own[...] = near_buf[...].astype(F32)
+
+    @pl.when(place == per_tree - 1)
+    def _():
+        gn_own[...] = jnp.zeros((rows, width), F32)
+
+    gn1 = gn1 + gn_own[...]
     x = x_ref[...].astype(F32)
     r1 = lax.rsqrt(jnp.mean(x * x, axis=-1, keepdims=True) + EPS)
     hat1 = x * r1
@@ -694,34 +776,26 @@
     inner = jnp.mean(scaled * hat1, axis=-1, keepdims=True)
     ing_ref[...] = (gmid_ref[...] + r1 * (scaled - hat1 * inner)).astype(BF)
 
+    total = gd_buf[0]
+    for i in range(7):
+        gain_over(i).wait_recv()
+        total = total + gd_buf[i + 1]
+    total = pltpu.roll(total, lax.rem(8 - dp, 8) * deep, 1)
+    gg1_ref[...] = total[0:1, 0:deep] / g1_ref[...].astype(F32)
+    gg2_ref[...] = total[1:2, 0:deep] / g2_ref[...].astype(F32)
     ga = a_settle.total()
-    one_sum = None
-    for j, (ref, own) in enumerate(((gq_out, wq_in), (gk_out, wk_in), (gv_out, wv_in))):
-        part = ga[:, j * wide : (j + 1) * wide]
-        ref[...] = part
-        part = jnp.sum(part * own[...].astype(F32), axis=1, keepdims=True)
-        one_sum = part if one_sum is None else one_sum + part
-    gout_ref[...] = ga[:, 3 * wide : 4 * wide].T
-    lane = lax.broadcasted_iota(jnp.int32, (deep, 128), 1)
-    gain_buf[0] = jnp.where(lane < 64, one_sum, two_sum)
-    for i in range(3):
-        gain_copy(i).start()
-    total = gain_buf[0]
-    for i in range(3):
-        gain_copy(i).wait_recv()
-        total = total + gain_buf[i + 1]
-    turned = total.T
-    gg1_ref[...] = turned[0:1] / g1_ref[...].astype(F32)
-    gg2_ref[...] = turned[64:65] / g2_ref[...].astype(F32)
+    for j, ref in enumerate((gq_out, gk_out, gv_out)):
+        ref[...] = ga[:, j * wide : (j + 1) * wide]
     for i in range(3):
         gain_copy(i).wait_send()
-    for item in (down_fold, gn1_fold, gmb_spread, f_settle, a_settle):
+    for i in range(7):
+        gain_over(i).wait_send()
+    for item in (down_fold, halo_fold, gn1_fold, *gmb_spreads, f_settle, o_settle, a_settle):
         item.finish()
 
     @pl.when(place >= 1)
     def _():
-        for i in range(4):
-            back_copy(i).wait_send()
+        near_back().wait_send()
 
     @pl.when(place >= 2)
     def _():
@@ -742,7 +816,7 @@
     shape = jax.ShapeDtypeStruct
     vmem = pl.BlockSpec(memory_space=pltpu.VMEM)
     smem = pl.BlockSpec(memory_space=pltpu.SMEM)
-    copies = 5 * 3 + 3 * 8 + 2 + 3 * blocks + 3 * 3 + 2 * 7 + 5 + 3
+    copies = 7 * 3 + 4 * 8 + 3 + 3 * blocks + 5 * 3 + 3 * 7 + 2 + 3 + 7
     results = pl.pallas_call(
         kernel,
         out_shape=[
@@ -755,7 +829,7 @@
             shape((wide, deep), F32),
             shape((1, deep), F32),
             shape((deep, hidden), F32),
-            shape((hidden, deep), F32),
+            shape((deep, hidden), F32),
         ],
         in_specs=[smem, smem] + [vmem] * 10,
         out_specs=[vmem] * 10,
@@ -793,12 +867,16 @@
             pltpu.VMEM((token, width), BF),
             pltpu.VMEM((4, deep, 2 * hidden), BF),
             pltpu.VMEM((3, deep, 2 * hidden), BF),
-            pltpu.VMEM((4, deep, width), BF),
-            pltpu.VMEM((3, deep, width), BF),
+            pltpu.VMEM((width, wide), BF),
+            pltpu.VMEM((4, deep, wide), BF),
+            pltpu.VMEM((3, deep, wide), BF),
+            pltpu.VMEM((4, deep, 128 * pl.cdiv(3 * wide, 128)), BF),
+            pltpu.VMEM((3, deep, 128 * pl.cdiv(3 * wide, 128)), BF),
             pltpu.VMEM((wide, token), F32),
-            pltpu.VMEM((WINDOW, 2 * wide), BF),
-            pltpu.VMEM((WINDOW, 2 * wide), BF),
-            pltpu.VMEM((4, deep, 128), F32),
+            pltpu.VMEM((rows, width), BF),
+            pltpu.VMEM((2, WINDOW - token, width), BF),
+            pltpu.VMEM((4, 8, width), F32),
+            pltpu.VMEM((8, 8, width), F32),
             pltpu.SemaphoreType.DMA((copies,)),
             pltpu.SemaphoreType.DMA((copies,)),
         ],
@@ -807,11 +885,25 @@
         ),
     )(
         segments, parents, layer_input, cotangent, norm1_gain[None], w_query, w_key, w_value, w_out,
-        norm2_gain[None], w_up, w_down,
-    )
-    results = list(results)
-    results[2], results[7] = results[2][0], results[7][0]
+        norm2_gain[None], w_up, w_down.T,
+    )
+    results = list(hand_over(results))
+    results[2], results[7], results[9] = results[2][0], results[7][0], results[9].T
     return tuple(results)
+
+
+def hand_over(arrays):
+    def body(*refs):
+        for source, target in zip(refs[: len(arrays)], refs[len(arrays) :]):
+            target[...] = source[...]
+
+    vmem = pl.BlockSpec(memory_space=pltpu.VMEM)
+    return pl.pallas_call(
+        body,
+        out_shape=[jax.ShapeDtypeStruct(a.shape, a.dtype) for a in arrays],
+        in_specs=[vmem] * len(arrays),
+        out_specs=[vmem] * len(arrays),
+    )(*arrays)
 
 
 epsilon = 1e-06

time: 203 us -> 180 us (0.89)
  Pallas kernels: 191 us -> 180 us
  local copies, waits for them, and re-layouts: 9.99 us -> 0 us
    pallas_call x1, Pallas kernels: 191 us -> 177 us  [fast_shards(): pl.pallas_call(kernel, out_shape=[shape((rows, width), BF), shape((rows,...]
    unnamed x29 -> x0, local copies, waits for them, and re-layouts: 9.99 us -> none
    pallas_call x0 -> x1, Pallas kernels: none -> 2.82 us  [hand_over(): pl.pallas_call(body, out_shape=[jax.ShapeDtypeStruct(a.shape, a.dtype) fo...]
where the time goes in v4:
time: 180 us
  Pallas kernels  180 us (100%)
    pallas_call x1, Pallas kernels, fast_shards(): pl.pallas_call(kernel, out_shape=[shape((rows, width), BF), shape((rows,...  177 us

profile of v4, /device:TPU:0, one launch (start us, length us, event | category | flops | bytes accessed | tf_op | source)
XLA Modules:
  0.0 180.2 jit_solution(634194229343170284)
XLA Ops:
  0.6 176.7 %shard_map.195 = (bf16[320,768]{1,0:T(8,128)(2,1)}, bf16[320,768]{1,0:T(8,128)(2,1)}, f32[1,96]{1,0:T(1,128)}, f32[96,192]{1,0:T(8,128)}, f32[96,192]{1,0:T(8,12...) custom-call(s32[10240]{0:T(1024)} %seg_ref.1, ...), custom_call_target="tpu_custom_call" | custom-call | tf_op jit(solution)/shard_map/pallas_call | solution.py:820
  177.4 2.8 %shard_map.196 = (bf16[320,768]{1,0:T(8,128)(2,1)}, bf16[320,768]{1,0:T(8,128)(2,1)}, f32[1,96]{1,0:T(1,128)}, f32[96,192]{1,0:T(8,128)}, f32[96,192]{1,0:T(8,12...) custom-call(bf16[320,768]{1,0:T(8,128)(2,1)} %get-tuple-element.30.r, ...), custom_call_target="tpu_custom_call" | custom-call | tf_op jit(solution)/shard_map/pallas_call | solution.py:901

commit v5 on v4

--- a/solution.py
+++ b/solution.py
@@ -299,9 +299,33 @@
         lambda i: cot_all.at[pl.ds(i * rows, rows)],
         lambda i: n2_ref.at[pl.ds(i * rows, rows)],
     )
-    f_settle = Settle(links, links.take(7), dp, t, f_ref, deep, gfy_ref, gfz_ref)
+    f_settles = [
+        Settle(
+            links,
+            links.take(7),
+            dp,
+            t,
+            f_ref.at[:, pl.ds(j * hidden, hidden)],
+            deep,
+            gfy_ref.at[:, :, pl.ds(j * hidden, hidden)],
+            gfz_ref.at[:, :, pl.ds(j * hidden, hidden)],
+        )
+        for j in range(2)
+    ]
     o_settle = Settle(links, links.take(7), dp, t, go_ref, deep, goy_ref, goz_ref)
-    a_settle = Settle(links, links.take(7), dp, t, w_ref.at[:, pl.ds(0, gay_ref.shape[2])], deep, gay_ref, gaz_ref)
+    a_settles = [
+        Settle(
+            links,
+            links.take(7),
+            dp,
+            t,
+            w_ref.at[:, pl.ds(a, n)],
+            deep,
+            gay_ref.at[:, :, pl.ds(a, n)],
+            gaz_ref.at[:, :, pl.ds(a, n)],
+        )
+        for a, n in ((0, 2 * wide), (2 * wide, gay_ref.shape[2] - 2 * wide))
+    ]
     b1 = links.take(1)
     b2 = links.take(1)
     near_back = lambda: links.copy(cot_all.at[pl.ds(3 * rows, rows)], near_buf, b1, b1, (lax.rem(dp + 7, 8), t))
@@ -562,11 +586,17 @@
         g = tn(n2_ref[:, pl.ds(at, 256)], gu_ref[...])
         gt_buf[0, :, pl.ds(at, 256)] = nt(ones, (g * f_ref[pl.ds(at, 256), 0:hidden].astype(F32)).astype(BF))
         f_ref[pl.ds(at, 256), 0:hidden] = g.astype(BF)
+        return 0
+
+    lax.fori_loop(0, width // 256, ffn_grads, 0)
+    f_settles[0].start()
+
+    def down_grads(j, _):
+        at = pl.multiple_of(j * 256, 256)
         f_ref[pl.ds(at, 256), hidden : 2 * hidden] = tn(cot_all[:, pl.ds(at, 256)], a_ref[...]).astype(BF)
         return 0
 
-    lax.fori_loop(0, width // 256, ffn_grads, 0)
-    f_settle.start()
+    lax.fori_loop(0, width // 256, down_grads, 0)
 
     for j in range(2):
         here = slice(j * part, (j + 1) * part)
@@ -580,6 +610,7 @@
         gmid_ref[here, :] = gmid
         gmb_ref[pl.ds(t * rows + j * part, part), :] = gmid.astype(BF)
         gmb_spreads[j].start()
+    f_settles[1].start()
     for item in gn_folds:
         item.finish()
 
@@ -602,6 +633,7 @@
         item.forward()
     for item in gmb_spreads:
         item.wait()
+    down_fold.copy(1).start()
 
     def context_grads(i, _):
         at = pl.multiple_of(i * SEG, SEG)
@@ -616,6 +648,8 @@
         return 0
 
     lax.fori_loop(0, blocks, context_grads, 0)
+    for step in (2, 1, 3):
+        f_settles[0].pass_on(step)
     go_ref[...] = nn(ct_ref[pl.ds(t * wide, wide), :], gmb_ref[...]).astype(BF).T
     o_settle.start()
     qm_ref, gm_ref = a_ref, gu_ref
@@ -700,11 +734,11 @@
         return 0
 
     lax.fori_loop(0, 4, halo_outer, 0)
+    for step in (2, 1, 3):
+        f_settles[1].pass_on(step)
     for i in range(blocks - 1, 1, -1):
         piece(i, back, back + i + 1, i == blocks - 1)
 
-    for step in (2, 1, 3):
-        f_settle.pass_on(step)
     for step in (2, 1, 3):
         o_settle.pass_on(step)
     for i in range(1, -1, -1):
@@ -716,8 +750,6 @@
     def _():
         near_back().start()
 
-    down_fold.copy(1).start()
-
     def turn_queries(i, _):
         at = pl.multiple_of(i * SEG, SEG)
         q_ref[pl.ds(at, SEG), 0:wide] = (dqt_ref[:, pl.ds(at, SEG)] * HD**-0.5).astype(BF).T
@@ -725,24 +757,30 @@
 
     lax.fori_loop(0, blocks, turn_queries, 0)
 
+    keep = pl.ds(WINDOW, token)
+    own_k, own_v = pool_ref[keep, 0:wide].astype(BF), pool_ref[pl.ds(ext + WINDOW, token), 0:wide].astype(BF)
+    k_ref[keep, 0:wide] = own_k
+    v_ref[keep, 0:wide] = own_v
+    grads = [
+        tn(xe_ref[0:WINDOW, :], ref[0:WINDOW, 0:wide]) + tn(n1_ref[...], ref[WINDOW:, 0:wide]) for ref in (k_ref, v_ref)
+    ]
+    w_ref[0:width, 0 : 2 * wide] = jnp.concatenate([g.astype(BF) for g in grads], axis=1)
+    a_settles[0].start()
+    grads.append(tn(n1_ref[...], q_ref[:, 0:wide]))
+    w_ref[0:width, 2 * wide : 3 * wide] = grads[2].astype(BF)
+    a_settles[1].start()
     def own_outer(k, _):
         outer(WINDOW + (t ^ (3 - k)) * rows, k, gn1_fold, True)
         return 0
 
     lax.fori_loop(0, 4, own_outer, 0)
-    grads = [
-        tn(n1_ref[...], q_ref[:, 0:wide]),
-        tn(xe_ref[0:WINDOW, :], k_ref[0:WINDOW, 0:wide]) + tn(n1_ref[...], k_ref[WINDOW:, 0:wide]),
-        tn(xe_ref[0:WINDOW, :], v_ref[0:WINDOW, 0:wide]) + tn(n1_ref[...], v_ref[WINDOW:, 0:wide]),
-    ]
-    w_ref[0:width, 0 : 3 * wide] = jnp.concatenate([g.astype(BF) for g in grads], axis=1)
-    a_settle.start()
-    terms = sum(g * w[:, 0:wide].astype(F32) for g, w in zip(grads, (wq_ref, wk_ref, wv_ref)))
+    terms = sum(g * w[:, 0:wide].astype(F32) for g, w in zip(grads, (wk_ref, wv_ref, wq_ref)))
     first_row = lax.broadcasted_iota(jnp.int32, (8, width), 0) == 0
     gt_buf[0] = jnp.where(first_row, nt(ones[:, 0:wide], terms.astype(BF)), gt_buf[0])
     for i in range(3):
         gain_copy(i).start()
-    out_ref[...] = (mid_ref[...] + down_fold.total(down_own[...])).astype(BF)
+    for step in (2, 1, 3):
+        a_settles[0].pass_on(step)
     total = gt_buf[0]
     for i in range(3):
         gain_copy(i).wait_recv()
@@ -750,13 +788,13 @@
     gd_buf[0] = total
     for i in range(7):
         gain_over(i).start()
-    gf = f_settle.total()
-    gup_ref[...] = gf[:, 0:hidden]
-    gdown_ref[...] = gf[:, hidden : 2 * hidden]
+    gup_ref[...] = f_settles[0].total()
+    gdown_ref[...] = f_settles[1].total()
     gout_ref[...] = o_settle.total().T
+
     for step in (2, 1, 3):
-        a_settle.pass_on(step)
-
+        a_settles[1].pass_on(step)
+    out_ref[...] = (mid_ref[...] + down_fold.total(down_own[...])).astype(BF)
     gn1 = gn1_fold.total(gn_own[...])
 
     @pl.when(place < per_tree - 1)
@@ -783,14 +821,15 @@
     total = pltpu.roll(total, lax.rem(8 - dp, 8) * deep, 1)
     gg1_ref[...] = total[0:1, 0:deep] / g1_ref[...].astype(F32)
     gg2_ref[...] = total[1:2, 0:deep] / g2_ref[...].astype(F32)
-    ga = a_settle.total()
-    for j, ref in enumerate((gq_out, gk_out, gv_out)):
-        ref[...] = ga[:, j * wide : (j + 1) * wide]
+    ga = a_settles[0].total()
+    gk_out[...] = ga[:, 0:wide]
+    gv_out[...] = ga[:, wide : 2 * wide]
+    gq_out[...] = a_settles[1].total()[:, 0:wide]
     for i in range(3):
         gain_copy(i).wait_send()
     for i in range(7):
         gain_over(i).wait_send()
-    for item in (down_fold, halo_fold, gn1_fold, *gmb_spreads, f_settle, o_settle, a_settle):
+    for item in (down_fold, halo_fold, gn1_fold, *gmb_spreads, *f_settles, o_settle, *a_settles):
         item.finish()
 
     @pl.when(place >= 1)
@@ -816,7 +855,7 @@
     shape = jax.ShapeDtypeStruct
     vmem = pl.BlockSpec(memory_space=pltpu.VMEM)
     smem = pl.BlockSpec(memory_space=pltpu.SMEM)
-    copies = 7 * 3 + 4 * 8 + 3 + 3 * blocks + 5 * 3 + 3 * 7 + 2 + 3 + 7
+    copies = 7 * 3 + 4 * 8 + 3 + 3 * blocks + 5 * 3 + 5 * 7 + 2 + 3 + 7
     results = pl.pallas_call(
         kernel,
         out_shape=[

time: 180 us -> 171 us (0.950)
  Pallas kernels: 180 us -> 170 us
    pallas_call x1, Pallas kernels: 177 us -> 167 us  [fast_shards(): pl.pallas_call(kernel, out_shape=[shape((rows, width), BF), shape((rows,...]
where the time goes in v5:
time: 171 us
  Pallas kernels  170 us (99%)
    pallas_call x1, Pallas kernels, fast_shards(): pl.pallas_call(kernel, out_shape=[shape((rows, width), BF), shape((rows,...  167 us

profile of v5, /device:TPU:0, one launch (start us, length us, event | category | flops | bytes accessed | tf_op | source)
XLA Modules:
  0.0 170.7 jit_solution(6964607617334646013)
XLA Ops:
  0.6 167.2 %shard_map.195 = (bf16[320,768]{1,0:T(8,128)(2,1)}, bf16[320,768]{1,0:T(8,128)(2,1)}, f32[1,96]{1,0:T(1,128)}, f32[96,192]{1,0:T(8,128)}, f32[96,192]{1,0:T(8,12...) custom-call(s32[10240]{0:T(1024)} %seg_ref.1, ...), custom_call_target="tpu_custom_call" | custom-call | tf_op jit(solution)/shard_map/pallas_call | solution.py:859
  167.9 2.8 %shard_map.196 = (bf16[320,768]{1,0:T(8,128)(2,1)}, bf16[320,768]{1,0:T(8,128)(2,1)}, f32[1,96]{1,0:T(1,128)}, f32[96,192]{1,0:T(8,128)}, f32[96,192]{1,0:T(8,12...) custom-call(bf16[320,768]{1,0:T(8,128)(2,1)} %get-tuple-element.30.r, ...), custom_call_target="tpu_custom_call" | custom-call | tf_op jit(solution)/shard_map/pallas_call | solution.py:940

commit v6 on v5

--- a/solution.py
+++ b/solution.py
@@ -199,8 +199,8 @@
             (z * 2 + self.y, self.t),
         )
 
-    def start(self):
-        for step in (2, 1, 3, 0):
+    def start(self, steps=(2, 1, 3, 0)):
+        for step in steps:
             self.across(step).start()
 
     def pass_on(self, step):
@@ -510,13 +510,17 @@
         def _():
             c_spread(i - 1).forward()
 
+        @pl.when(i == 2)
+        def _():
+            wout_spread.forward()
+
         return 0
 
     lax.fori_loop(0, blocks, attend, 0)
     c_spread(blocks - 1).forward()
     for step in (1, 3, 2):
         d_gather.forward(step)
-    wout_spread.forward()
+    cot_spread.forward()
     wout_spread.wait()
 
     def middle(i, _):
@@ -532,7 +536,6 @@
     lax.fori_loop(0, blocks, middle, 0)
     for j in range(width // 256):
         mid_ref[:, j * 256 : (j + 1) * 256] = pool_ref[pl.ds(j * token + t * rows, rows), :]
-    cot_spread.forward()
     cot_spread.wait()
     u_gather.wait()
     d_gather.wait()

time: 171 us -> 170 us (level)
  no operation moved by 1% of the time
where the time goes in v6:
time: 170 us
  Pallas kernels  169 us (99%)
    pallas_call x1, Pallas kernels, fast_shards(): pl.pallas_call(kernel, out_shape=[shape((rows, width), BF), shape((rows,...  166 us

profile of v6, /device:TPU:0, one launch (start us, length us, event | category | flops | bytes accessed | tf_op | source)
XLA Modules:
  0.0 169.8 jit_solution(9405187053048316486)
XLA Ops:
  0.6 166.3 %shard_map.195 = (bf16[320,768]{1,0:T(8,128)(2,1)}, bf16[320,768]{1,0:T(8,128)(2,1)}, f32[1,96]{1,0:T(1,128)}, f32[96,192]{1,0:T(8,128)}, f32[96,192]{1,0:T(8,12...) custom-call(s32[10240]{0:T(1024)} %seg_ref.1, ...), custom_call_target="tpu_custom_call" | custom-call | tf_op jit(solution)/shard_map/pallas_call | solution.py:862
  167.0 2.8 %shard_map.196 = (bf16[320,768]{1,0:T(8,128)(2,1)}, bf16[320,768]{1,0:T(8,128)(2,1)}, f32[1,96]{1,0:T(1,128)}, f32[96,192]{1,0:T(8,128)}, f32[96,192]{1,0:T(8,12...) custom-call(bf16[320,768]{1,0:T(8,128)(2,1)} %get-tuple-element.30.r, ...), custom_call_target="tpu_custom_call" | custom-call | tf_op jit(solution)/shard_map/pallas_call | solution.py:943
